TPU v7x, 32 devices: a whole 2x2x4 slice. The times are simulated.
32 devices in a mesh: gx: 4 (over z), gy: 8 (over y, x, core).
Axes of the slice: x: 2, y: 2, z: 4, core: 2. Of those that a mesh axis runs over, the one named last changes fastest.
Arguments:
- right_side: float32 [2, 512, 1024], P(None, 'gx', 'gy'), may hold values from -6 to 6
- shift_coef: float32 [512, 1024], P('gx', 'gy'), may hold values from 0.0001 to 0.001
- viscosity: float32 [512, 1024], P('gx', 'gy'), may hold values from 1 to 10
- wet_tiles: int32 [4, 8], P('gx', 'gy'), may hold values from 0 to 1, as said below
Outputs:
- velocity: float32 [2, 512, 1024], P(None, 'gx', 'gy')
Inputs may be any that keep to these rules, and one draw needn't show every extreme that they name: `wet_tiles`: 1 marks a wet tile of 128 x 128 cells, 0 a dry one.
All inputs are finite; a program needn't handle non-finite values.
Results may differ from a plain program's by a relative error of at most 0.00002.
Values sent between devices are 32-bit elements; how exact they have to be, the bound alone decides.
No kernel may reach another device: no remote copies, remote signals or barrier semaphores. Data moves between devices by JAX's collectives and lax.ppermute only.
A program may use at most 64 MiB of HBM per device.

v0:
```python
import jax
import jax.numpy as jnp
from jax import lax
from jax.sharding import PartitionSpec as P

TILE = 128
LOCAL = 4
COARSE = 4
COARSE_SWEEPS = 8


OMEGA = 0.8


def extended(array, sides, width):
    for axis, dim in sides:
        devices, length = (lax.axis_size(axis), array.shape[dim])
        up = [(i, (i + 1) % devices) for i in range(devices - 1)]
        down = [(j, i) for i, j in up]
        last = lax.slice_in_dim(array, length - width, length, axis=dim)
        leading = lax.slice_in_dim(array, 0, width, axis=dim)
        before = lax.ppermute(last, axis, up)
        after = lax.ppermute(leading, axis, down)
        array = jnp.concatenate([before, array, after], axis=dim)
    return array


def swapped(block, axis, bit):
    count = lax.axis_size(axis)
    route = []
    for low in range(count):
        high = low | 1 << bit
        if high != low and high < count:
            route += [(low, high), (high, low)]
    return lax.ppermute(block, axis, route)


def pad_last(field):
    return jnp.pad(field, [(0, 0)] * (field.ndim - 2) + [(1, 1), (1, 1)])


def face_coefs(padded):
    inner = padded[1:-1, 1:-1]
    return jnp.stack(
        [
            jnp.minimum(inner, padded[:-2, 1:-1]),
            jnp.minimum(inner, padded[2:, 1:-1]),
            jnp.minimum(inner, padded[1:-1, :-2]),
            jnp.minimum(inner, padded[1:-1, 2:]),
        ]
    )


def apply_padded(padded, conduct, reaction, spacing):
    inner = padded[:, 1:-1, 1:-1]
    outflow = conduct[0] * (inner - padded[:, :-2, 1:-1]) + conduct[1] * (
        inner - padded[:, 2:, 1:-1]
    )
    outflow = (
        outflow
        + conduct[2] * (inner - padded[:, 1:-1, :-2])
        + conduct[3] * (inner - padded[:, 1:-1, 2:])
    )
    return reaction * inner + spacing * outflow


def shrink(field):
    size_x, size_y = field.shape[-2:]
    blocks = field.reshape(field.shape[:-2] + (size_x // 2, 2, size_y // 2, 2))
    return jnp.mean(blocks, axis=(-3, -1))


def widen(field):
    return jnp.repeat(jnp.repeat(field, 2, axis=-2), 2, axis=-1)


def level_solve(grid_level, source, reaction, viscous):
    conduct = face_coefs(pad_last(viscous))
    spacing = 0.25**grid_level
    diagonal = reaction + spacing * jnp.sum(conduct, axis=0)
    if grid_level == LOCAL + COARSE:
        iterate = jnp.zeros_like(source)
        for sweep_index in range(COARSE_SWEEPS):
            iterate = (
                iterate
                + OMEGA
                * (source - apply_padded(pad_last(iterate), conduct, reaction, spacing))
                / diagonal
            )
        return iterate
    iterate = OMEGA * source / diagonal
    residual = source - apply_padded(pad_last(iterate), conduct, reaction, spacing)
    correction = level_solve(grid_level + 1, shrink(residual), shrink(reaction), shrink(viscous))
    iterate = iterate + widen(correction)
    return (
        iterate
        + OMEGA * (source - apply_padded(pad_last(iterate), conduct, reaction, spacing)) / diagonal
    )


def operate(iterate, conduct, reaction, spacing):
    padded = extended(iterate, (("gx", 1), ("gy", 2)), 1)
    return apply_padded(padded, conduct, reaction, spacing)


def pair_rows(stacked, bit_index):
    partner = swapped(stacked, "gx", bit_index)
    is_upper = lax.axis_index("gx") // 2**bit_index % 2 == 1
    lower_part = jnp.where(is_upper, partner, stacked)
    upper_part = jnp.where(is_upper, stacked, partner)
    return jnp.concatenate([lower_part, upper_part], 1)


def pair_cols(stacked, bit_index):
    partner = swapped(stacked, "gy", bit_index)
    is_upper = lax.axis_index("gy") // 2**bit_index % 2 == 1
    lower_part = jnp.where(is_upper, partner, stacked)
    upper_part = jnp.where(is_upper, stacked, partner)
    return jnp.concatenate([lower_part, upper_part], 2)


def per_device(right_side, shift_coef, viscosity, wet_tiles):
    wetness = jnp.repeat(jnp.repeat(wet_tiles, TILE, axis=0), TILE, axis=1).astype(jnp.float32)
    source = right_side * wetness
    reaction = shift_coef
    viscous = viscosity * wetness
    banded = extended(viscous[None], (("gx", 1), ("gy", 2)), 2**LOCAL)[0]
    stored = []
    for grid_level in range(LOCAL):
        margin = 2 ** (LOCAL - grid_level)
        padded = banded[
            margin - 1 : banded.shape[0] - margin + 1, margin - 1 : banded.shape[1] - margin + 1
        ]
        banded = shrink(banded)
        conduct = face_coefs(padded)
        spacing = 0.25**grid_level
        diagonal = reaction + spacing * jnp.sum(conduct, axis=0)
        iterate = OMEGA * source / diagonal
        residual = source - operate(iterate, conduct, reaction, spacing)
        stored.append((source, iterate, conduct, reaction, spacing, diagonal))
        source, reaction, viscous = (shrink(residual), shrink(reaction), shrink(viscous))
    stacked = jnp.concatenate([source, reaction[None], viscous[None]], 0)
    row_count, col_count = (source.shape[1], source.shape[2])
    for bit_index in range(lax.axis_size("gx").bit_length() - 1):
        stacked = pair_rows(stacked, bit_index)
    for bit_index in range(lax.axis_size("gy").bit_length() - 1):
        stacked = pair_cols(stacked, bit_index)
    whole_correction = level_solve(LOCAL, stacked[:2], stacked[2], stacked[3])
    correction = lax.dynamic_slice(
        whole_correction,
        (jnp.int32(0), lax.axis_index("gx") * row_count, lax.axis_index("gy") * col_count),
        (2, row_count, col_count),
    )
    for source, iterate, conduct, reaction, spacing, diagonal in reversed(stored):
        iterate = iterate + widen(correction)
        correction = (
            iterate + OMEGA * (source - operate(iterate, conduct, reaction, spacing)) / diagonal
        )
    return correction


def solution(mesh):
    placed = (P(None, "gx", "gy"), P("gx", "gy"), P("gx", "gy"), P("gx", "gy"))
    return jax.shard_map(
        per_device, mesh=mesh, in_specs=placed, out_specs=P(None, "gx", "gy"), check_vma=False
    )
```

profile of v0, /device:TPU:3, one launch (start us, length us, event | category | flops | bytes accessed | tf_op | source)
XLA Modules:
  0.0 221.8 jit_solution(4599988943618148035)
XLA Ops:
  1.5 3.2 %collective-permute-start = (f32[1,16,128]{2,1,0:T(8,128)S(1)}, f32[1,16,128]{2,1,0:T(8,128)S(1)}, u32[]{:S(2)}, u32[]{:S(2)}) collective-permute-start(f32[1,16,128]{2,1,0:T(8,128)S(1)} %get-tuple-element.77), channel_id=1, source_target_pairs={{0,8},{8,16},{16,24},{1,9},{9,17},{17,25},{2,10},{10,18},{18,26},{... | collective-permute-start | bytes 24584 | tf_op jit(solution)/shard_map/ppermute | solution.py:22
  6.9 5.5 %reshape.380 = f32[64,2,64,2]{3,2,1,0:T(8,128)} reshape(f32[128,128]{1,0:T(8,128)S(1)} %broadcast_multiply_fusion) | data formatting | bytes 131072 | tf_op jit(solution)/shard_map/reshape | solution.py:69
  12.3 2.8 %reduce_sum.407 = f32[64,64]{1,0:T(8,128)S(1)} reduce(f32[64,2,64,2]{3,2,1,0:T(8,128)} %reshape.380, f32[]{:T(128)} %constant.160.clone.1), dimensions={1,3}, to_apply=%region_11.0 | reduce | flops 12288 | bytes 81924 | tf_op jit(solution)/shard_map/reduce_sum | solution.py:70
  16.9 4.0 %collective-permute-start.2 = (f32[1,160,16]{2,1,0:T(8,128)S(1)}, f32[1,160,16]{2,1,0:T(8,128)S(1)}, u32[]{:S(2)}, u32[]{:S(2)}) collective-permute-start(f32[1,160,16]{2,1,0:T(8,128)S(1)} %get-tuple-element.63), channel_id=1, source_target_pairs={{0,1},{1,2},{2,3},{3,4},{4,5},{5,6},{6,7},{8,9},{9,10},{10,11},{11... | collective-permute-start | bytes 30728 | tf_op jit(solution)/shard_map/ppermute | solution.py:22
  20.9 1.9 collective-permute-start.3
  22.9 5.5 %reshape.376 = f32[64,2,64,2]{3,2,1,0:T(8,128)} reshape(f32[128,128]{1,0:T(8,128)S(1)} %copy-done) | data formatting | bytes 131072 | tf_op jit(solution)/shard_map/reshape | solution.py:69
  28.5 2.8 %reduce_sum.388 = f32[64,64]{1,0:T(8,128)S(1)} reduce(f32[64,2,64,2]{3,2,1,0:T(8,128)} %reshape.376, f32[]{:T(128)} %constant.160.clone.1), dimensions={1,3}, to_apply=%region_1.0 | reduce | flops 12288 | bytes 81924 | tf_op jit(solution)/shard_map/reduce_sum | solution.py:70
  32.1 4.3 %collective-permute-start.4 = (f32[2,1,128]{1,2,0:T(8,128)S(1)}, f32[2,1,128]{1,2,0:T(8,128)S(1)}, u32[]{:S(2)}, u32[]{:S(2)}) collective-permute-start(f32[2,1,128]{1,2,0:T(8,128)S(1)} %get-tuple-element.61), channel_id=1, source_target_pairs={{0,8},{8,16},{16,24},{1,9},{9,17},{17,25},{2,10},{10,18},{18,26},{... | collective-permute-start | bytes 3080 | tf_op jit(solution)/shard_map/ppermute | solution.py:22
  37.8 5.1 %reshape_squeeze.9 = f32[80,2,80,2]{3,2,1,0:T(8,128)} reshape(f32[1,160,160]{2,1,0:T(8,128)S(1)} %pad_maximum_fusion) | data formatting | bytes 204800 | tf_op jit(solution)/shard_map/reshape;squeeze | solution.py:69
  42.8 4.3 %reduce_sum.389 = f32[80,80]{1,0:T(8,128)S(1)} reduce(f32[80,2,80,2]{3,2,1,0:T(8,128)} %reshape_squeeze.9, f32[]{:T(128)} %constant.160.clone.1), dimensions={1,3}, to_apply=%region_2.0 | reduce | flops 19200 | bytes 128004 | tf_op jit(solution)/shard_map/reduce_sum | solution.py:70
  47.3 4.8 %collective-permute-start.6 = (f32[2,130,1]{1,2,0:T(1,128)S(1)}, f32[2,130,1]{1,2,0:T(1,128)S(1)}, u32[]{:S(2)}, u32[]{:S(2)}) collective-permute-start(f32[2,130,1]{1,2,0:T(1,128)S(1)} %get-tuple-element.55), channel_id=1, source_target_pairs={{0,1},{1,2},{2,3},{3,4},{4,5},{5,6},{6,7},{8,9},{9,10},{10,11},{11... | collective-permute-start | bytes 3128 | tf_op jit(solution)/shard_map/ppermute | solution.py:22
  52.1 1.9 collective-permute-start.7
  55.3 2.6 %collective-permute-done.7 = f32[2,130,1]{1,2,0:T(1,128)S(1)} collective-permute-done((f32[2,130,1]{1,2,0:T(1,128)S(1)}, f32[2,130,1]{1,2,0:T(1,128)S(1)}, u32[]{:S(2)}, u32[]{:S(2)}) %collective-permute-start.7) | collective-permute-done | bytes 1072 | tf_op jit(solution)/shard_map/ppermute | solution.py:23
  58.2 9.7 %reshape.375 = f32[2,64,2,64,2]{4,3,2,1,0:T(8,128)} reshape(f32[2,128,128]{2,1,0:T(8,128)S(1)} %copy.175) | data formatting | bytes 262144 | tf_op jit(solution)/shard_map/reshape | solution.py:69
  68.0 4.5 %reduce_sum.387 = f32[2,64,64]{2,1,0:T(8,128)S(1)} reduce(f32[2,64,2,64,2]{4,3,2,1,0:T(8,128)} %reshape.375, f32[]{:T(128)} %constant.160.clone.1), dimensions={2,4}, to_apply=%region_0.0 | reduce | flops 24576 | bytes 163844 | tf_op jit(solution)/shard_map/reduce_sum | solution.py:70
  72.6 4.3 %collective-permute-start.8 = (f32[2,1,64]{2,1,0:T(1,128)S(1)}, f32[2,1,64]{2,1,0:T(1,128)S(1)}, u32[]{:S(2)}, u32[]{:S(2)}) collective-permute-start(f32[2,1,64]{2,1,0:T(1,128)S(1)} %get-tuple-element.75), channel_id=1, source_target_pairs={{0,8},{8,16},{16,24},{1,9},{9,17},{17,25},{2,10},{10,18},{18,26},{... | collective-permute-start | bytes 1544 | tf_op jit(solution)/shard_map/ppermute | solution.py:22
  81.2 3.4 %collective-permute-start.10 = (f32[2,66,1]{2,1,0:T(8,128)S(1)}, f32[2,66,1]{2,1,0:T(8,128)S(1)}, u32[]{:S(2)}, u32[]{:S(2)}) collective-permute-start(f32[2,66,1]{2,1,0:T(8,128)S(1)} %get-tuple-element.67), channel_id=1, source_target_pairs={{0,1},{1,2},{2,3},{3,4},{4,5},{5,6},{6,7},{8,9},{9,10},{10,11},{11... | collective-permute-start | bytes 1592 | tf_op jit(solution)/shard_map/ppermute | solution.py:22
  87.0 4.2 %collective-permute-done.11 = f32[2,66,1]{2,1,0:T(8,128)S(1)} collective-permute-done((f32[2,66,1]{2,1,0:T(8,128)S(1)}, f32[2,66,1]{2,1,0:T(8,128)S(1)}, u32[]{:S(2)}, u32[]{:S(2)}) %collective-permute-start.11) | collective-permute-done | bytes 560 | tf_op jit(solution)/shard_map/ppermute | solution.py:23
  91.4 2.2 reshape.377
  93.9 3.2 %collective-permute-start.12 = (f32[2,1,32]{2,1,0:T(1,128)S(1)}, f32[2,1,32]{2,1,0:T(1,128)S(1)}, u32[]{:S(2)}, u32[]{:S(2)}) collective-permute-start(f32[2,1,32]{2,1,0:T(1,128)S(1)} %get-tuple-element.89), channel_id=1, source_target_pairs={{0,8},{8,16},{16,24},{1,9},{9,17},{17,25},{2,10},{10,18},{18,26},{... | collective-permute-start | bytes 776 | tf_op jit(solution)/shard_map/ppermute | solution.py:22
  98.7 2.7 %collective-permute-done.13 = f32[2,1,32]{2,1,0:T(1,128)S(1)} collective-permute-done((f32[2,1,32]{2,1,0:T(1,128)S(1)}, f32[2,1,32]{2,1,0:T(1,128)S(1)}, u32[]{:S(2)}, u32[]{:S(2)}) %collective-permute-start.13) | collective-permute-done | bytes 288 | tf_op jit(solution)/shard_map/ppermute | solution.py:23
  101.5 3.3 %collective-permute-start.14 = (f32[2,34,1]{2,1,0:T(8,128)S(1)}, f32[2,34,1]{2,1,0:T(8,128)S(1)}, u32[]{:S(2)}, u32[]{:S(2)}) collective-permute-start(f32[2,34,1]{2,1,0:T(8,128)S(1)} %get-tuple-element.81), channel_id=1, source_target_pairs={{0,1},{1,2},{2,3},{3,4},{4,5},{5,6},{6,7},{8,9},{9,10},{10,11},{11... | collective-permute-start | bytes 824 | tf_op jit(solution)/shard_map/ppermute | solution.py:22
  106.9 4.1 %collective-permute-done.15 = f32[2,34,1]{2,1,0:T(8,128)S(1)} collective-permute-done((f32[2,34,1]{2,1,0:T(8,128)S(1)}, f32[2,34,1]{2,1,0:T(8,128)S(1)}, u32[]{:S(2)}, u32[]{:S(2)}) %collective-permute-start.15) | collective-permute-done | bytes 304 | tf_op jit(solution)/shard_map/ppermute | solution.py:23
  111.6 3.2 %collective-permute-start.16 = (f32[2,1,16]{2,1,0:T(1,128)S(1)}, f32[2,1,16]{2,1,0:T(1,128)S(1)}, u32[]{:S(2)}, u32[]{:S(2)}) collective-permute-start(f32[2,1,16]{2,1,0:T(1,128)S(1)} %get-tuple-element.98), channel_id=1, source_target_pairs={{0,8},{8,16},{16,24},{1,9},{9,17},{17,25},{2,10},{10,18},{18,26},{... | collective-permute-start | bytes 392 | tf_op jit(solution)/shard_map/ppermute | solution.py:22
  116.2 2.9 %collective-permute-done.17 = f32[2,1,16]{2,1,0:T(1,128)S(1)} collective-permute-done((f32[2,1,16]{2,1,0:T(1,128)S(1)}, f32[2,1,16]{2,1,0:T(1,128)S(1)}, u32[]{:S(2)}, u32[]{:S(2)}) %collective-permute-start.17) | collective-permute-done | bytes 160 | tf_op jit(solution)/shard_map/ppermute | solution.py:23
  119.3 3.3 %collective-permute-start.18 = (f32[2,18,1]{2,1,0:T(8,128)S(1)}, f32[2,18,1]{2,1,0:T(8,128)S(1)}, u32[]{:S(2)}, u32[]{:S(2)}) collective-permute-start(f32[2,18,1]{2,1,0:T(8,128)S(1)} %get-tuple-element.94), channel_id=1, source_target_pairs={{0,1},{1,2},{2,3},{3,4},{4,5},{5,6},{6,7},{8,9},{9,10},{10,11},{11... | collective-permute-start | bytes 440 | tf_op jit(solution)/shard_map/ppermute | solution.py:22
  122.6 1.9 collective-permute-start.19
  124.5 4.1 %collective-permute-done.19 = f32[2,18,1]{2,1,0:T(8,128)S(1)} collective-permute-done((f32[2,18,1]{2,1,0:T(8,128)S(1)}, f32[2,18,1]{2,1,0:T(8,128)S(1)}, u32[]{:S(2)}, u32[]{:S(2)}) %collective-permute-start.19) | collective-permute-done | bytes 176 | tf_op jit(solution)/shard_map/ppermute | solution.py:23
  129.0 2.6 %collective-permute-done.20 = f32[4,8,8]{2,1,0:T(8,128)S(1)} collective-permute-done((f32[4,8,8]{2,1,0:T(8,128)S(1)}, f32[4,8,8]{2,1,0:T(8,128)S(1)}, u32[]{:S(2)}, u32[]{:S(2)}) %collective-permute-start.20) | collective-permute-done | bytes 1056 | tf_op jit(solution)/shard_map/ppermute | solution.py:35
  131.7 3.7 %collective-permute-done.21 = f32[4,16,8]{2,1,0:T(8,128)S(1)} collective-permute-done((f32[4,16,8]{2,1,0:T(8,128)S(1)}, f32[4,16,8]{2,1,0:T(8,128)S(1)}, u32[]{:S(2)}, u32[]{:S(2)}) %collective-permute-start.21) | collective-permute-done | bytes 2080 | tf_op jit(solution)/shard_map/ppermute | solution.py:35
  137.0 2.7 %collective-permute-done.23 = f32[4,32,16]{1,2,0:T(8,128)S(1)} collective-permute-done((f32[4,32,16]{1,2,0:T(8,128)S(1)}, f32[4,32,16]{1,2,0:T(8,128)S(1)}, u32[]{:S(2)}, u32[]{:S(2)}) %collective-permute-start.23) | collective-permute-done | bytes 8224 | tf_op jit(solution)/shard_map/ppermute | solution.py:35
  140.9 2.1 collective-permute-done.24
  153.9 3.0 %collective-permute-done.26 = f32[2,1,16]{2,1,0:T(1,128)S(1)} collective-permute-done((f32[2,1,16]{2,1,0:T(1,128)S(1)}, f32[2,1,16]{2,1,0:T(1,128)S(1)}, u32[]{:S(2)}, u32[]{:S(2)}) %collective-permute-start.26) | collective-permute-done | bytes 160 | tf_op jit(solution)/shard_map/ppermute | solution.py:23
  157.0 7.7 %collective-permute-start.27 = (f32[2,18,1]{2,1,0:T(8,128)S(1)}, f32[2,18,1]{2,1,0:T(8,128)S(1)}, u32[]{:S(2)}, u32[]{:S(2)}) collective-permute-start(f32[2,18,1]{2,1,0:T(8,128)S(1)} %get-tuple-element.92), channel_id=1, source_target_pairs={{0,1},{1,2},{2,3},{3,4},{4,5},{5,6},{6,7},{8,9},{9,10},{10,11},{11... | collective-permute-start | bytes 440 | tf_op jit(solution)/shard_map/ppermute | solution.py:22
  164.7 1.9 collective-permute-start.28
  166.6 4.1 %collective-permute-done.28 = f32[2,18,1]{2,1,0:T(8,128)S(1)} collective-permute-done((f32[2,18,1]{2,1,0:T(8,128)S(1)}, f32[2,18,1]{2,1,0:T(8,128)S(1)}, u32[]{:S(2)}, u32[]{:S(2)}) %collective-permute-start.28) | collective-permute-done | bytes 176 | tf_op jit(solution)/shard_map/ppermute | solution.py:23
  171.0 2.4 %collective-permute-start.29 = (f32[2,1,32]{2,1,0:T(1,128)S(1)}, f32[2,1,32]{2,1,0:T(1,128)S(1)}, u32[]{:S(2)}, u32[]{:S(2)}) collective-permute-start(f32[2,1,32]{2,1,0:T(1,128)S(1)} %get-tuple-element.83), channel_id=1, source_target_pairs={{0,8},{8,16},{16,24},{1,9},{9,17},{17,25},{2,10},{10,18},{18,26},{... | collective-permute-start | bytes 776 | tf_op jit(solution)/shard_map/ppermute | solution.py:22
  174.8 3.0 %collective-permute-done.30 = f32[2,1,32]{2,1,0:T(1,128)S(1)} collective-permute-done((f32[2,1,32]{2,1,0:T(1,128)S(1)}, f32[2,1,32]{2,1,0:T(1,128)S(1)}, u32[]{:S(2)}, u32[]{:S(2)}) %collective-permute-start.30) | collective-permute-done | bytes 288 | tf_op jit(solution)/shard_map/ppermute | solution.py:23
  177.9 3.3 %collective-permute-start.31 = (f32[2,34,1]{2,1,0:T(8,128)S(1)}, f32[2,34,1]{2,1,0:T(8,128)S(1)}, u32[]{:S(2)}, u32[]{:S(2)}) collective-permute-start(f32[2,34,1]{2,1,0:T(8,128)S(1)} %get-tuple-element.79), channel_id=1, source_target_pairs={{0,1},{1,2},{2,3},{3,4},{4,5},{5,6},{6,7},{8,9},{9,10},{10,11},{11... | collective-permute-start | bytes 824 | tf_op jit(solution)/shard_map/ppermute | solution.py:22
  183.2 4.3 %collective-permute-done.32 = f32[2,34,1]{2,1,0:T(8,128)S(1)} collective-permute-done((f32[2,34,1]{2,1,0:T(8,128)S(1)}, f32[2,34,1]{2,1,0:T(8,128)S(1)}, u32[]{:S(2)}, u32[]{:S(2)}) %collective-permute-start.32) | collective-permute-done | bytes 304 | tf_op jit(solution)/shard_map/ppermute | solution.py:23
  190.8 3.0 %collective-permute-done.34 = f32[2,1,64]{2,1,0:T(1,128)S(1)} collective-permute-done((f32[2,1,64]{2,1,0:T(1,128)S(1)}, f32[2,1,64]{2,1,0:T(1,128)S(1)}, u32[]{:S(2)}, u32[]{:S(2)}) %collective-permute-start.34) | collective-permute-done | bytes 544 | tf_op jit(solution)/shard_map/ppermute | solution.py:23
  193.9 3.3 %collective-permute-start.35 = (f32[2,66,1]{2,1,0:T(8,128)S(1)}, f32[2,66,1]{2,1,0:T(8,128)S(1)}, u32[]{:S(2)}, u32[]{:S(2)}) collective-permute-start(f32[2,66,1]{2,1,0:T(8,128)S(1)} %get-tuple-element.65), channel_id=1, source_target_pairs={{0,1},{1,2},{2,3},{3,4},{4,5},{5,6},{6,7},{8,9},{9,10},{10,11},{11... | collective-permute-start | bytes 1592 | tf_op jit(solution)/shard_map/ppermute | solution.py:22
  197.2 1.9 collective-permute-start.36
  199.2 4.6 %collective-permute-done.36 = f32[2,66,1]{2,1,0:T(8,128)S(1)} collective-permute-done((f32[2,66,1]{2,1,0:T(8,128)S(1)}, f32[2,66,1]{2,1,0:T(8,128)S(1)}, u32[]{:S(2)}, u32[]{:S(2)}) %collective-permute-start.36) | collective-permute-done | bytes 560 | tf_op jit(solution)/shard_map/ppermute | solution.py:23
  207.8 3.8 %collective-permute-done.38 = f32[2,1,128]{1,2,0:T(8,128)S(1)} collective-permute-done((f32[2,1,128]{1,2,0:T(8,128)S(1)}, f32[2,1,128]{1,2,0:T(8,128)S(1)}, u32[]{:S(2)}, u32[]{:S(2)}) %collective-permute-start.38) | collective-permute-done | bytes 1056 | tf_op jit(solution)/shard_map/ppermute | solution.py:23
  211.7 3.3 %collective-permute-start.39 = (f32[2,130,1]{1,2,0:T(1,128)S(1)}, f32[2,130,1]{1,2,0:T(1,128)S(1)}, u32[]{:S(2)}, u32[]{:S(2)}) collective-permute-start(f32[2,130,1]{1,2,0:T(1,128)S(1)} %get-tuple-element.53), channel_id=1, source_target_pairs={{0,1},{1,2},{2,3},{3,4},{4,5},{5,6},{6,7},{8,9},{9,10},{10,11},{11... | collective-permute-start | bytes 3128 | tf_op jit(solution)/shard_map/ppermute | solution.py:22
  215.0 1.9 collective-permute-start.40
  216.9 3.9 %collective-permute-done.40 = f32[2,130,1]{1,2,0:T(1,128)S(1)} collective-permute-done((f32[2,130,1]{1,2,0:T(1,128)S(1)}, f32[2,130,1]{1,2,0:T(1,128)S(1)}, u32[]{:S(2)}, u32[]{:S(2)}) %collective-permute-start.40) | collective-permute-done | bytes 1072 | tf_op jit(solution)/shard_map/ppermute | solution.py:23
  (243 shorter events, 47.5 us)
Async XLA Ops:
  1.5 15.3 %collective-permute-start = (f32[1,16,128]{2,1,0:T(8,128)S(1)}, f32[1,16,128]{2,1,0:T(8,128)S(1)}, u32[]{:S(2)}, u32[]{:S(2)}) collective-permute-start(f32[1,16,128]{2,1,0:T(8,128)S(1)} %get-tuple-element.77), channel_id=1, source_target_pairs={{0,8},{8,16},{16,24},{1,9},{9,17},{17,25},{2,10},{10,18},{18,26},{... | collective-permute-start | bytes 24584 | tf_op jit(solution)/shard_map/ppermute | solution.py:22
  4.7 12.1 %collective-permute-start.1 = (f32[1,16,128]{2,1,0:T(8,128)S(1)}, f32[1,16,128]{2,1,0:T(8,128)S(1)}, u32[]{:S(2)}, u32[]{:S(2)}) collective-permute-start(f32[1,16,128]{2,1,0:T(8,128)S(1)} %get-tuple-element.78), channel_id=1, source_target_pairs={{8,0},{16,8},{24,16},{9,1},{17,9},{25,17},{10,2},{18,10},{26,18},{... | collective-permute-start | bytes 24584 | tf_op jit(solution)/shard_map/ppermute | solution.py:23
  12.3 10.5 %copy-start = (f32[128,128]{1,0:T(8,128)S(1)}, f32[128,128]{1,0:T(8,128)}, u32[]{:S(2)}) copy-start(f32[128,128]{1,0:T(8,128)} %param.5) | copy-start | bytes 196612
  15.2 13.3 %copy-start.1 = (f32[2,128,128]{2,1,0:T(8,128)S(1)}, f32[2,128,128]{2,1,0:T(8,128)}, u32[]{:S(2)}) copy-start(f32[2,128,128]{2,1,0:T(8,128)} %param.4) | copy-start | bytes 393220
  16.9 14.6 %collective-permute-start.2 = (f32[1,160,16]{2,1,0:T(8,128)S(1)}, f32[1,160,16]{2,1,0:T(8,128)S(1)}, u32[]{:S(2)}, u32[]{:S(2)}) collective-permute-start(f32[1,160,16]{2,1,0:T(8,128)S(1)} %get-tuple-element.63), channel_id=1, source_target_pairs={{0,1},{1,2},{2,3},{3,4},{4,5},{5,6},{6,7},{8,9},{9,10},{10,11},{11... | collective-permute-start | bytes 30728 | tf_op jit(solution)/shard_map/ppermute | solution.py:22
  20.9 10.6 %collective-permute-start.3 = (f32[1,160,16]{2,1,0:T(8,128)S(1)}, f32[1,160,16]{2,1,0:T(8,128)S(1)}, u32[]{:S(2)}, u32[]{:S(2)}) collective-permute-start(f32[1,160,16]{2,1,0:T(8,128)S(1)} %get-tuple-element.64), channel_id=1, source_target_pairs={{1,0},{2,1},{3,2},{4,3},{5,4},{6,5},{7,6},{9,8},{10,9},{11,10},{12... | collective-permute-start | bytes 30728 | tf_op jit(solution)/shard_map/ppermute | solution.py:23
  32.1 15.1 %collective-permute-start.4 = (f32[2,1,128]{1,2,0:T(8,128)S(1)}, f32[2,1,128]{1,2,0:T(8,128)S(1)}, u32[]{:S(2)}, u32[]{:S(2)}) collective-permute-start(f32[2,1,128]{1,2,0:T(8,128)S(1)} %get-tuple-element.61), channel_id=1, source_target_pairs={{0,8},{8,16},{16,24},{1,9},{9,17},{17,25},{2,10},{10,18},{18,26},{... | collective-permute-start | bytes 3080 | tf_op jit(solution)/shard_map/ppermute | solution.py:22
  36.3 10.8 %collective-permute-start.5 = (f32[2,1,128]{1,2,0:T(8,128)S(1)}, f32[2,1,128]{1,2,0:T(8,128)S(1)}, u32[]{:S(2)}, u32[]{:S(2)}) collective-permute-start(f32[2,1,128]{1,2,0:T(8,128)S(1)} %get-tuple-element.62), channel_id=1, source_target_pairs={{8,0},{16,8},{24,16},{9,1},{17,9},{25,17},{10,2},{18,10},{26,18},{... | collective-permute-start | bytes 3080 | tf_op jit(solution)/shard_map/ppermute | solution.py:23
  47.3 8.1 %collective-permute-start.6 = (f32[2,130,1]{1,2,0:T(1,128)S(1)}, f32[2,130,1]{1,2,0:T(1,128)S(1)}, u32[]{:S(2)}, u32[]{:S(2)}) collective-permute-start(f32[2,130,1]{1,2,0:T(1,128)S(1)} %get-tuple-element.55), channel_id=1, source_target_pairs={{0,1},{1,2},{2,3},{3,4},{4,5},{5,6},{6,7},{8,9},{9,10},{10,11},{11... | collective-permute-start | bytes 3128 | tf_op jit(solution)/shard_map/ppermute | solution.py:22
  52.1 5.8 %collective-permute-start.7 = (f32[2,130,1]{1,2,0:T(1,128)S(1)}, f32[2,130,1]{1,2,0:T(1,128)S(1)}, u32[]{:S(2)}, u32[]{:S(2)}) collective-permute-start(f32[2,130,1]{1,2,0:T(1,128)S(1)} %get-tuple-element.56), channel_id=1, source_target_pairs={{1,0},{2,1},{3,2},{4,3},{5,4},{6,5},{7,6},{9,8},{10,9},{11,10},{12... | collective-permute-start | bytes 3128 | tf_op jit(solution)/shard_map/ppermute | solution.py:23
  72.6 7.1 %collective-permute-start.8 = (f32[2,1,64]{2,1,0:T(1,128)S(1)}, f32[2,1,64]{2,1,0:T(1,128)S(1)}, u32[]{:S(2)}, u32[]{:S(2)}) collective-permute-start(f32[2,1,64]{2,1,0:T(1,128)S(1)} %get-tuple-element.75), channel_id=1, source_target_pairs={{0,8},{8,16},{16,24},{1,9},{9,17},{17,25},{2,10},{10,18},{18,26},{... | collective-permute-start | bytes 1544 | tf_op jit(solution)/shard_map/ppermute | solution.py:22
  76.8 4.3 %collective-permute-start.9 = (f32[2,1,64]{2,1,0:T(1,128)S(1)}, f32[2,1,64]{2,1,0:T(1,128)S(1)}, u32[]{:S(2)}, u32[]{:S(2)}) collective-permute-start(f32[2,1,64]{2,1,0:T(1,128)S(1)} %get-tuple-element.76), channel_id=1, source_target_pairs={{8,0},{16,8},{24,16},{9,1},{17,9},{25,17},{10,2},{18,10},{26,18},{... | collective-permute-start | bytes 1544 | tf_op jit(solution)/shard_map/ppermute | solution.py:23
  81.2 5.8 %collective-permute-start.10 = (f32[2,66,1]{2,1,0:T(8,128)S(1)}, f32[2,66,1]{2,1,0:T(8,128)S(1)}, u32[]{:S(2)}, u32[]{:S(2)}) collective-permute-start(f32[2,66,1]{2,1,0:T(8,128)S(1)} %get-tuple-element.67), channel_id=1, source_target_pairs={{0,1},{1,2},{2,3},{3,4},{4,5},{5,6},{6,7},{8,9},{9,10},{10,11},{11... | collective-permute-start | bytes 1592 | tf_op jit(solution)/shard_map/ppermute | solution.py:22
  84.7 6.6 %collective-permute-start.11 = (f32[2,66,1]{2,1,0:T(8,128)S(1)}, f32[2,66,1]{2,1,0:T(8,128)S(1)}, u32[]{:S(2)}, u32[]{:S(2)}) collective-permute-start(f32[2,66,1]{2,1,0:T(8,128)S(1)} %get-tuple-element.68), channel_id=1, source_target_pairs={{1,0},{2,1},{3,2},{4,3},{5,4},{6,5},{7,6},{9,8},{10,9},{11,10},{12... | collective-permute-start | bytes 1592 | tf_op jit(solution)/shard_map/ppermute | solution.py:23
  93.9 4.8 %collective-permute-start.12 = (f32[2,1,32]{2,1,0:T(1,128)S(1)}, f32[2,1,32]{2,1,0:T(1,128)S(1)}, u32[]{:S(2)}, u32[]{:S(2)}) collective-permute-start(f32[2,1,32]{2,1,0:T(1,128)S(1)} %get-tuple-element.89), channel_id=1, source_target_pairs={{0,8},{8,16},{16,24},{1,9},{9,17},{17,25},{2,10},{10,18},{18,26},{... | collective-permute-start | bytes 776 | tf_op jit(solution)/shard_map/ppermute | solution.py:22
  97.1 4.3 %collective-permute-start.13 = (f32[2,1,32]{2,1,0:T(1,128)S(1)}, f32[2,1,32]{2,1,0:T(1,128)S(1)}, u32[]{:S(2)}, u32[]{:S(2)}) collective-permute-start(f32[2,1,32]{2,1,0:T(1,128)S(1)} %get-tuple-element.90), channel_id=1, source_target_pairs={{8,0},{16,8},{24,16},{9,1},{17,9},{25,17},{10,2},{18,10},{26,18},{... | collective-permute-start | bytes 776 | tf_op jit(solution)/shard_map/ppermute | solution.py:23
  101.5 5.4 %collective-permute-start.14 = (f32[2,34,1]{2,1,0:T(8,128)S(1)}, f32[2,34,1]{2,1,0:T(8,128)S(1)}, u32[]{:S(2)}, u32[]{:S(2)}) collective-permute-start(f32[2,34,1]{2,1,0:T(8,128)S(1)} %get-tuple-element.81), channel_id=1, source_target_pairs={{0,1},{1,2},{2,3},{3,4},{4,5},{5,6},{6,7},{8,9},{9,10},{10,11},{11... | collective-permute-start | bytes 824 | tf_op jit(solution)/shard_map/ppermute | solution.py:22
  104.8 6.2 %collective-permute-start.15 = (f32[2,34,1]{2,1,0:T(8,128)S(1)}, f32[2,34,1]{2,1,0:T(8,128)S(1)}, u32[]{:S(2)}, u32[]{:S(2)}) collective-permute-start(f32[2,34,1]{2,1,0:T(8,128)S(1)} %get-tuple-element.82), channel_id=1, source_target_pairs={{1,0},{2,1},{3,2},{4,3},{5,4},{6,5},{7,6},{9,8},{10,9},{11,10},{12... | collective-permute-start | bytes 824 | tf_op jit(solution)/shard_map/ppermute | solution.py:23
  111.6 4.6 %collective-permute-start.16 = (f32[2,1,16]{2,1,0:T(1,128)S(1)}, f32[2,1,16]{2,1,0:T(1,128)S(1)}, u32[]{:S(2)}, u32[]{:S(2)}) collective-permute-start(f32[2,1,16]{2,1,0:T(1,128)S(1)} %get-tuple-element.98), channel_id=1, source_target_pairs={{0,8},{8,16},{16,24},{1,9},{9,17},{17,25},{2,10},{10,18},{18,26},{... | collective-permute-start | bytes 392 | tf_op jit(solution)/shard_map/ppermute | solution.py:22
  114.9 4.3 %collective-permute-start.17 = (f32[2,1,16]{2,1,0:T(1,128)S(1)}, f32[2,1,16]{2,1,0:T(1,128)S(1)}, u32[]{:S(2)}, u32[]{:S(2)}) collective-permute-start(f32[2,1,16]{2,1,0:T(1,128)S(1)} %get-tuple-element.99), channel_id=1, source_target_pairs={{8,0},{16,8},{24,16},{9,1},{17,9},{25,17},{10,2},{18,10},{26,18},{... | collective-permute-start | bytes 392 | tf_op jit(solution)/shard_map/ppermute | solution.py:23
  119.3 5.3 %collective-permute-start.18 = (f32[2,18,1]{2,1,0:T(8,128)S(1)}, f32[2,18,1]{2,1,0:T(8,128)S(1)}, u32[]{:S(2)}, u32[]{:S(2)}) collective-permute-start(f32[2,18,1]{2,1,0:T(8,128)S(1)} %get-tuple-element.94), channel_id=1, source_target_pairs={{0,1},{1,2},{2,3},{3,4},{4,5},{5,6},{6,7},{8,9},{9,10},{10,11},{11... | collective-permute-start | bytes 440 | tf_op jit(solution)/shard_map/ppermute | solution.py:22
  122.6 6.0 %collective-permute-start.19 = (f32[2,18,1]{2,1,0:T(8,128)S(1)}, f32[2,18,1]{2,1,0:T(8,128)S(1)}, u32[]{:S(2)}, u32[]{:S(2)}) collective-permute-start(f32[2,18,1]{2,1,0:T(8,128)S(1)} %get-tuple-element.95), channel_id=1, source_target_pairs={{1,0},{2,1},{3,2},{4,3},{5,4},{6,5},{7,6},{9,8},{10,9},{11,10},{12... | collective-permute-start | bytes 440 | tf_op jit(solution)/shard_map/ppermute | solution.py:23
  129.0 2.7 %collective-permute-start.20 = (f32[4,8,8]{2,1,0:T(8,128)S(1)}, f32[4,8,8]{2,1,0:T(8,128)S(1)}, u32[]{:S(2)}, u32[]{:S(2)}) collective-permute-start(f32[4,8,8]{2,1,0:T(8,128)S(1)} %pad_maximum_fusion.76), channel_id=1, source_target_pairs={{0,8},{8,0},{16,24},{24,16},{1,9},{9,1},{17,25},{25,17},{2,10},{10... | collective-permute-start | bytes 3080 | tf_op jit(solution)/shard_map/ppermute | solution.py:35
  131.6 3.8 %collective-permute-start.21 = (f32[4,16,8]{2,1,0:T(8,128)S(1)}, f32[4,16,8]{2,1,0:T(8,128)S(1)}, u32[]{:S(2)}, u32[]{:S(2)}) collective-permute-start(f32[4,16,8]{2,1,0:T(8,128)S(1)} %pad_maximum_fusion.56), channel_id=1, source_target_pairs={{0,16},{16,0},{8,24},{24,8},{1,17},{17,1},{9,25},{25,9},{2,18},{18... | collective-permute-start | bytes 6152 | tf_op jit(solution)/shard_map/ppermute | solution.py:35
  135.7 1.2 collective-permute-start.22
  136.9 2.8 %collective-permute-start.23 = (f32[4,32,16]{1,2,0:T(8,128)S(1)}, f32[4,32,16]{1,2,0:T(8,128)S(1)}, u32[]{:S(2)}, u32[]{:S(2)}) collective-permute-start(f32[4,32,16]{1,2,0:T(8,128)S(1)} %pad_maximum_fusion.57), channel_id=1, source_target_pairs={{0,2},{2,0},{1,3},{3,1},{4,6},{6,4},{5,7},{7,5},{8,10},{10,8},{9,1... | collective-permute-start | bytes 24584 | tf_op jit(solution)/shard_map/ppermute | solution.py:35
  139.7 3.2 %collective-permute-start.24 = (f32[4,32,32]{1,2,0:T(8,128)S(1)}, f32[4,32,32]{1,2,0:T(8,128)S(1)}, u32[]{:S(2)}, u32[]{:S(2)}) collective-permute-start(f32[4,32,32]{1,2,0:T(8,128)S(1)} %pad_maximum_fusion.36), channel_id=1, source_target_pairs={{0,4},{4,0},{1,5},{5,1},{2,6},{6,2},{3,7},{7,3},{8,12},{12,8},{9,1... | collective-permute-start | bytes 49160 | tf_op jit(solution)/shard_map/ppermute | solution.py:35
  150.8 3.2 %collective-permute-start.25 = (f32[2,1,16]{2,1,0:T(1,128)S(1)}, f32[2,1,16]{2,1,0:T(1,128)S(1)}, u32[]{:S(2)}, u32[]{:S(2)}) collective-permute-start(f32[2,1,16]{2,1,0:T(1,128)S(1)} %get-tuple-element.96), channel_id=1, source_target_pairs={{0,8},{8,16},{16,24},{1,9},{9,17},{17,25},{2,10},{10,18},{18,26},{... | collective-permute-start | bytes 392 | tf_op jit(solution)/shard_map/ppermute | solution.py:22
  152.6 4.3 %collective-permute-start.26 = (f32[2,1,16]{2,1,0:T(1,128)S(1)}, f32[2,1,16]{2,1,0:T(1,128)S(1)}, u32[]{:S(2)}, u32[]{:S(2)}) collective-permute-start(f32[2,1,16]{2,1,0:T(1,128)S(1)} %get-tuple-element.97), channel_id=1, source_target_pairs={{8,0},{16,8},{24,16},{9,1},{17,9},{25,17},{10,2},{18,10},{26,18},{... | collective-permute-start | bytes 392 | tf_op jit(solution)/shard_map/ppermute | solution.py:23
  157.0 9.6 %collective-permute-start.27 = (f32[2,18,1]{2,1,0:T(8,128)S(1)}, f32[2,18,1]{2,1,0:T(8,128)S(1)}, u32[]{:S(2)}, u32[]{:S(2)}) collective-permute-start(f32[2,18,1]{2,1,0:T(8,128)S(1)} %get-tuple-element.92), channel_id=1, source_target_pairs={{0,1},{1,2},{2,3},{3,4},{4,5},{5,6},{6,7},{8,9},{9,10},{10,11},{11... | collective-permute-start | bytes 440 | tf_op jit(solution)/shard_map/ppermute | solution.py:22
  164.7 6.0 %collective-permute-start.28 = (f32[2,18,1]{2,1,0:T(8,128)S(1)}, f32[2,18,1]{2,1,0:T(8,128)S(1)}, u32[]{:S(2)}, u32[]{:S(2)}) collective-permute-start(f32[2,18,1]{2,1,0:T(8,128)S(1)} %get-tuple-element.93), channel_id=1, source_target_pairs={{1,0},{2,1},{3,2},{4,3},{5,4},{6,5},{7,6},{9,8},{10,9},{11,10},{12... | collective-permute-start | bytes 440 | tf_op jit(solution)/shard_map/ppermute | solution.py:23
  171.0 3.7 %collective-permute-start.29 = (f32[2,1,32]{2,1,0:T(1,128)S(1)}, f32[2,1,32]{2,1,0:T(1,128)S(1)}, u32[]{:S(2)}, u32[]{:S(2)}) collective-permute-start(f32[2,1,32]{2,1,0:T(1,128)S(1)} %get-tuple-element.83), channel_id=1, source_target_pairs={{0,8},{8,16},{16,24},{1,9},{9,17},{17,25},{2,10},{10,18},{18,26},{... | collective-permute-start | bytes 776 | tf_op jit(solution)/shard_map/ppermute | solution.py:22
  173.5 4.3 %collective-permute-start.30 = (f32[2,1,32]{2,1,0:T(1,128)S(1)}, f32[2,1,32]{2,1,0:T(1,128)S(1)}, u32[]{:S(2)}, u32[]{:S(2)}) collective-permute-start(f32[2,1,32]{2,1,0:T(1,128)S(1)} %get-tuple-element.84), channel_id=1, source_target_pairs={{8,0},{16,8},{24,16},{9,1},{17,9},{25,17},{10,2},{18,10},{26,18},{... | collective-permute-start | bytes 776 | tf_op jit(solution)/shard_map/ppermute | solution.py:23
  177.9 5.3 %collective-permute-start.31 = (f32[2,34,1]{2,1,0:T(8,128)S(1)}, f32[2,34,1]{2,1,0:T(8,128)S(1)}, u32[]{:S(2)}, u32[]{:S(2)}) collective-permute-start(f32[2,34,1]{2,1,0:T(8,128)S(1)} %get-tuple-element.79), channel_id=1, source_target_pairs={{0,1},{1,2},{2,3},{3,4},{4,5},{5,6},{6,7},{8,9},{9,10},{10,11},{11... | collective-permute-start | bytes 824 | tf_op jit(solution)/shard_map/ppermute | solution.py:22
  181.2 6.2 %collective-permute-start.32 = (f32[2,34,1]{2,1,0:T(8,128)S(1)}, f32[2,34,1]{2,1,0:T(8,128)S(1)}, u32[]{:S(2)}, u32[]{:S(2)}) collective-permute-start(f32[2,34,1]{2,1,0:T(8,128)S(1)} %get-tuple-element.80), channel_id=1, source_target_pairs={{1,0},{2,1},{3,2},{4,3},{5,4},{6,5},{7,6},{9,8},{10,9},{11,10},{12... | collective-permute-start | bytes 824 | tf_op jit(solution)/shard_map/ppermute | solution.py:23
  187.8 3.0 %collective-permute-start.33 = (f32[2,1,64]{2,1,0:T(1,128)S(1)}, f32[2,1,64]{2,1,0:T(1,128)S(1)}, u32[]{:S(2)}, u32[]{:S(2)}) collective-permute-start(f32[2,1,64]{2,1,0:T(1,128)S(1)} %get-tuple-element.69), channel_id=1, source_target_pairs={{0,8},{8,16},{16,24},{1,9},{9,17},{17,25},{2,10},{10,18},{18,26},{... | collective-permute-start | bytes 1544 | tf_op jit(solution)/shard_map/ppermute | solution.py:22
  189.5 4.3 %collective-permute-start.34 = (f32[2,1,64]{2,1,0:T(1,128)S(1)}, f32[2,1,64]{2,1,0:T(1,128)S(1)}, u32[]{:S(2)}, u32[]{:S(2)}) collective-permute-start(f32[2,1,64]{2,1,0:T(1,128)S(1)} %get-tuple-element.70), channel_id=1, source_target_pairs={{8,0},{16,8},{24,16},{9,1},{17,9},{25,17},{10,2},{18,10},{26,18},{... | collective-permute-start | bytes 1544 | tf_op jit(solution)/shard_map/ppermute | solution.py:23
  193.9 5.3 %collective-permute-start.35 = (f32[2,66,1]{2,1,0:T(8,128)S(1)}, f32[2,66,1]{2,1,0:T(8,128)S(1)}, u32[]{:S(2)}, u32[]{:S(2)}) collective-permute-start(f32[2,66,1]{2,1,0:T(8,128)S(1)} %get-tuple-element.65), channel_id=1, source_target_pairs={{0,1},{1,2},{2,3},{3,4},{4,5},{5,6},{6,7},{8,9},{9,10},{10,11},{11... | collective-permute-start | bytes 1592 | tf_op jit(solution)/shard_map/ppermute | solution.py:22
  197.2 6.6 %collective-permute-start.36 = (f32[2,66,1]{2,1,0:T(8,128)S(1)}, f32[2,66,1]{2,1,0:T(8,128)S(1)}, u32[]{:S(2)}, u32[]{:S(2)}) collective-permute-start(f32[2,66,1]{2,1,0:T(8,128)S(1)} %get-tuple-element.66), channel_id=1, source_target_pairs={{1,0},{2,1},{3,2},{4,3},{5,4},{6,5},{7,6},{9,8},{10,9},{11,10},{12... | collective-permute-start | bytes 1592 | tf_op jit(solution)/shard_map/ppermute | solution.py:23
  204.3 3.6 %collective-permute-start.37 = (f32[2,1,128]{1,2,0:T(8,128)S(1)}, f32[2,1,128]{1,2,0:T(8,128)S(1)}, u32[]{:S(2)}, u32[]{:S(2)}) collective-permute-start(f32[2,1,128]{1,2,0:T(8,128)S(1)} %get-tuple-element.57), channel_id=1, source_target_pairs={{0,8},{8,16},{16,24},{1,9},{9,17},{17,25},{2,10},{10,18},{18,26},{... | collective-permute-start | bytes 3080 | tf_op jit(solution)/shard_map/ppermute | solution.py:22
  205.9 5.7 %collective-permute-start.38 = (f32[2,1,128]{1,2,0:T(8,128)S(1)}, f32[2,1,128]{1,2,0:T(8,128)S(1)}, u32[]{:S(2)}, u32[]{:S(2)}) collective-permute-start(f32[2,1,128]{1,2,0:T(8,128)S(1)} %get-tuple-element.58), channel_id=1, source_target_pairs={{8,0},{16,8},{24,16},{9,1},{17,9},{25,17},{10,2},{18,10},{26,18},{... | collective-permute-start | bytes 3080 | tf_op jit(solution)/shard_map/ppermute | solution.py:23
  211.7 5.2 %collective-permute-start.39 = (f32[2,130,1]{1,2,0:T(1,128)S(1)}, f32[2,130,1]{1,2,0:T(1,128)S(1)}, u32[]{:S(2)}, u32[]{:S(2)}) collective-permute-start(f32[2,130,1]{1,2,0:T(1,128)S(1)} %get-tuple-element.53), channel_id=1, source_target_pairs={{0,1},{1,2},{2,3},{3,4},{4,5},{5,6},{6,7},{8,9},{9,10},{10,11},{11... | collective-permute-start | bytes 3128 | tf_op jit(solution)/shard_map/ppermute | solution.py:22
  215.0 5.8 %collective-permute-start.40 = (f32[2,130,1]{1,2,0:T(1,128)S(1)}, f32[2,130,1]{1,2,0:T(1,128)S(1)}, u32[]{:S(2)}, u32[]{:S(2)}) collective-permute-start(f32[2,130,1]{1,2,0:T(1,128)S(1)} %get-tuple-element.54), channel_id=1, source_target_pairs={{1,0},{2,1},{3,2},{4,3},{5,4},{6,5},{7,6},{9,8},{10,9},{11,10},{12... | collective-permute-start | bytes 3128 | tf_op jit(solution)/shard_map/ppermute | solution.py:23
where the time goes:
time: 223 us; the launch traced here: 222 us
  starting transfers between devices  92.6 us (42%)
  waiting for transfers between devices  64.7 us (29%)
  local copies, waits for them, and re-layouts  38.7 us (17%)
  other arithmetic  23.8 us (11%)
    ppermute x18, starting transfers between devices, extended(): before = lax.ppermute(last, axis, up)  62.1 us
    ppermute x18, waiting for transfers between devices, extended(): after = lax.ppermute(leading, axis, down)  51.8 us
    ppermute x18, starting transfers between devices, extended(): after = lax.ppermute(leading, axis, down)  29.1 us
    reshape x10, local copies, waits for them, and re-layouts, shrink(): blocks = field.reshape(field.shape[:-2] + (size_x // 2, 2, size_y // 2, 2))  24.7 us
    reduce_sum x27, other arithmetic, shrink(): return jnp.mean(blocks, axis=(-3, -1))  17.7 us
    ppermute x5, waiting for transfers between devices, swapped(): return lax.ppermute(block, axis, route)  12.2 us
    another operation x3, local copies, waits for them, and re-layouts, shrink(): blocks = field.reshape(field.shape[:-2] + (size_x // 2, 2, size_y // 2, 2))  6.13 us
  transfers between devices with their start and end apart: 41, of which 21 were waited for; matrix products, arithmetic and copies ran while one was open for 15% of the time, Pallas kernels for 0%

commit v1 on v0

v1 whole, which is shorter than its diff:
```python
import functools

import jax
import jax.numpy as jnp
from jax import lax
from jax.experimental import pallas as pl
from jax.experimental.pallas import tpu as pltpu
from jax.sharding import PartitionSpec as P

LOCAL = 4
COARSE = 4
COARSE_SWEEPS = 8
OMEGA = 0.8
KEEP = 1.0 - OMEGA

LANES = 128
SUB = 8
HALO = 24
WIDE = 32
GUARD = 8
ROWS = [(LANES + 2 * HALO) >> level for level in range(LOCAL)]
TILES = [-(-rows // SUB) for rows in ROWS]
HELD = [GUARD + SUB * tiles + 16 for tiles in TILES]
RIM = [HALO >> level for level in range(LOCAL)]
F32 = jnp.float32
VMEM_LIMIT = 48 * 1024 * 1024

X0, X1, EAST, WEST, SOUTH, WEIGHT, S0, S1 = range(8)


def iota(dim, shape=(SUB, LANES)):
    return lax.broadcasted_iota(jnp.int32, shape, dim)


def lane_take(tile, index):
    return jnp.take_along_axis(tile, index, axis=1)


def lane_roll(tile, shift):
    return pltpu.roll(tile, shift % LANES, 1)


def eastern(columns, lane):
    rolled = [lane_roll(c, -1) for c in columns]
    if len(columns) == 1:
        return rolled
    return [jnp.where(lane == LANES - 1, rolled[1 - i], rolled[i]) for i in range(2)]


def western(columns, lane):
    rolled = [lane_roll(c, 1) for c in columns]
    if len(columns) == 1:
        return rolled
    return [jnp.where(lane == 0, rolled[1 - i], rolled[i]) for i in range(2)]


def bands_kernel(wet, right_side, shift_coef, viscosity, first, second):
    odd = lax.axis_index("gx") % 2
    wetness = wet[0, 0].astype(F32)
    bottom = LANES - HALO
    starts = (bottom - bottom * odd, bottom * odd)
    for start, out in zip(starts, (first, second)):
        rows = pl.ds(pl.multiple_of(start, SUB), HALO)
        out[0:HALO, :] = right_side[0, rows, :] * wetness
        out[HALO : 2 * HALO, :] = right_side[1, rows, :] * wetness
        out[2 * HALO : 3 * HALO, :] = shift_coef[rows, :]
        out[3 * HALO : 4 * HALO, :] = viscosity[rows, :] * wetness


def strips_kernel(
    size_x, wet, right_side, shift_coef, viscosity, got_first, got_second, held, first, second
):
    index_x = lax.axis_index("gx")
    odd_x = index_x % 2 == 1
    odd_y = lax.axis_index("gy") % 2 == 1
    wetness = wet[0, 0].astype(F32)
    above = (index_x > 0).astype(F32)
    below = (index_x < size_x - 1).astype(F32)
    top = GUARD + HALO
    low = top + LANES
    held[:, 0:GUARD, :] = jnp.zeros((4, GUARD, LANES), F32)
    held[:, low + HALO :, :] = jnp.zeros((4, HELD[0] - low - HALO, LANES), F32)
    for field in range(4):
        rows = slice(field * HALO, (field + 1) * HALO)
        one, two = got_first[rows, :], got_second[rows, :]
        before = jnp.where(odd_x, one, two)
        after = jnp.where(odd_x, two, one)
        if field == 3:
            before, after = before * above, after * below
        own = (
            right_side[field] * wetness
            if field < 2
            else (shift_coef[...] if field == 2 else viscosity[...] * wetness)
        )
        held[field, GUARD:top, :] = before
        held[field, top:low, :] = own
        held[field, low : low + HALO, :] = after
    lane = iota(1)
    for tile in range(TILES[0]):
        row = GUARD + SUB * tile
        left = right = None
        for field in range(4):
            value = held[field, row : row + SUB, :]
            to_left = lane_roll(value, WIDE * field)
            to_right = lane_roll(value, WIDE * field - (LANES - WIDE))
            if field == 0:
                left, right = to_left, to_right
            else:
                left = jnp.where(lane < WIDE * field, left, to_left)
                right = jnp.where(lane < WIDE * field, right, to_right)
        first[SUB * tile : SUB * tile + SUB, :] = jnp.where(odd_y, left, right)
        second[SUB * tile : SUB * tile + SUB, :] = jnp.where(odd_y, right, left)


def relax_level(level, count, source, reaction, viscous, put):
    lane = iota(1)
    for tile in range(TILES[level]):
        row = GUARD + SUB * tile
        here = [viscous(c, row) for c in range(count)]
        east = [jnp.minimum(a, b) for a, b in zip(here, eastern(here, lane))]
        west = western(east, lane)
        for c in range(count):
            north = jnp.minimum(here[c], viscous(c, row - 1))
            south = jnp.minimum(here[c], viscous(c, row + 1))
            diagonal = reaction(c, row) + (east[c] + west[c] + (north + south))
            weight = OMEGA / diagonal
            put(c, row, east[c], west[c], south, weight)
            put(c, row, None, source(0, c, row) * weight, source(1, c, row) * weight, None)


def down_kernel(
    size_y,
    devices,
    held,
    got_first,
    got_second,
    chunks,
    state0,
    state1,
    state2,
    state3,
    beside,
    beside_coefs,
    left_over,
    coef1,
    coef2,
    coef3,
):
    index_y = lax.axis_index("gy")
    odd_y = index_y % 2 == 1
    left_ok = (index_y > 0).astype(F32)
    right_ok = (index_y < size_y - 1).astype(F32)
    lane = iota(1)
    sub = iota(0)
    states = [state0, state1, state2, state3]
    coefs = [None, coef1, coef2, coef3]

    beside[:, 0:GUARD, :] = jnp.zeros((4, GUARD, LANES), F32)
    beside[:, GUARD + ROWS[0] :, :] = jnp.zeros((4, HELD[0] - GUARD - ROWS[0], LANES), F32)
    for tile in range(TILES[0]):
        rows = slice(SUB * tile, SUB * tile + SUB)
        one, two = got_first[rows, :], got_second[rows, :]
        after = jnp.where(odd_y, two, one)
        before = jnp.where(odd_y, one, two)
        for field in range(4):
            value_after = lane_roll(after, -WIDE * field)
            value_before = lane_roll(before, LANES - WIDE - WIDE * field)
            if field == 3:
                value_after, value_before = value_after * right_ok, value_before * left_ok
            blank = jnp.full((SUB, LANES), 1.0 if field == 2 else 0.0, F32)
            value = jnp.where(
                lane < HALO, value_after, jnp.where(lane >= LANES - HALO, value_before, blank)
            )
            beside[field, GUARD + SUB * tile : GUARD + SUB * tile + SUB, :] = value

    for level in range(LOCAL):
        end = GUARD + SUB * TILES[level]
        states[level][:, 0:GUARD, :] = jnp.zeros((8, GUARD, LANES), F32)
        states[level][:, end:, :] = jnp.zeros((8, HELD[level] - end, LANES), F32)
        if level == 0:
            beside_coefs[:, 0:GUARD, :] = jnp.zeros((3, GUARD, LANES), F32)
            beside_coefs[:, end:, :] = jnp.zeros((3, HELD[0] - end, LANES), F32)
        else:
            for slot, fill in ((0, 1.0), (1, 0.0)):
                coefs[level][slot, 0:GUARD, :] = jnp.full((GUARD, LANES), fill, F32)
                coefs[level][slot, end:, :] = jnp.full((HELD[level] - end, LANES), fill, F32)
    left_over[:, 0:GUARD, :] = jnp.zeros((4, GUARD, LANES), F32)
    left_over[:, GUARD + ROWS[0] :, :] = jnp.zeros((4, HELD[0] - GUARD - ROWS[0], LANES), F32)

    def tile_of(ref, slot, row):
        return ref[slot, row : row + SUB, :]

    for level in range(LOCAL):
        state, coef = states[level], coefs[level]
        count = 2 if level == 0 else 1
        if level == 0:

            def source(comp, c, row):
                return tile_of(held if c == 0 else beside, comp, row)

            def reaction(c, row):
                return tile_of(held if c == 0 else beside, 2, row)

            def viscous(c, row):
                return tile_of(held if c == 0 else beside, 3, row)

            def iterate(comp, c, row):
                return tile_of(state0, 2 * comp + c, row)

            def face(kind, c, row):
                return tile_of(state0, 4 + kind, row) if c == 0 else tile_of(beside_coefs, kind, row)

            def put(c, row, east, a, b, weight):
                rows = slice(row, row + SUB)
                if east is None:
                    state0[c, rows, :] = a
                    state0[2 + c, rows, :] = b
                elif c == 0:
                    state0[4, rows, :] = east
                    state0[5, rows, :] = a
                    state0[6, rows, :] = b
                    state0[7, rows, :] = weight
                else:
                    beside_coefs[0, rows, :] = east
                    beside_coefs[1, rows, :] = a
                    beside_coefs[2, rows, :] = b

        else:

            def source(comp, c, row):
                return tile_of(state, S0 + comp, row)

            def reaction(c, row):
                return tile_of(coef, 0, row)

            def viscous(c, row):
                return tile_of(coef, 1, row)

            def iterate(comp, c, row):
                return tile_of(state, X0 + comp, row)

            def face(kind, c, row):
                return tile_of(state, EAST + kind, row)

            def put(c, row, east, a, b, weight):
                rows = slice(row, row + SUB)
                if east is None:
                    state[X0, rows, :] = a
                    state[X1, rows, :] = b
                else:
                    state[EAST, rows, :] = east
                    state[WEST, rows, :] = a
                    state[SOUTH, rows, :] = b
                    state[WEIGHT, rows, :] = weight

        relax_level(level, count, source, reaction, viscous, put)
        for tile in range(TILES[level]):
            row = GUARD + SUB * tile
            for comp in range(2):
                here = [iterate(comp, c, row) for c in range(count)]
                east, west = eastern(here, lane), western(here, lane)
                for c in range(count):
                    total = face(0, c, row) * east[c] + face(1, c, row) * west[c]
                    total = total + (
                        face(2, c, row) * iterate(comp, c, row + 1)
                        + face(2, c, row - 1) * iterate(comp, c, row - 1)
                    )
                    left_over[2 * comp + c, row : row + SUB, :] = (
                        KEEP * source(comp, c, row) + total
                    )

        def pairs(ref, slot, start):
            value = ref[slot, pl.ds(start, SUB, stride=2), :]
            value = value + ref[slot, pl.ds(start + 1, SUB, stride=2), :]
            return value + lane_roll(value, -1)

        def coef_ref(kind, c):
            if level == 0:
                return (held if c == 0 else beside), 2 + kind
            return coef, kind

        if level < LOCAL - 1:
            spread = (2 * lane) & (LANES - 1)

            def narrowed(refs, start):
                values = [lane_take(pairs(ref, slot, start), spread) for ref, slot in refs]
                if len(values) == 1:
                    return values[0]
                return jnp.where(lane < LANES // 2, values[0], values[1])

            for tile in range(TILES[level + 1]):
                start = GUARD + 2 * SUB * tile
                rows = slice(GUARD + SUB * tile, GUARD + SUB * tile + SUB)
                for comp in range(2):
                    refs = [(left_over, 2 * comp + c) for c in range(count)]
                    states[level + 1][S0 + comp, rows, :] = 0.25 * narrowed(refs, start)
                for kind, scale in ((0, 0.25), (1, 0.0625)):
                    refs = [coef_ref(kind, c) for c in range(count)]
                    coefs[level + 1][kind, rows, :] = scale * narrowed(refs, start)
        else:
            start = GUARD + RIM[level]
            spread = 2 * (lane & (SUB - 1))
            own = [
                0.25 * lane_take(pairs(left_over, 0, start), spread),
                0.25 * lane_take(pairs(left_over, 2, start), spread),
                0.25 * lane_take(pairs(coef, 0, start), spread),
                0.0625 * lane_take(pairs(coef, 1, start), spread),
            ]
            chosen = ((lane >> 3) & (SUB - 1)) == sub
            lower = lane < LANES // 2

            def packed(a, b):
                value = jnp.where(chosen, jnp.where(lower, a, b), 0.0)
                return jnp.sum(value, axis=0, keepdims=True)

            tile = jnp.where(sub % 2 == 0, packed(own[0], own[1]), packed(own[2], own[3]))
            for block in range(2 * devices // SUB):
                chunks[SUB * block : SUB * block + SUB, :] = tile


def coarse_solve(fields, rows_total, cols_total):
    shape = fields[0].shape
    width = shape[1]
    row, lane = iota(0, shape), iota(1, shape)

    def shifted(value, amount, axis):
        return pltpu.roll(value, amount % shape[axis], axis)

    def folded(value, step, scale):
        other = jnp.where(
            (row & step) != 0, shifted(value, step, 0), shifted(value, -step, 0)
        )
        value = value + other
        other = jnp.where(
            (lane & step) != 0, shifted(value, step, 1), shifted(value, -step, 1)
        )
        return scale * (value + other)

    sources = fields[:2]
    reaction = jnp.where(lane < cols_total, fields[2], 1.0)
    viscous = fields[3]
    stored = []
    for level in range(COARSE + 1):
        step = 1 << level
        east = jnp.minimum(viscous, shifted(viscous, -step, 1))
        east = jnp.where(lane < cols_total - step, east, 0.0)
        south = jnp.minimum(viscous, shifted(viscous, -step, 0))
        south = jnp.where(row < rows_total - step, south, 0.0)
        west, north = shifted(east, step, 1), shifted(south, step, 0)
        diagonal = reaction + ((east + west) + (north + south))
        weight = OMEGA / diagonal

        def around(value, east=east, west=west, north=north, south=south, step=step):
            total = east * shifted(value, -step, 1) + west * shifted(value, step, 1)
            return total + (south * shifted(value, -step, 0) + north * shifted(value, step, 0))

        iterates = [weight * s for s in sources]
        if level == COARSE:
            for _ in range(COARSE_SWEEPS - 1):
                iterates = [
                    KEEP * x + weight * (s + around(x)) for x, s in zip(iterates, sources)
                ]
            break
        stored.append((sources, iterates, weight, around))
        sources = [
            folded(KEEP * s + around(x), step, 0.25) for x, s in zip(iterates, sources)
        ]
        reaction = folded(reaction, step, 0.25)
        viscous = folded(viscous, step, 0.0625)
    for sources, before, weight, around in reversed(stored):
        iterates = [x + c for x, c in zip(before, iterates)]
        iterates = [KEEP * x + weight * (s + around(x)) for x, s in zip(iterates, sources)]
    return iterates


def up_kernel(
    size_x,
    size_y,
    gathered,
    held,
    state0,
    state1,
    state2,
    state3,
    out,
    grid,
    whole,
    window,
    wide0,
    wide1,
    wide2,
    wide3,
    corr1,
    corr2,
    corr3,
):
    index_x, index_y = lax.axis_index("gx"), lax.axis_index("gy")
    cells = LANES >> LOCAL
    rows_total, cols_total = cells * size_x, cells * size_y
    width = max(LANES, cols_total)
    columns = width // LANES
    per_column = LANES // cells

    lane = iota(1)
    tall = iota(1, (2 * size_x, LANES))
    for column in range(columns):
        targets = [[jnp.zeros((2 * size_x, LANES), F32)] * cells for _ in range(2)]
        for place in range(min(per_column, size_y - column * per_column)):
            j = column * per_column + place
            chunk = jnp.concatenate(
                [gathered[pl.ds(2 * j + h, size_x, stride=2 * size_y), :] for h in range(2)], 0
            )
            mine = (tall // cells) == place
            turns = {}
            for half in range(2):
                for r in range(cells):
                    shift = (cells * (place - r) - half * LANES // 2) % LANES
                    if shift not in turns:
                        turns[shift] = lane_roll(chunk, shift)
                    targets[half][r] = jnp.where(mine, turns[shift], targets[half][r])
        lanes = slice(LANES * column, LANES * column + LANES)
        for half in range(2):
            for r in range(cells):
                for h in range(2):
                    grid[2 * h + half, column, pl.ds(r, size_x, stride=cells), :] = targets[half][r][
                        h * size_x : (h + 1) * size_x
                    ]
    fields = [
        jnp.concatenate([grid[f, c] for c in range(columns)], 1) if columns > 1 else grid[f, 0]
        for f in range(4)
    ]
    corrections = coarse_solve(fields, rows_total, cols_total)

    narrow = (((((lane + 32) & (LANES - 1)) - 32) >> 1)) & (LANES - 1)
    for comp in range(2):
        turned = pltpu.roll(corrections[comp], (width - cells * index_y) % width, 1)
        if columns == 1:
            whole[comp, GUARD : GUARD + rows_total, :] = turned
        else:
            tall_lane = iota(1, (rows_total, LANES))
            whole[comp, GUARD : GUARD + rows_total, :] = jnp.where(
                tall_lane < LANES // 2, turned[:, :LANES], turned[:, width - LANES :]
            )
        whole[comp, 0:GUARD, :] = jnp.zeros((GUARD, LANES), F32)
        whole[comp, GUARD + rows_total :, :] = jnp.zeros((2 * SUB, LANES), F32)
        start = pl.multiple_of(cells * index_x, SUB)
        window[comp] = whole[comp, pl.ds(start, 4 * SUB), :]
        for tile in range(2):
            value = lane_take(window[comp, 7 + SUB * tile : 15 + SUB * tile, :], narrow)
            begin = GUARD + RIM[3] - 2 + 2 * SUB * tile
            wide3[comp, pl.ds(begin, SUB, stride=2), :] = value
            wide3[comp, pl.ds(begin + 1, SUB, stride=2), :] = value

    states = [state0, state1, state2, state3]
    wides = [wide0, wide1, wide2, wide3]
    corrs = [None, corr1, corr2, corr3]
    for level in (3, 2, 1):
        state, wide, corr = states[level], wides[level], corrs[level]
        first = (GUARD + RIM[level] - 1) // SUB * SUB
        last = GUARD + RIM[level] + (LANES >> level)
        for row in range(first, last + 1, SUB):
            rows = slice(row, row + SUB)
            for comp in range(2):

                def total(at, comp=comp):
                    return state[X0 + comp, at : at + SUB, :] + wide[comp, at : at + SUB, :]

                here = total(row)
                around = state[EAST, rows, :] * lane_roll(here, -1)
                around = around + state[WEST, rows, :] * lane_roll(here, 1)
                around = around + (
                    state[SOUTH, rows, :] * total(row + 1)
                    + state[SOUTH, row - 1 : row - 1 + SUB, :] * total(row - 1)
                )
                corr[comp, rows, :] = KEEP * here + state[WEIGHT, rows, :] * (
                    state[S0 + comp, rows, :] + around
                )
        fine = level - 1
        begin = GUARD + RIM[level] - 1
        target = GUARD + RIM[fine] - 2
        for tile in range(-(-((LANES >> level) + 2) // SUB)):
            at = begin + SUB * tile
            to = target + 2 * SUB * tile
            for comp in range(2):
                value = corr[comp, at : at + SUB, :]
                if fine > 0:
                    copies = [(comp, lane_take(value, narrow))]
                else:
                    half = lane >> 1
                    copies = [
                        (2 * comp, lane_take(value, half)),
                        (2 * comp + 1, lane_take(value, half + LANES // 2)),
                    ]
                for slot, copy in copies:
                    wides[fine][slot, pl.ds(to, SUB, stride=2), :] = copy
                    wides[fine][slot, pl.ds(to + 1, SUB, stride=2), :] = copy

    for tile in range(LANES // SUB):
        row = GUARD + HALO + SUB * tile
        rows = slice(row, row + SUB)
        for comp in range(2):

            def total(c, at, comp=comp):
                slot = 2 * comp + c
                return state0[slot, at : at + SUB, :] + wide0[slot, at : at + SUB, :]

            here, other = total(0, row), total(1, row)
            east = jnp.where(lane == LANES - 1, lane_roll(other, -1), lane_roll(here, -1))
            west = jnp.where(lane == 0, lane_roll(other, 1), lane_roll(here, 1))
            around = state0[4, rows, :] * east + state0[5, rows, :] * west
            around = around + (
                state0[6, rows, :] * total(0, row + 1)
                + state0[6, row - 1 : row - 1 + SUB, :] * total(0, row - 1)
            )
            out[comp, SUB * tile : SUB * tile + SUB, :] = KEEP * here + state0[7, rows, :] * (
                held[comp, rows, :] + around
            )


def params():
    return pltpu.CompilerParams(vmem_limit_bytes=VMEM_LIMIT)


VMEM_SPEC = pl.BlockSpec(memory_space=pltpu.VMEM)
SMEM_SPEC = pl.BlockSpec(memory_space=pltpu.SMEM)


def swap_routes(size_x, size_y):
    def index(i, j):
        return i * size_y + j

    routes = []
    for axis in range(2):
        size = (size_x, size_y)[axis]
        for offset in range(2):
            route = []
            for i in range(size_x):
                for j in range(size_y):
                    here = (i, j)[axis]
                    other = here + 1 if here % 2 == offset else here - 1
                    if 0 <= other < size:
                        peer = (other, j) if axis == 0 else (i, other)
                    else:
                        peer = (i, j ^ 1) if axis == 0 else (i ^ 1, j)
                    route.append((index(i, j), index(*peer)))
            routes.append(route)
    return routes


def per_device(size_x, size_y, right_side, shift_coef, viscosity, wet_tiles):
    axes = ("gx", "gy")
    devices = size_x * size_y
    routes = swap_routes(size_x, size_y)
    band = jax.ShapeDtypeStruct((4 * HALO, LANES), F32)
    first, second = pl.pallas_call(
        bands_kernel,
        out_shape=(band, band),
        in_specs=[SMEM_SPEC, VMEM_SPEC, VMEM_SPEC, VMEM_SPEC],
        out_specs=(VMEM_SPEC, VMEM_SPEC),
        compiler_params=params(),
        name="bands",
    )(wet_tiles, right_side, shift_coef, viscosity)
    first = lax.ppermute(first, axes, routes[0])
    second = lax.ppermute(second, axes, routes[1])
    strip = jax.ShapeDtypeStruct((ROWS[0], LANES), F32)
    held, first, second = pl.pallas_call(
        functools.partial(strips_kernel, size_x),
        out_shape=(pltpu.VMEM((4, HELD[0], LANES), F32), strip, strip),
        in_specs=[SMEM_SPEC] + [VMEM_SPEC] * 5,
        out_specs=(VMEM_SPEC,) * 3,
        compiler_params=params(),
        name="strips",
    )(wet_tiles, right_side, shift_coef, viscosity, first, second)
    first = lax.ppermute(first, axes, routes[2])
    second = lax.ppermute(second, axes, routes[3])
    chunks, *states = pl.pallas_call(
        functools.partial(down_kernel, size_y, devices),
        out_shape=(jax.ShapeDtypeStruct((2 * devices, LANES), F32),)
        + tuple(pltpu.VMEM((8, HELD[level], LANES), F32) for level in range(LOCAL)),
        in_specs=[VMEM_SPEC] * 3,
        out_specs=(VMEM_SPEC,) * (1 + LOCAL),
        scratch_shapes=[
            pltpu.VMEM((4, HELD[0], LANES), F32),
            pltpu.VMEM((3, HELD[0], LANES), F32),
            pltpu.VMEM((4, HELD[0], LANES), F32),
        ]
        + [pltpu.VMEM((2, HELD[level], LANES), F32) for level in range(1, LOCAL)],
        compiler_params=params(),
        name="down",
    )(held, first, second)
    gathered = lax.all_to_all(chunks, axes, 0, 0, tiled=True)
    rows_total = (LANES >> LOCAL) * size_x
    columns = max(LANES, (LANES >> LOCAL) * size_y) // LANES
    return pl.pallas_call(
        functools.partial(up_kernel, size_x, size_y),
        out_shape=jax.ShapeDtypeStruct((2, LANES, LANES), F32),
        in_specs=[VMEM_SPEC] * (2 + LOCAL),
        out_specs=VMEM_SPEC,
        scratch_shapes=[
            pltpu.VMEM((4, columns, rows_total, LANES), F32),
            pltpu.VMEM((2, GUARD + rows_total + 2 * SUB, LANES), F32),
            pltpu.VMEM((2, 4 * SUB, LANES), F32),
            pltpu.VMEM((4, HELD[0], LANES), F32),
        ]
        + [pltpu.VMEM((2, HELD[level], LANES), F32) for level in range(1, LOCAL)]
        + [pltpu.VMEM((2, HELD[level], LANES), F32) for level in range(1, LOCAL)],
        compiler_params=params(),
        name="up",
    )(gathered, held, *states)


def solution(mesh):
    sizes = dict(mesh.shape)
    placed = (P(None, "gx", "gy"), P("gx", "gy"), P("gx", "gy"), P("gx", "gy"))
    return jax.shard_map(
        functools.partial(per_device, sizes["gx"], sizes["gy"]),
        mesh=mesh,
        in_specs=placed,
        out_specs=P(None, "gx", "gy"),
        check_vma=False,
    )
```

time: 223 us -> 33.6 us (0.15)
  the two profiles are of different devices: /device:TPU:3 before, /device:TPU:0 now
where the time goes in v1:
time: 33.6 us; the launch traced here: 33.4 us
  blocking collectives  12.8 us (38%)
  starting transfers between devices  6.37 us (19%)
  Pallas kernels  6.34 us (19%)
  waiting for transfers between devices  4.58 us (14%)
  local copies, waits for them, and re-layouts  2.58 us (8%)
  between operations  0.69 us (2%)
    all_to_all x1, blocking collectives, per_device(): gathered = lax.all_to_all(chunks, axes, 0, 0, tiled=True)  12.8 us
    pallas_call x1, Pallas kernels, per_device(): pl.pallas_call(functools.partial(up_kernel, size_x, size_y), out_shape=ja...  3.31 us
    ppermute x1, starting transfers between devices, per_device(): second = lax.ppermute(second, axes, routes[3])  3.21 us
    ppermute x1, starting transfers between devices, per_device(): first = lax.ppermute(first, axes, routes[0])  3.09 us
    pallas_call x1, Pallas kernels, per_device(): pl.pallas_call(functools.partial(down_kernel, size_y, devices), out_shape...  2.8 us
    unnamed x6, local copies, waits for them, and re-layouts  2.58 us
    ppermute x1, waiting for transfers between devices, per_device(): second = lax.ppermute(second, axes, routes[3])  2.51 us
    ppermute x1, waiting for transfers between devices, per_device(): first = lax.ppermute(first, axes, routes[0])  2.07 us
  transfers between devices with their start and end apart: 4, of which 2 were waited for; matrix products, arithmetic and copies ran while one was open for 0% of the time, Pallas kernels for 0%

profile of v1, /device:TPU:0, one launch (start us, length us, event | category | flops | bytes accessed | tf_op | source)
XLA Modules:
  0.0 33.4 jit_solution(4881940929213185049)
XLA Ops:
  0.7 0.0 copy-start
  0.7 0.9 %copy-done = f32[2,128,128]{2,1,0:T(8,128)S(1)} copy-done((f32[2,128,128]{2,1,0:T(8,128)S(1)}, f32[2,128,128]{2,1,0:T(8,128)}, u32[]{:S(2)}) %copy-start) | copy-done | bytes 131096
  1.6 0.0 copy-start.1
  1.6 0.8 %copy-done.1 = f32[128,128]{1,0:T(8,128)S(1)} copy-done((f32[128,128]{1,0:T(8,128)S(1)}, f32[128,128]{1,0:T(8,128)}, u32[]{:S(2)}) %copy-start.1) | copy-done | bytes 65560
  2.4 0.0 copy-start.2
  2.4 0.8 %copy-done.2 = f32[128,128]{1,0:T(8,128)S(1)} copy-done((f32[128,128]{1,0:T(8,128)S(1)}, f32[128,128]{1,0:T(8,128)}, u32[]{:S(2)}) %copy-start.2) | copy-done | bytes 65560
  3.3 3.1 %collective-permute-start = (f32[96,128]{1,0:T(8,128)S(1)}, f32[96,128]{1,0:T(8,128)S(1)}, u32[]{:S(2)}, u32[]{:S(2)}) collective-permute-start(f32[96,128]{1,0:T(8,128)S(1)} %get-tuple-element.15), channel_id=1, source_target_pairs={{0,8},{1,9},{2,10},{3,11},{4,12},{5,13},{6,14},{7,15},{8,0},{9,1},... | collective-permute-start | bytes 147464 | tf_op jit(solution)/shard_map/ppermute | solution.py:563
  6.3 0.0 collective-permute-start.1
  6.3 2.1 %collective-permute-done.got_first = f32[96,128]{1,0:T(8,128)S(1)} collective-permute-done((f32[96,128]{1,0:T(8,128)S(1)}, f32[96,128]{1,0:T(8,128)S(1)}, u32[]{:S(2)}, u32[]{:S(2)}) %collective-permute-start) | collective-permute-done | bytes 49184 | tf_op jit(solution)/shard_map/ppermute | solution.py:563
  8.4 0.0 collective-permute-done.1.got_second
  8.4 0.2 strips.1
  8.6 0.1 collective-permute-start.2
  8.7 3.2 %collective-permute-start.3 = (f32[176,128]{1,0:T(8,128)S(1)}, f32[176,128]{1,0:T(8,128)S(1)}, u32[]{:S(2)}, u32[]{:S(2)}) collective-permute-start(f32[176,128]{1,0:T(8,128)S(1)} %get-tuple-element.19), channel_id=1, source_target_pairs={{0,8},{1,2},{2,1},{3,4},{4,3},{5,6},{6,5},{7,15},{8,0},{9,10},{10,... | collective-permute-start | bytes 270344 | tf_op jit(solution)/shard_map/ppermute | solution.py:575
  11.9 0.0 collective-permute-done.2.got_first
  11.9 2.5 %collective-permute-done.3.got_second = f32[176,128]{1,0:T(8,128)S(1)} collective-permute-done((f32[176,128]{1,0:T(8,128)S(1)}, f32[176,128]{1,0:T(8,128)S(1)}, u32[]{:S(2)}, u32[]{:S(2)}) %collective-permute-start.3) | collective-permute-done | bytes 90144 | tf_op jit(solution)/shard_map/ppermute | solution.py:575
  14.4 2.8 %down.1 = (f32[64,128]{1,0:T(8,128)S(1)}, f32[8,200,128]{2,1,0:T(8,128)S(1)}, f32[8,112,128]{2,1,0:T(8,128)S(1)}, f32[8,72,128]{2,1,0:T(8,128)S(1)}, f32[8,48,128]{2,1,0:T(8,128)S(1)}) custom-call(f32[4,200,128]{2,1,0:T(8,128)S(1)} %get-tuple-element.17.held, f32[176,128]{1,0:T(8,128)S(1)} %collective-permute-done.2.got_first, ...), custom_call_target="tpu_custom_call" | custom-call | tf_op jit(solution)/shard_map/down/pallas_call | solution.py:576
  17.2 12.8 %all_to_all.11 = f32[32,2,128]{2,1,0:T(2,128)S(1)} all-to-all(f32[32,2,128]{2,1,0:T(2,128)S(1)} %bitcast.3), channel_id=1, replica_groups=mesh['gx'=4,'gy'=8] {'gx','gy'}, dimensions={0} | all-to-all | bytes 65536 | tf_op jit(solution)/shard_map/all_to_all | solution.py:591
  30.0 3.3 %up.1 = f32[2,128,128]{2,1,0:T(8,128)} custom-call(f32[64,128]{1,0:T(8,128)S(1)} %bitcast.2, f32[4,200,128]{2,1,0:T(8,128)S(1)} %get-tuple-element.17.held, f32[8,200,128]{2,1,0:T(8,128)S(1)} %get-tuple-element.21.state0, f32[8,112,128]{2,1,0:T(8,128)S(1)} %get-tuple-element.22.state1, f32[8,72,128]{2,1,0:T(8,128)S(1)} %get-tuple-element.23.state2, ...), custom_call_target="tpu_custom_call" | custom-call | tf_op jit(solution)/shard_map/up/pallas_call | solution.py:594
  (1 shorter events, 0.0 us)
Async XLA Ops:
  0.7 0.9 %copy-start = (f32[2,128,128]{2,1,0:T(8,128)S(1)}, f32[2,128,128]{2,1,0:T(8,128)}, u32[]{:S(2)}) copy-start(f32[2,128,128]{2,1,0:T(8,128)} %right_side.3) | copy-start | bytes 393220
  1.6 0.8 %copy-start.1 = (f32[128,128]{1,0:T(8,128)S(1)}, f32[128,128]{1,0:T(8,128)}, u32[]{:S(2)}) copy-start(f32[128,128]{1,0:T(8,128)} %shift_coef.3) | copy-start | bytes 196612
  2.4 0.8 %copy-start.2 = (f32[128,128]{1,0:T(8,128)S(1)}, f32[128,128]{1,0:T(8,128)}, u32[]{:S(2)}) copy-start(f32[128,128]{1,0:T(8,128)} %viscosity.3) | copy-start | bytes 196612
  3.3 5.2 %collective-permute-start = (f32[96,128]{1,0:T(8,128)S(1)}, f32[96,128]{1,0:T(8,128)S(1)}, u32[]{:S(2)}, u32[]{:S(2)}) collective-permute-start(f32[96,128]{1,0:T(8,128)S(1)} %get-tuple-element.15), channel_id=1, source_target_pairs={{0,8},{1,9},{2,10},{3,11},{4,12},{5,13},{6,14},{7,15},{8,0},{9,1},... | collective-permute-start | bytes 147464 | tf_op jit(solution)/shard_map/ppermute | solution.py:563
  6.3 2.1 %collective-permute-start.1 = (f32[96,128]{1,0:T(8,128)S(1)}, f32[96,128]{1,0:T(8,128)S(1)}, u32[]{:S(2)}, u32[]{:S(2)}) collective-permute-start(f32[96,128]{1,0:T(8,128)S(1)} %get-tuple-element.16), channel_id=1, source_target_pairs={{0,1},{1,0},{2,3},{3,2},{4,5},{5,4},{6,7},{7,6},{8,16},{9,17},{10,... | collective-permute-start | bytes 147464 | tf_op jit(solution)/shard_map/ppermute | solution.py:564
  8.6 3.3 %collective-permute-start.2 = (f32[176,128]{1,0:T(8,128)S(1)}, f32[176,128]{1,0:T(8,128)S(1)}, u32[]{:S(2)}, u32[]{:S(2)}) collective-permute-start(f32[176,128]{1,0:T(8,128)S(1)} %get-tuple-element.18), channel_id=1, source_target_pairs={{0,1},{1,0},{2,3},{3,2},{4,5},{5,4},{6,7},{7,6},{8,9},{9,8},{10,11... | collective-permute-start | bytes 270344 | tf_op jit(solution)/shard_map/ppermute | solution.py:574
  8.7 5.7 %collective-permute-start.3 = (f32[176,128]{1,0:T(8,128)S(1)}, f32[176,128]{1,0:T(8,128)S(1)}, u32[]{:S(2)}, u32[]{:S(2)}) collective-permute-start(f32[176,128]{1,0:T(8,128)S(1)} %get-tuple-element.19), channel_id=1, source_target_pairs={{0,8},{1,2},{2,1},{3,4},{4,3},{5,6},{6,5},{7,15},{8,0},{9,10},{10,... | collective-permute-start | bytes 270344 | tf_op jit(solution)/shard_map/ppermute | solution.py:575

commit v2 on v1

--- a/solution.py
+++ b/solution.py
@@ -54,21 +54,29 @@
     return [jnp.where(lane == 0, rolled[1 - i], rolled[i]) for i in range(2)]
 
 
-def bands_kernel(wet, right_side, shift_coef, viscosity, first, second):
+def bands_kernel(wet, right_side, shift_coef, viscosity, held, first, second, sems):
     odd = lax.axis_index("gx") % 2
     wetness = wet[0, 0].astype(F32)
+    top = GUARD + HALO
+    own = pl.ds(top, LANES)
+    sources = (right_side.at[0], right_side.at[1], shift_coef, viscosity)
+    copies = [
+        pltpu.make_async_copy(sources[field], held.at[field, own, :], sems.at[field])
+        for field in range(4)
+    ]
+    for copy in copies:
+        copy.start()
     bottom = LANES - HALO
-    starts = (bottom - bottom * odd, bottom * odd)
-    for start, out in zip(starts, (first, second)):
-        rows = pl.ds(pl.multiple_of(start, SUB), HALO)
-        out[0:HALO, :] = right_side[0, rows, :] * wetness
-        out[HALO : 2 * HALO, :] = right_side[1, rows, :] * wetness
-        out[2 * HALO : 3 * HALO, :] = shift_coef[rows, :]
-        out[3 * HALO : 4 * HALO, :] = viscosity[rows, :] * wetness
+    starts = (top + bottom - bottom * odd, top + bottom * odd)
+    for field in range(4):
+        copies[field].wait()
+        for start, out in zip(starts, (first, second)):
+            value = held[field, pl.ds(pl.multiple_of(start, SUB), HALO), :]
+            out[field * HALO : (field + 1) * HALO, :] = value if field == 2 else value * wetness
 
 
 def strips_kernel(
-    size_x, wet, right_side, shift_coef, viscosity, got_first, got_second, held, first, second
+    size_x, wet, before_held, got_first, got_second, held, first, second
 ):
     index_x = lax.axis_index("gx")
     odd_x = index_x % 2 == 1
@@ -87,13 +95,9 @@
         after = jnp.where(odd_x, two, one)
         if field == 3:
             before, after = before * above, after * below
-        own = (
-            right_side[field] * wetness
-            if field < 2
-            else (shift_coef[...] if field == 2 else viscosity[...] * wetness)
-        )
         held[field, GUARD:top, :] = before
-        held[field, top:low, :] = own
+        if field != 2:
+            held[field, top:low, :] = before_held[field, top:low, :] * wetness
         held[field, low : low + HALO, :] = after
     lane = iota(1)
     for tile in range(TILES[0]):
@@ -552,27 +556,29 @@
     devices = size_x * size_y
     routes = swap_routes(size_x, size_y)
     band = jax.ShapeDtypeStruct((4 * HALO, LANES), F32)
-    first, second = pl.pallas_call(
+    held, first, second = pl.pallas_call(
         bands_kernel,
-        out_shape=(band, band),
-        in_specs=[SMEM_SPEC, VMEM_SPEC, VMEM_SPEC, VMEM_SPEC],
-        out_specs=(VMEM_SPEC, VMEM_SPEC),
+        out_shape=(pltpu.VMEM((4, HELD[0], LANES), F32), band, band),
+        in_specs=[SMEM_SPEC] + [pl.BlockSpec(memory_space=pltpu.HBM)] * 3,
+        out_specs=(VMEM_SPEC,) * 3,
+        scratch_shapes=[pltpu.SemaphoreType.DMA((4,))],
         compiler_params=params(),
         name="bands",
-    )(wet_tiles, right_side, shift_coef, viscosity)
+    )(wet_tiles, *[pltpu.with_memory_space_constraint(a, pltpu.HBM) for a in (right_side, shift_coef, viscosity)])
+    second = lax.ppermute(second, axes, routes[1])
     first = lax.ppermute(first, axes, routes[0])
-    second = lax.ppermute(second, axes, routes[1])
     strip = jax.ShapeDtypeStruct((ROWS[0], LANES), F32)
     held, first, second = pl.pallas_call(
         functools.partial(strips_kernel, size_x),
         out_shape=(pltpu.VMEM((4, HELD[0], LANES), F32), strip, strip),
-        in_specs=[SMEM_SPEC] + [VMEM_SPEC] * 5,
+        in_specs=[SMEM_SPEC] + [VMEM_SPEC] * 3,
         out_specs=(VMEM_SPEC,) * 3,
+        input_output_aliases={1: 0},
         compiler_params=params(),
         name="strips",
-    )(wet_tiles, right_side, shift_coef, viscosity, first, second)
+    )(wet_tiles, held, first, second)
+    second = lax.ppermute(second, axes, routes[3])
     first = lax.ppermute(first, axes, routes[2])
-    second = lax.ppermute(second, axes, routes[3])
     chunks, *states = pl.pallas_call(
         functools.partial(down_kernel, size_y, devices),
         out_shape=(jax.ShapeDtypeStruct((2 * devices, LANES), F32),)

time: 33.6 us -> 32 us (0.952)
  local copies, waits for them, and re-layouts: 2.58 us -> 0 us
  Pallas kernels: 6.34 us -> 7.33 us
    unnamed x6 -> x0, local copies, waits for them, and re-layouts: 2.58 us -> none
    pallas_call x1, Pallas kernels: 0.01 us -> 0.98 us  [per_device(): pl.pallas_call(bands_kernel, out_shape=(pltpu.VMEM((4, HELD[0], LANES), F...]
where the time goes in v2:
time: 32 us; the launch traced here: 31.8 us
  blocking collectives  12.8 us (40%)
  Pallas kernels  7.33 us (23%)
  starting transfers between devices  6.37 us (20%)
  waiting for transfers between devices  4.58 us (14%)
  between operations  0.69 us (2%)
    all_to_all x1, blocking collectives, per_device(): gathered = lax.all_to_all(chunks, axes, 0, 0, tiled=True)  12.8 us
    pallas_call x1, Pallas kernels, per_device(): pl.pallas_call(functools.partial(up_kernel, size_x, size_y), out_shape=ja...  3.31 us
    ppermute x1, starting transfers between devices, per_device(): second = lax.ppermute(second, axes, routes[3])  3.21 us
    ppermute x1, starting transfers between devices, per_device(): first = lax.ppermute(first, axes, routes[0])  3.09 us
    pallas_call x1, Pallas kernels, per_device(): pl.pallas_call(functools.partial(down_kernel, size_y, devices), out_shape...  2.8 us
    ppermute x1, waiting for transfers between devices, per_device(): second = lax.ppermute(second, axes, routes[3])  2.51 us
    ppermute x1, waiting for transfers between devices, per_device(): first = lax.ppermute(first, axes, routes[0])  2.07 us
    pallas_call x1, Pallas kernels, per_device(): pl.pallas_call(bands_kernel, out_shape=(pltpu.VMEM((4, HELD[0], LANES), F...  0.98 us
  transfers between devices with their start and end apart: 4, of which 2 were waited for; matrix products, arithmetic and copies ran while one was open for 0% of the time, Pallas kernels for 0%

profile of v2, /device:TPU:0, one launch (start us, length us, event | category | flops | bytes accessed | tf_op | source)
XLA Modules:
  0.0 31.8 jit_solution(5802827461891450848)
XLA Ops:
  0.7 1.0 %bands.1 = (f32[4,200,128]{2,1,0:T(8,128)S(1)}, f32[96,128]{1,0:T(8,128)S(1)}, f32[96,128]{1,0:T(8,128)S(1)}) custom-call(s32[1,1]{1,0:T(1,128)S(6)} %copy.7.wet, f32[2,128,128]{2,1,0:T(8,128)} %right_side.1, f32[128,128]{1,0:T(8,128)} %shift_coef.1, f32[128,128]{1,0:T(8,128)} %viscosity.1), custom_call_target="tpu_custom_call" | custom-call | tf_op jit(solution)/shard_map/bands/pallas_call | solution.py:559
  1.6 3.1 %collective-permute-start = (f32[96,128]{1,0:T(8,128)S(1)}, f32[96,128]{1,0:T(8,128)S(1)}, u32[]{:S(2)}, u32[]{:S(2)}) collective-permute-start(f32[96,128]{1,0:T(8,128)S(1)} %get-tuple-element.17), channel_id=1, source_target_pairs={{0,8},{1,9},{2,10},{3,11},{4,12},{5,13},{6,14},{7,15},{8,0},{9,1},... | collective-permute-start | bytes 147464 | tf_op jit(solution)/shard_map/ppermute | solution.py:569
  4.7 0.0 collective-permute-start.1
  4.7 2.1 %collective-permute-done.got_first = f32[96,128]{1,0:T(8,128)S(1)} collective-permute-done((f32[96,128]{1,0:T(8,128)S(1)}, f32[96,128]{1,0:T(8,128)S(1)}, u32[]{:S(2)}, u32[]{:S(2)}) %collective-permute-start) | collective-permute-done | bytes 49184 | tf_op jit(solution)/shard_map/ppermute | solution.py:569
  6.8 0.0 collective-permute-done.1.got_second
  6.8 0.2 strips.1
  7.1 0.1 collective-permute-start.2
  7.1 3.2 %collective-permute-start.3 = (f32[176,128]{1,0:T(8,128)S(1)}, f32[176,128]{1,0:T(8,128)S(1)}, u32[]{:S(2)}, u32[]{:S(2)}) collective-permute-start(f32[176,128]{1,0:T(8,128)S(1)} %get-tuple-element.21), channel_id=1, source_target_pairs={{0,8},{1,2},{2,1},{3,4},{4,3},{5,6},{6,5},{7,15},{8,0},{9,10},{10,... | collective-permute-start | bytes 270344 | tf_op jit(solution)/shard_map/ppermute | solution.py:580
  10.3 0.0 collective-permute-done.2.got_first
  10.3 2.5 %collective-permute-done.3.got_second = f32[176,128]{1,0:T(8,128)S(1)} collective-permute-done((f32[176,128]{1,0:T(8,128)S(1)}, f32[176,128]{1,0:T(8,128)S(1)}, u32[]{:S(2)}, u32[]{:S(2)}) %collective-permute-start.3) | collective-permute-done | bytes 90144 | tf_op jit(solution)/shard_map/ppermute | solution.py:580
  12.9 2.8 %down.1 = (f32[64,128]{1,0:T(8,128)S(1)}, f32[8,200,128]{2,1,0:T(8,128)S(1)}, f32[8,112,128]{2,1,0:T(8,128)S(1)}, f32[8,72,128]{2,1,0:T(8,128)S(1)}, f32[8,48,128]{2,1,0:T(8,128)S(1)}) custom-call(f32[4,200,128]{2,1,0:T(8,128)S(1)} %get-tuple-element.19.held, f32[176,128]{1,0:T(8,128)S(1)} %collective-permute-done.2.got_first, ...), custom_call_target="tpu_custom_call" | custom-call | tf_op jit(solution)/shard_map/down/pallas_call | solution.py:582
  15.7 12.8 %all_to_all.11 = f32[32,2,128]{2,1,0:T(2,128)S(1)} all-to-all(f32[32,2,128]{2,1,0:T(2,128)S(1)} %bitcast.3), channel_id=1, replica_groups=mesh['gx'=4,'gy'=8] {'gx','gy'}, dimensions={0} | all-to-all | bytes 65536 | tf_op jit(solution)/shard_map/all_to_all | solution.py:597
  28.5 3.3 %up.1 = f32[2,128,128]{2,1,0:T(8,128)} custom-call(f32[64,128]{1,0:T(8,128)S(1)} %bitcast.2, f32[4,200,128]{2,1,0:T(8,128)S(1)} %get-tuple-element.19.held, f32[8,200,128]{2,1,0:T(8,128)S(1)} %get-tuple-element.23.state0, f32[8,112,128]{2,1,0:T(8,128)S(1)} %get-tuple-element.24.state1, f32[8,72,128]{2,1,0:T(8,128)S(1)} %get-tuple-element.25.state2, ...), custom_call_target="tpu_custom_call" | custom-call | tf_op jit(solution)/shard_map/up/pallas_call | solution.py:600
Async XLA Ops:
  1.6 5.2 %collective-permute-start = (f32[96,128]{1,0:T(8,128)S(1)}, f32[96,128]{1,0:T(8,128)S(1)}, u32[]{:S(2)}, u32[]{:S(2)}) collective-permute-start(f32[96,128]{1,0:T(8,128)S(1)} %get-tuple-element.17), channel_id=1, source_target_pairs={{0,8},{1,9},{2,10},{3,11},{4,12},{5,13},{6,14},{7,15},{8,0},{9,1},... | collective-permute-start | bytes 147464 | tf_op jit(solution)/shard_map/ppermute | solution.py:569
  4.7 2.1 %collective-permute-start.1 = (f32[96,128]{1,0:T(8,128)S(1)}, f32[96,128]{1,0:T(8,128)S(1)}, u32[]{:S(2)}, u32[]{:S(2)}) collective-permute-start(f32[96,128]{1,0:T(8,128)S(1)} %get-tuple-element.18), channel_id=1, source_target_pairs={{0,1},{1,0},{2,3},{3,2},{4,5},{5,4},{6,7},{7,6},{8,16},{9,17},{10,... | collective-permute-start | bytes 147464 | tf_op jit(solution)/shard_map/ppermute | solution.py:568
  7.1 3.3 %collective-permute-start.2 = (f32[176,128]{1,0:T(8,128)S(1)}, f32[176,128]{1,0:T(8,128)S(1)}, u32[]{:S(2)}, u32[]{:S(2)}) collective-permute-start(f32[176,128]{1,0:T(8,128)S(1)} %get-tuple-element.20), channel_id=1, source_target_pairs={{0,1},{1,0},{2,3},{3,2},{4,5},{5,4},{6,7},{7,6},{8,9},{9,8},{10,11... | collective-permute-start | bytes 270344 | tf_op jit(solution)/shard_map/ppermute | solution.py:581
  7.1 5.7 %collective-permute-start.3 = (f32[176,128]{1,0:T(8,128)S(1)}, f32[176,128]{1,0:T(8,128)S(1)}, u32[]{:S(2)}, u32[]{:S(2)}) collective-permute-start(f32[176,128]{1,0:T(8,128)S(1)} %get-tuple-element.21), channel_id=1, source_target_pairs={{0,8},{1,2},{2,1},{3,4},{4,3},{5,6},{6,5},{7,15},{8,0},{9,10},{10,... | collective-permute-start | bytes 270344 | tf_op jit(solution)/shard_map/ppermute | solution.py:580

commit v3 on v0

v3 whole, which is shorter than its diff:
```python
import functools

import jax
import jax.numpy as jnp
from jax import lax
from jax.experimental import pallas as pl
from jax.experimental.pallas import tpu as pltpu
from jax.sharding import PartitionSpec as P

LOCAL = 4
COARSE = 4
COARSE_SWEEPS = 8
OMEGA = 0.8
KEEP = 1.0 - OMEGA

LANES = 128
HALF = LANES // 2
SUB = 8
HALO = 16
GUARD = 8
CELLS = LANES >> LOCAL
ROWS = [(LANES + 2 * HALO) >> level for level in range(LOCAL)]
TILES = [-(-rows // SUB) for rows in ROWS]
HELD = [GUARD + SUB * tiles + 16 for tiles in TILES]
RIM = [HALO >> level for level in range(LOCAL)]
TOP = GUARD + HALO
LOW = TOP + LANES
HALF_TILES = TILES[0] // 2
MESSAGE = ROWS[0] // 2
CHUNK = 4
F32 = jnp.float32
VMEM_LIMIT = 48 * 1024 * 1024

EVEN, ODD, LEFT_ODD, RIGHT_EVEN = range(4)
SWEPT, CENTRE, SIDE, ACROSS = 0, 4, 6, 8
STATE = 10
ITERATE, WEIGHT = 10, 14


def iota(dim, shape=(SUB, LANES)):
    return lax.broadcasted_iota(jnp.int32, shape, dim)


def lane_take(tile, index):
    return jnp.take_along_axis(tile, index, axis=1)


def lane_roll(tile, shift):
    return pltpu.roll(tile, shift % LANES, 1)


def tile_at(ref, slot, row):
    return ref[slot, row : row + SUB, :]


def bands_kernel(wet, right_side, shift_coef, viscosity, held, first, second, sems):
    odd = lax.axis_index("gx") % 2
    wetness = wet[0, 0].astype(F32)
    own = pl.ds(TOP, LANES)
    sources = (right_side.at[0], right_side.at[1], shift_coef, viscosity)
    copies = [
        pltpu.make_async_copy(sources[field], held.at[field, own, :], sems.at[field])
        for field in range(4)
    ]
    for copy in copies:
        copy.start()
    bottom = LANES - HALO
    starts = (TOP + bottom - bottom * odd, TOP + bottom * odd)
    for field in range(4):
        copies[field].wait()
        for start, out in zip(starts, (first, second)):
            value = held[field, pl.ds(pl.multiple_of(start, SUB), HALO), :]
            out[field * HALO : (field + 1) * HALO, :] = value if field == 2 else value * wetness


def strips_kernel(size_x, wet, before_held, got_first, got_second, held, first, second):
    index_x = lax.axis_index("gx")
    odd_x = index_x % 2 == 1
    odd_y = lax.axis_index("gy") % 2 == 1
    wetness = wet[0, 0].astype(F32)
    above = (index_x > 0).astype(F32)
    below = (index_x < size_x - 1).astype(F32)
    for field in range(4):
        rows = slice(field * HALO, (field + 1) * HALO)
        one, two = got_first[rows, :], got_second[rows, :]
        before = jnp.where(odd_x, one, two)
        after = jnp.where(odd_x, two, one)
        if field == 3:
            before, after = before * above, after * below
        held[field, GUARD:TOP, :] = before
        if field != 2:
            held[field, TOP:LOW, :] = before_held[field, TOP:LOW, :] * wetness
        held[field, LOW : LOW + HALO, :] = after
    lane = iota(1)
    for tile in range(HALF_TILES):
        left = right = None
        for half in range(2):
            row = GUARD + SUB * (tile + half * HALF_TILES)
            for field in range(4):
                value = held[field, row : row + SUB, :]
                place = HALF * half + HALO * field
                other = HALF * (1 - half) + HALO * field
                to_left = lane_roll(value, place)
                to_right = lane_roll(value, other - (LANES - HALO))
                if left is None:
                    left, right = to_left, to_right
                else:
                    left = jnp.where(lane >= place, to_left, left)
                    right = jnp.where((lane >= other) & (lane < other + HALO), to_right, right)
        rows = slice(SUB * tile, SUB * tile + SUB)
        first[rows, :] = jnp.where(odd_y, left, right)
        second[rows, :] = jnp.where(odd_y, right, left)


def down_kernel(size_y, devices, held, got_first, got_second, chunks, *refs):
    states, refs = refs[:LOCAL], refs[LOCAL:]
    fields, refs = refs[:LOCAL], refs[LOCAL:]
    iterates, refs = refs[:LOCAL], refs[LOCAL:]
    faces, refs = refs[:LOCAL], refs[LOCAL:]
    sums, ring = refs[:LOCAL], refs[LOCAL]
    index_y = lax.axis_index("gy")
    odd_y = index_y % 2 == 1
    lane, sub = iota(1), iota(0)
    side_ok = jnp.where(
        lane < 96, (index_y < size_y - 1).astype(F32), (index_y > 0).astype(F32)
    )
    odd_row = (sub & 1) == 1
    inner = lane < HALF

    spread = 2 * lane
    for tile in range(HALF_TILES):
        rows = slice(SUB * tile, SUB * tile + SUB)
        one, two = got_first[rows, :], got_second[rows, :]
        after = jnp.where(odd_y, two, one)
        before = jnp.where(odd_y, one, two)
        for half in range(2):
            row = GUARD + SUB * (tile + half * HALF_TILES)
            rims = jnp.where(inner, after, before) if half == 0 else jnp.where(inner, before, after)
            base = jnp.where((lane < 96) == (half == 0), 0, HALF) + 2 * (lane & 7)
            for field in range(4):
                own = held[field, row : row + SUB, :]
                for parity in range(2):
                    mine = lane_take(own, (spread + parity) & (LANES - 1))
                    rim = lane_take(rims, base + (HALO * field + parity))
                    if field == 3:
                        rim = rim * side_ok
                    fields[0][2 * field + parity, row : row + SUB, :] = jnp.where(inner, mine, rim)

    def source_slot(level, comp, kind):
        return 2 * comp + kind if level == 0 else 4 * comp + kind

    def iterate_slot(level, comp, kind):
        return 2 * comp + kind if level == 0 else 4 * comp + kind

    for level in range(LOCAL):
        field, iterate, face, state, summed = (
            fields[level],
            iterates[level],
            faces[level],
            states[level],
            sums[level],
        )
        reaction_at, viscous_at = (4, 6) if level == 0 else (8, 10)
        for tile in range(TILES[level]):
            row = GUARD + SUB * tile
            rows = slice(row, row + SUB)
            here = [tile_at(field, viscous_at + p, row) for p in range(2)]
            if level == 0:
                left_odd, right_even = lane_roll(here[1], 1), lane_roll(here[0], -1)
            else:
                left_odd = tile_at(field, viscous_at + LEFT_ODD, row)
                right_even = tile_at(field, viscous_at + RIGHT_EVEN, row)
            middle = jnp.minimum(here[0], here[1])
            outer = [jnp.minimum(here[0], left_odd), jnp.minimum(here[1], right_even)]
            face[0, rows, :] = middle
            weights = []
            for p in range(2):
                north = jnp.minimum(here[p], tile_at(field, viscous_at + p, row - 1))
                south = jnp.minimum(here[p], tile_at(field, viscous_at + p, row + 1))
                diagonal = tile_at(field, reaction_at + p, row) + (
                    (middle + outer[p]) + (north + south)
                )
                weights.append(OMEGA / diagonal)
                face[1 + p, rows, :] = outer[p]
                face[3 + p, rows, :] = south
                face[5 + p, rows, :] = weights[p]
            if level > 0:
                weights += [lane_roll(weights[1], 1), lane_roll(weights[0], -1)]
            for comp in range(2):
                for kind, weight in enumerate(weights):
                    iterate[iterate_slot(level, comp, kind), rows, :] = weight * tile_at(
                        field, source_slot(level, comp, kind), row
                    )
        for tile in range(TILES[level]):
            row = GUARD + SUB * tile
            rows = slice(row, row + SUB)
            middle = face[0, rows, :]
            outer = [face[1 + p, rows, :] for p in range(2)]
            south = [face[3 + p, rows, :] for p in range(2)]
            north = [tile_at(face, 3 + p, row - 1) for p in range(2)]
            weights = [face[5 + p, rows, :] for p in range(2)]
            for comp in range(2):
                here = [tile_at(iterate, iterate_slot(level, comp, p), row) for p in range(2)]
                if level == 0:
                    beyond = [lane_roll(here[1], 1), lane_roll(here[0], -1)]
                else:
                    beyond = [
                        tile_at(iterate, iterate_slot(level, comp, kind), row)
                        for kind in (LEFT_ODD, RIGHT_EVEN)
                    ]
                total = None
                for p in range(2):
                    slot = iterate_slot(level, comp, p)
                    around = middle * here[1 - p] + outer[p] * beyond[p]
                    around = around + (
                        south[p] * tile_at(iterate, slot, row + 1)
                        + north[p] * tile_at(iterate, slot, row - 1)
                    )
                    left = KEEP * tile_at(field, source_slot(level, comp, p), row) + around
                    state[SWEPT + 2 * comp + p, rows, :] = here[p] + weights[p] * left
                    if level == LOCAL - 1:
                        ring[2 * comp + p, rows, :] = left
                        state[ITERATE + 2 * comp + p, rows, :] = here[p]
                    total = left if total is None else total + left
                summed[comp, rows, :] = total
            for p in range(2):
                within = jnp.where(odd_row, north[p], south[p])
                across = jnp.where(odd_row, south[p], north[p])
                state[CENTRE + p, rows, :] = KEEP + weights[p] * (middle + within)
                state[SIDE + p, rows, :] = weights[p] * outer[p]
                state[ACROSS + p, rows, :] = weights[p] * across
                if level == LOCAL - 1:
                    state[WEIGHT + p, rows, :] = weights[p]

        def pairs(ref, slot, start):
            return (
                ref[slot, pl.ds(start, SUB, stride=2), :]
                + ref[slot, pl.ds(start + 1, SUB, stride=2), :]
            )

        def coefficient(at, start):
            return pairs(field, at, start) + pairs(field, at + 1, start)

        if level < LOCAL - 1:
            coarse = fields[level + 1]
            takes = [(spread + offset) & (LANES - 1) for offset in (0, 1, -1, 2)]
            for tile in range(TILES[level + 1]):
                start = GUARD + 2 * SUB * tile
                rows = slice(GUARD + SUB * tile, GUARD + SUB * tile + SUB)
                viscous = 0.0625 * coefficient(viscous_at, start)
                reaction = 0.25 * coefficient(reaction_at, start)
                for kind in range(4):
                    coarse[10 + kind, rows, :] = lane_take(viscous, takes[kind])
                for kind in range(2):
                    coarse[8 + kind, rows, :] = lane_take(reaction, takes[kind])
                for comp in range(2):
                    source = 0.25 * pairs(summed, comp, start)
                    for kind in range(4):
                        coarse[4 * comp + kind, rows, :] = lane_take(source, takes[kind])
            continue

        start = GUARD + RIM[level]
        column = lane & (SUB - 1)
        own = [
            lane_take(0.25 * pairs(summed, 0, start), column),
            lane_take(0.25 * pairs(summed, 1, start), column),
            lane_take(0.25 * coefficient(reaction_at, start), column),
            lane_take(0.0625 * coefficient(viscous_at, start), column),
        ]
        chosen = ((lane >> 3) & (SUB - 1)) == sub
        edge = (lane >> 4) & 3
        place = lane & 15

        def packed(value):
            return jnp.sum(value, axis=0, keepdims=True)

        def joined(a, b):
            return packed(jnp.where(chosen, jnp.where(inner, a, b), 0.0))

        rims = jnp.zeros((SUB, LANES), F32)
        for part in range(2):
            for p in range(2):
                index = jnp.where(edge < 2, column, 0 if p == 0 else SUB - 1)
                along = (edge == part) & ((place >> 3) == p) & (sub == (0 if part == 0 else SUB - 1))
                up = (edge == 2 + p) & (place == sub + SUB * part)
                row = start + SUB * part
                value = jnp.where(
                    inner,
                    lane_take(tile_at(ring, p, row), index),
                    lane_take(tile_at(ring, 2 + p, row), index),
                )
                rims = jnp.where(along | up, value, rims)
        kind = sub % CHUNK
        tile = jnp.where(
            kind == 0,
            joined(own[0], own[1]),
            jnp.where(kind == 1, joined(own[2], own[3]), jnp.where(kind == 2, packed(rims), 0.0)),
        )
        for block in range(CHUNK * devices // SUB):
            chunks[SUB * block : SUB * block + SUB, :] = tile


def coarse_solve(fields, rows_total, cols_total):
    shape = fields[0].shape
    width = shape[1]
    row, lane = iota(0, shape), iota(1, shape)

    def along(value, amount):
        return pltpu.roll(value, amount % width, 1)

    def down(value, amount):
        return pltpu.roll(value, amount % shape[0], 0)

    sources = fields[:2]
    reaction = jnp.where(lane < cols_total, fields[2], 1.0)
    viscous = fields[3]
    stored = []
    for level in range(COARSE):
        step = 1 << level
        odd_lane, odd_row = (lane & step) != 0, (row & step) != 0

        def paired(value):
            return (
                jnp.where(odd_lane, along(value, step), value),
                jnp.where(odd_lane, value, along(value, -step)),
            )

        def outside(value):
            return (
                jnp.where(odd_lane, along(value, 2 * step), along(value, step)),
                jnp.where(odd_lane, along(value, -step), along(value, -2 * step)),
            )

        here, reactions = paired(viscous), paired(reaction)
        beyond = outside(viscous)
        beyond = (
            jnp.where(lane < 2 * step, 0.0, beyond[0]),
            jnp.where(lane < cols_total - 2 * step, beyond[1], 0.0),
        )
        middle = jnp.minimum(here[0], here[1])
        outer = [jnp.minimum(a, b) for a, b in zip(here, beyond)]
        north, south, weights = [], [], []
        for p in range(2):
            above = jnp.where(row < step, 0.0, down(here[p], step))
            below = jnp.where(row < rows_total - step, down(here[p], -step), 0.0)
            north.append(jnp.minimum(here[p], above))
            south.append(jnp.minimum(here[p], below))
            diagonal = reactions[p] + ((middle + outer[p]) + (north[p] + south[p]))
            weights.append(OMEGA / diagonal)
        weights_beyond = (along(weights[1], 2 * step), along(weights[0], -2 * step))
        swept, remaining = [], []
        for source in sources:
            values, values_beyond = paired(source), outside(source)
            x = [w * s for w, s in zip(weights, values)]
            x_beyond = [w * s for w, s in zip(weights_beyond, values_beyond)]
            total = None
            for p in range(2):
                around = middle * x[1 - p] + outer[p] * x_beyond[p]
                around = around + (south[p] * down(x[p], -step) + north[p] * down(x[p], step))
                left = KEEP * values[p] + around
                swept.append(x[p] + weights[p] * left)
                total = left if total is None else total + left
            remaining.append(total)
        centre, side, across = [], [], []
        for p in range(2):
            within = jnp.where(odd_row, north[p], south[p])
            out = jnp.where(odd_row, south[p], north[p])
            centre.append(KEEP + weights[p] * (middle + within))
            side.append(weights[p] * outer[p])
            across.append(weights[p] * out)
        stored.append((step, odd_lane, odd_row, swept, centre, side, across))

        def folded(value, scale):
            return scale * (value + jnp.where(odd_row, down(value, step), down(value, -step)))

        sources = [folded(total, 0.25) for total in remaining]
        reaction = folded(reactions[0] + reactions[1], 0.25)
        viscous = folded(here[0] + here[1], 0.0625)

    block = 1 << COARSE
    rows_left, cols_left = rows_total // block, cols_total // block
    cells = [(i, j) for i in range(rows_left) for j in range(cols_left)]

    def spread_cells(value):
        found = {}
        for i, j in cells:
            column, place = divmod(block * j, LANES)
            tile = value[block * i : block * i + SUB, LANES * column : LANES * column + LANES]
            found[i, j] = lane_take(tile, jnp.full((SUB, LANES), place, jnp.int32))
        return found

    source_cells = [spread_cells(s) for s in sources]
    reaction_cells, viscous_cells = spread_cells(reaction), spread_cells(viscous)
    pulls, weight_cells = {}, {}
    for i, j in cells:
        near = [c for c in ((i - 1, j), (i + 1, j), (i, j - 1), (i, j + 1)) if c in viscous_cells]
        links = [(c, jnp.minimum(viscous_cells[i, j], viscous_cells[c])) for c in near]
        diagonal = reaction_cells[i, j] + sum(c for _, c in links)
        weight_cells[i, j] = OMEGA / diagonal
        pulls[i, j] = [(c, weight_cells[i, j] * link) for c, link in links]
    solved = []
    for comp in range(2):
        pushed = {c: weight_cells[c] * source_cells[comp][c] for c in cells}
        values = pushed
        for _ in range(COARSE_SWEEPS - 1):
            values = {
                c: (KEEP * values[c] + pushed[c])
                + sum(pull * values[other] for other, pull in pulls[c])
                for c in cells
            }
        solved.append(values)

    def laid(values, di, dj):
        tiles = []
        nothing = jnp.zeros((SUB, LANES), F32)
        for tile in range(shape[0] // SUB):
            i = SUB * tile // block
            if di:
                i += 1 if (SUB * tile // (block // 2)) % 2 else -1
            columns = []
            for column in range(width // LANES):
                place = iota(1) // block + column * (LANES // block)
                value = nothing
                for j in range(cols_left):
                    if (i, j) in values and column * LANES <= (j - dj) * block < (column + 1) * LANES:
                        value = jnp.where(place == j - dj, values[i, j], value)
                columns.append(value)
            tiles.append(columns[0] if len(columns) == 1 else jnp.concatenate(columns, 1))
        return jnp.concatenate(tiles, 0)

    corrections = None
    for step, odd_lane, odd_row, swept, centre, side, across in reversed(stored):
        found = []
        for comp in range(2):
            if corrections is None:
                here = laid(solved[comp], 0, 0)
                beyond = [laid(solved[comp], 0, -1), laid(solved[comp], 0, 1)]
                out = laid(solved[comp], 1, 0)
            else:
                here = corrections[comp]
                beyond = [along(here, 2 * step), along(here, -2 * step)]
                out = jnp.where(odd_row, down(here, -step), down(here, step))
            parts = [
                (swept[2 * comp + p] + centre[p] * here) + (side[p] * beyond[p] + across[p] * out)
                for p in range(2)
            ]
            found.append(jnp.where(odd_lane, parts[1], parts[0]))
        corrections = found
    return corrections


def up_kernel(size_x, size_y, gathered, state0, state1, state2, state3, out, *refs):
    grid, whole, swept3, corr1, corr2, corr3, merged0, merged1, merged2 = refs
    index_x, index_y = lax.axis_index("gx"), lax.axis_index("gy")
    rows_total, cols_total = CELLS * size_x, CELLS * size_y
    width = max(LANES, cols_total)
    columns = width // LANES
    per_column = LANES // CELLS
    lane, sub = iota(1), iota(0)

    tall = iota(1, (2 * size_x, LANES))
    for column in range(columns):
        targets = [[jnp.zeros((2 * size_x, LANES), F32)] * CELLS for _ in range(2)]
        for place in range(min(per_column, size_y - column * per_column)):
            j = column * per_column + place
            chunk = jnp.concatenate(
                [
                    gathered[pl.ds(CHUNK * j + h, size_x, stride=CHUNK * size_y), :]
                    for h in range(2)
                ],
                0,
            )
            mine = (tall // CELLS) == place
            turns = {}
            for half in range(2):
                for r in range(CELLS):
                    shift = (CELLS * (place - r) - half * HALF) % LANES
                    if shift not in turns:
                        turns[shift] = lane_roll(chunk, shift)
                    targets[half][r] = jnp.where(mine, turns[shift], targets[half][r])
        for half in range(2):
            for r in range(CELLS):
                for h in range(2):
                    grid[2 * h + half, column, pl.ds(r, size_x, stride=CELLS), :] = targets[half][r][
                        h * size_x : (h + 1) * size_x
                    ]
    fields = [
        jnp.concatenate([grid[f, c] for c in range(columns)], 1) if columns > 1 else grid[f, 0]
        for f in range(4)
    ]

    def ring_row(dx, dy):
        i = jnp.clip(index_x + dx, 0, size_x - 1)
        j = jnp.clip(index_y + dy, 0, size_y - 1)
        return jnp.broadcast_to(
            gathered[pl.ds(CHUNK * (i * size_y + j) + 2, 1), :], (SUB, LANES)
        )

    beside = {
        (dx, dy): ring_row(dx, dy) for dx in (-1, 0, 1) for dy in (-1, 0, 1) if dx or dy
    }
    start = GUARD + RIM[3]
    for comp in range(2):
        base = comp * HALF
        for p in range(2):
            slot = 2 * comp + p
            end = 7 if p else 0
            corner_lane = LANES - 1 if p else SUB
            dy = -1 if p else 1
            for tile in range(2):
                at = start + SUB * tile
                index = base + (48 if p else 32) + SUB * tile + sub
                ringed = lane_take(beside[0, dy], index)
                swept = jnp.where(
                    lane == corner_lane,
                    tile_at(state3, ITERATE + slot, at) + tile_at(state3, WEIGHT + p, at) * ringed,
                    tile_at(state3, SWEPT + slot, at),
                )
                swept3[slot, at : at + SUB, :] = swept
            for dx, at, edge in ((-1, start - 1, 16), (1, start + 2 * SUB, 0)):
                index = base + edge + 8 * p
                ringed = jnp.where(
                    lane == corner_lane,
                    lane_take(beside[dx, dy], jnp.full((SUB, LANES), index + end, jnp.int32)),
                    lane_take(beside[dx, 0], index + (lane & 7)),
                )
                rows = slice(at, at + 1)
                swept3[slot, rows, :] = (
                    state3[ITERATE + slot, rows, :] + state3[WEIGHT + p, rows, :] * ringed[0:1]
                )

    corrections = coarse_solve(fields, rows_total, cols_total)

    for comp in range(2):
        for kind in range(3):
            shift = (width - CELLS * index_y + (0, -1, 1)[kind] + width) % width
            turned = pltpu.roll(corrections[comp], shift, 1)
            if columns > 1:
                tall_lane = iota(1, (rows_total, LANES))
                turned = jnp.where(
                    tall_lane < HALF, turned[:, :LANES], turned[:, width - LANES :]
                )
            slot = 3 * comp + kind
            whole[slot, 2 * GUARD : 2 * GUARD + rows_total, :] = turned
            whole[slot, 0 : 2 * GUARD, :] = jnp.zeros((2 * GUARD, LANES), F32)
            whole[slot, 2 * GUARD + rows_total :, :] = jnp.zeros((3 * SUB, LANES), F32)

    def swept_rows(ref, level, coarse_row, parity, here, beyond, across, comp):
        at = pl.ds(GUARD + RIM[level] + 2 * coarse_row + parity, SUB, stride=2)
        state = (state0, state1, state2, state3)[level]
        return [
            (ref[SWEPT + 2 * comp + p, at, :] + state[CENTRE + p, at, :] * here)
            + (state[SIDE + p, at, :] * beyond[p] + state[ACROSS + p, at, :] * across)
            for p in range(2)
        ]

    base = pl.multiple_of(CELLS * index_x, SUB)
    for comp in range(2):
        window = [whole[3 * comp + kind, pl.ds(base, 6 * SUB), :] for kind in range(3)]
        for tile in range(2):
            first = SUB * tile - 1
            at = 2 * GUARD + first
            here, right, left = [w[at : at + SUB] for w in window]
            for parity in range(2):
                shifted = at + (1 if parity else -1)
                across = window[0][shifted : shifted + SUB]
                found = swept_rows(swept3, 3, first, parity, here, (left, right), across, comp)
                rows = pl.ds(GUARD + RIM[3] + 2 * first + parity, SUB, stride=2)
                for p in range(2):
                    corr3[2 * comp + p, rows, :] = found[p]

    corrs = [None, corr1, corr2, corr3]
    merged = [merged0, merged1, merged2]
    near = ((((lane + 32) & (LANES - 1)) - 32) >> 1) & (LANES - 1)
    odd_lane = (lane & 1) == 1
    for level in (2, 1, 0):
        coarse = level + 1
        corr, state, whole_rows = corrs[coarse], (state0, state1, state2)[level], merged[level]
        count = (LANES >> coarse) + 2
        origin = GUARD + RIM[coarse]
        sides = {}
        for tile in range(-(-count // SUB)):
            at = origin - 1 + SUB * tile
            for comp in range(2):
                even, odd = tile_at(corr, 2 * comp, at), tile_at(corr, 2 * comp + 1, at)
                even_here, odd_here = lane_take(even, near), lane_take(odd, near)
                even_next = lane_take(even, (near + 1) & (LANES - 1))
                odd_last = lane_take(odd, (near - 1) & (LANES - 1))
                here = jnp.where(odd_lane, odd_here, even_here)
                whole_rows[3 * comp, at : at + SUB, :] = here
                whole_rows[3 * comp + 1, at : at + SUB, :] = jnp.where(
                    odd_lane, even_next, odd_here
                )
                whole_rows[3 * comp + 2, at : at + SUB, :] = jnp.where(
                    odd_lane, even_here, odd_last
                )
        if level > 0:
            first, tiles = -1, -(-count // SUB)
        else:
            first, tiles = 0, (count - 2) // SUB
        for tile in range(tiles):
            coarse_row = first + SUB * tile
            at = origin + coarse_row
            for comp in range(2):
                here, right, left = [tile_at(whole_rows, 3 * comp + k, at) for k in range(3)]
                for parity in range(2):
                    across = tile_at(whole_rows, 3 * comp, at + (1 if parity else -1))
                    found = swept_rows(
                        state, level, coarse_row, parity, here, (left, right), across, comp
                    )
                    if level > 0:
                        rows = pl.ds(GUARD + RIM[level] + 2 * coarse_row + parity, SUB, stride=2)
                        for p in range(2):
                            corrs[level][2 * comp + p, rows, :] = found[p]
                    else:
                        rows = pl.ds(2 * coarse_row + parity, SUB, stride=2)
                        out[comp, rows, :] = jnp.where(
                            odd_lane,
                            lane_take(found[1], lane >> 1),
                            lane_take(found[0], lane >> 1),
                        )


def params():
    return pltpu.CompilerParams(vmem_limit_bytes=VMEM_LIMIT)


VMEM_SPEC = pl.BlockSpec(memory_space=pltpu.VMEM)
SMEM_SPEC = pl.BlockSpec(memory_space=pltpu.SMEM)
HBM_SPEC = pl.BlockSpec(memory_space=pltpu.HBM)


def swap_routes(size_x, size_y):
    def index(i, j):
        return i * size_y + j

    routes = []
    for axis in range(2):
        size = (size_x, size_y)[axis]
        for offset in range(2):
            route = []
            for i in range(size_x):
                for j in range(size_y):
                    here = (i, j)[axis]
                    other = here + 1 if here % 2 == offset else here - 1
                    if 0 <= other < size:
                        peer = (other, j) if axis == 0 else (i, other)
                    else:
                        peer = (i, j ^ 1) if axis == 0 else (i ^ 1, j)
                    route.append((index(i, j), index(*peer)))
            routes.append(route)
    return routes


def per_device(size_x, size_y, right_side, shift_coef, viscosity, wet_tiles):
    axes = ("gx", "gy")
    devices = size_x * size_y
    routes = swap_routes(size_x, size_y)
    band = jax.ShapeDtypeStruct((4 * HALO, LANES), F32)
    held_shape = pltpu.VMEM((4, HELD[0], LANES), F32)
    held, first, second = pl.pallas_call(
        bands_kernel,
        out_shape=(held_shape, band, band),
        in_specs=[SMEM_SPEC] + [HBM_SPEC] * 3,
        out_specs=(VMEM_SPEC,) * 3,
        scratch_shapes=[pltpu.SemaphoreType.DMA((4,))],
        compiler_params=params(),
        name="bands",
    )(
        wet_tiles,
        *[
            pltpu.with_memory_space_constraint(array, pltpu.HBM)
            for array in (right_side, shift_coef, viscosity)
        ],
    )
    second = lax.ppermute(second, axes, routes[1])
    first = lax.ppermute(first, axes, routes[0])
    strip = jax.ShapeDtypeStruct((MESSAGE, LANES), F32)
    held, first, second = pl.pallas_call(
        functools.partial(strips_kernel, size_x),
        out_shape=(held_shape, strip, strip),
        in_specs=[SMEM_SPEC] + [VMEM_SPEC] * 3,
        out_specs=(VMEM_SPEC,) * 3,
        input_output_aliases={1: 0},
        compiler_params=params(),
        name="strips",
    )(wet_tiles, held, first, second)
    second = lax.ppermute(second, axes, routes[3])
    first = lax.ppermute(first, axes, routes[2])

    def buffers(counts):
        return [pltpu.VMEM((n, HELD[level], LANES), F32) for level, n in enumerate(counts)]

    chunks, *states = pl.pallas_call(
        functools.partial(down_kernel, size_y, devices),
        out_shape=(jax.ShapeDtypeStruct((CHUNK * devices, LANES), F32),)
        + tuple(buffers([STATE, STATE, STATE, STATE + 6])),
        in_specs=[VMEM_SPEC] * 3,
        out_specs=(VMEM_SPEC,) * (1 + LOCAL),
        scratch_shapes=buffers([8, 14, 14, 14])
        + buffers([4, 8, 8, 8])
        + buffers([7] * 4)
        + buffers([2] * 4)
        + [pltpu.VMEM((4, HELD[3], LANES), F32)],
        compiler_params=params(),
        name="down",
    )(held, first, second)
    gathered = lax.all_to_all(chunks, axes, 0, 0, tiled=True)
    rows_total = CELLS * size_x
    columns = max(LANES, CELLS * size_y) // LANES
    return pl.pallas_call(
        functools.partial(up_kernel, size_x, size_y),
        out_shape=jax.ShapeDtypeStruct((2, LANES, LANES), F32),
        in_specs=[VMEM_SPEC] * (1 + LOCAL),
        out_specs=VMEM_SPEC,
        scratch_shapes=[
            pltpu.VMEM((4, columns, rows_total, LANES), F32),
            pltpu.VMEM((6, rows_total + 5 * SUB, LANES), F32),
            pltpu.VMEM((4, HELD[3], LANES), F32),
        ]
        + [pltpu.VMEM((4, HELD[level], LANES), F32) for level in (1, 2, 3)]
        + [pltpu.VMEM((6, HELD[level + 1], LANES), F32) for level in (0, 1, 2)],
        compiler_params=params(),
        name="up",
    )(gathered, *states)


def solution(mesh):
    sizes = dict(mesh.shape)
    placed = (P(None, "gx", "gy"), P("gx", "gy"), P("gx", "gy"), P("gx", "gy"))
    return jax.shard_map(
        functools.partial(per_device, sizes["gx"], sizes["gy"]),
        mesh=mesh,
        in_specs=placed,
        out_specs=P(None, "gx", "gy"),
        check_vma=False,
    )
```

time: 223 us -> 29.7 us (0.13)
  the two profiles are of different devices: /device:TPU:3 before, /device:TPU:0 now
where the time goes in v3:
time: 29.7 us; the launch traced here: 29.5 us
  blocking collectives  12.4 us (42%)
  starting transfers between devices  6.37 us (21%)
  Pallas kernels  6.16 us (21%)
  waiting for transfers between devices  3.87 us (13%)
  between operations  0.69 us (2%)
    all_to_all x1, blocking collectives, per_device(): gathered = lax.all_to_all(chunks, axes, 0, 0, tiled=True)  12.4 us
    ppermute x1, starting transfers between devices, per_device(): second = lax.ppermute(second, axes, routes[3])  3.21 us
    ppermute x1, starting transfers between devices, per_device(): first = lax.ppermute(first, axes, routes[0])  3.09 us
    pallas_call x1, Pallas kernels, per_device(): pl.pallas_call(functools.partial(up_kernel, size_x, size_y), out_shape=ja...  2.7 us
    pallas_call x1, Pallas kernels, per_device(): pl.pallas_call(functools.partial(down_kernel, size_y, devices), out_shape...  2.23 us
    ppermute x1, waiting for transfers between devices, per_device(): second = lax.ppermute(second, axes, routes[3])  1.98 us
    ppermute x1, waiting for transfers between devices, per_device(): first = lax.ppermute(first, axes, routes[0])  1.89 us
    pallas_call x1, Pallas kernels, per_device(): pl.pallas_call(bands_kernel, out_shape=(held_shape, band, band), in_specs...  0.97 us
  transfers between devices with their start and end apart: 4, of which 2 were waited for; matrix products, arithmetic and copies ran while one was open for 0% of the time, Pallas kernels for 0%

profile of v3, /device:TPU:0, one launch (start us, length us, event | category | flops | bytes accessed | tf_op | source)
XLA Modules:
  0.0 29.5 jit_solution(17253156886934985973)
XLA Ops:
  0.7 1.0 %bands.1 = (f32[4,184,128]{2,1,0:T(8,128)S(1)}, f32[64,128]{1,0:T(8,128)S(1)}, f32[64,128]{1,0:T(8,128)S(1)}) custom-call(s32[1,1]{1,0:T(1,128)S(6)} %copy.7.wet, f32[2,128,128]{2,1,0:T(8,128)} %right_side.1, f32[128,128]{1,0:T(8,128)} %shift_coef.1, f32[128,128]{1,0:T(8,128)} %viscosity.1), custom_call_target="tpu_custom_call" | custom-call | tf_op jit(solution)/shard_map/bands/pallas_call | solution.py:661
  1.6 3.1 %collective-permute-start = (f32[64,128]{1,0:T(8,128)S(1)}, f32[64,128]{1,0:T(8,128)S(1)}, u32[]{:S(2)}, u32[]{:S(2)}) collective-permute-start(f32[64,128]{1,0:T(8,128)S(1)} %get-tuple-element.17), channel_id=1, source_target_pairs={{0,8},{1,9},{2,10},{3,11},{4,12},{5,13},{6,14},{7,15},{8,0},{9,1},... | collective-permute-start | bytes 98312 | tf_op jit(solution)/shard_map/ppermute | solution.py:677
  4.7 0.0 collective-permute-start.1
  4.7 1.9 %collective-permute-done.got_first = f32[64,128]{1,0:T(8,128)S(1)} collective-permute-done((f32[64,128]{1,0:T(8,128)S(1)}, f32[64,128]{1,0:T(8,128)S(1)}, u32[]{:S(2)}, u32[]{:S(2)}) %collective-permute-start) | collective-permute-done | bytes 32800 | tf_op jit(solution)/shard_map/ppermute | solution.py:677
  6.6 0.0 collective-permute-done.1.got_second
  6.6 0.2 strips.1
  6.9 0.1 collective-permute-start.2
  7.0 3.2 %collective-permute-start.3 = (f32[80,128]{1,0:T(8,128)S(1)}, f32[80,128]{1,0:T(8,128)S(1)}, u32[]{:S(2)}, u32[]{:S(2)}) collective-permute-start(f32[80,128]{1,0:T(8,128)S(1)} %get-tuple-element.21), channel_id=1, source_target_pairs={{0,8},{1,2},{2,1},{3,4},{4,3},{5,6},{6,5},{7,15},{8,0},{9,10},{10,... | collective-permute-start | bytes 122888 | tf_op jit(solution)/shard_map/ppermute | solution.py:688
  10.2 0.0 collective-permute-done.2.got_first
  10.2 2.0 %collective-permute-done.3.got_second = f32[80,128]{1,0:T(8,128)S(1)} collective-permute-done((f32[80,128]{1,0:T(8,128)S(1)}, f32[80,128]{1,0:T(8,128)S(1)}, u32[]{:S(2)}, u32[]{:S(2)}) %collective-permute-start.3) | collective-permute-done | bytes 40992 | tf_op jit(solution)/shard_map/ppermute | solution.py:688
  12.2 2.2 %down.1 = (f32[128,128]{1,0:T(8,128)S(1)}, f32[10,184,128]{2,1,0:T(8,128)S(1)}, f32[10,104,128]{2,1,0:T(8,128)S(1)}, f32[10,64,128]{2,1,0:T(8,128)S(1)}, f32[16,48,128]{2,1,0:T(8,128)S(1)}) custom-call(f32[4,184,128]{2,1,0:T(8,128)S(1)} %get-tuple-element.19.held, f32[80,128]{1,0:T(8,128)S(1)} %collective-permute-done.2.got_first, ...), custom_call_target="tpu_custom_call" | custom-call | tf_op jit(solution)/shard_map/down/pallas_call | solution.py:694
  14.4 12.4 %all_to_all.11 = f32[32,4,128]{2,1,0:T(4,128)S(1)} all-to-all(f32[32,4,128]{2,1,0:T(4,128)S(1)} %bitcast.3), channel_id=1, replica_groups=mesh['gx'=4,'gy'=8] {'gx','gy'}, dimensions={0} | all-to-all | bytes 131072 | tf_op jit(solution)/shard_map/all_to_all | solution.py:708
  26.8 2.7 %up.1 = f32[2,128,128]{2,1,0:T(8,128)} custom-call(f32[128,128]{1,0:T(8,128)S(1)} %bitcast.2, f32[10,184,128]{2,1,0:T(8,128)S(1)} %get-tuple-element.23.state0, f32[10,104,128]{2,1,0:T(8,128)S(1)} %get-tuple-element.24.state1, f32[10,64,128]{2,1,0:T(8,128)S(1)} %get-tuple-element.25.state2, f32[16,48,128]{2,1,0:T(8,128)S(1)} %get-tuple-element.26.state3), custom_call_target="tpu_custom_call" | custom-call | tf_op jit(solution)/shard_map/up/pallas_call | solution.py:711
Async XLA Ops:
  1.6 5.0 %collective-permute-start = (f32[64,128]{1,0:T(8,128)S(1)}, f32[64,128]{1,0:T(8,128)S(1)}, u32[]{:S(2)}, u32[]{:S(2)}) collective-permute-start(f32[64,128]{1,0:T(8,128)S(1)} %get-tuple-element.17), channel_id=1, source_target_pairs={{0,8},{1,9},{2,10},{3,11},{4,12},{5,13},{6,14},{7,15},{8,0},{9,1},... | collective-permute-start | bytes 98312 | tf_op jit(solution)/shard_map/ppermute | solution.py:677
  4.7 1.9 %collective-permute-start.1 = (f32[64,128]{1,0:T(8,128)S(1)}, f32[64,128]{1,0:T(8,128)S(1)}, u32[]{:S(2)}, u32[]{:S(2)}) collective-permute-start(f32[64,128]{1,0:T(8,128)S(1)} %get-tuple-element.18), channel_id=1, source_target_pairs={{0,1},{1,0},{2,3},{3,2},{4,5},{5,4},{6,7},{7,6},{8,16},{9,17},{10,... | collective-permute-start | bytes 98312 | tf_op jit(solution)/shard_map/ppermute | solution.py:676
  6.9 3.3 %collective-permute-start.2 = (f32[80,128]{1,0:T(8,128)S(1)}, f32[80,128]{1,0:T(8,128)S(1)}, u32[]{:S(2)}, u32[]{:S(2)}) collective-permute-start(f32[80,128]{1,0:T(8,128)S(1)} %get-tuple-element.20), channel_id=1, source_target_pairs={{0,1},{1,0},{2,3},{3,2},{4,5},{5,4},{6,7},{7,6},{8,9},{9,8},{10,11... | collective-permute-start | bytes 122888 | tf_op jit(solution)/shard_map/ppermute | solution.py:689
  7.0 5.2 %collective-permute-start.3 = (f32[80,128]{1,0:T(8,128)S(1)}, f32[80,128]{1,0:T(8,128)S(1)}, u32[]{:S(2)}, u32[]{:S(2)}) collective-permute-start(f32[80,128]{1,0:T(8,128)S(1)} %get-tuple-element.21), channel_id=1, source_target_pairs={{0,8},{1,2},{2,1},{3,4},{4,3},{5,6},{6,5},{7,15},{8,0},{9,10},{10,... | collective-permute-start | bytes 122888 | tf_op jit(solution)/shard_map/ppermute | solution.py:688

commit v4 on v3

--- a/solution.py
+++ b/solution.py
@@ -112,7 +112,7 @@
         second[rows, :] = jnp.where(odd_y, right, left)
 
 
-def down_kernel(size_y, devices, held, got_first, got_second, chunks, *refs):
+def down_kernel(size_y, devices, got_second, got_first, held, chunks, *refs):
     states, refs = refs[:LOCAL], refs[LOCAL:]
     fields, refs = refs[:LOCAL], refs[LOCAL:]
     iterates, refs = refs[:LOCAL], refs[LOCAL:]
@@ -704,7 +704,7 @@
         + [pltpu.VMEM((4, HELD[3], LANES), F32)],
         compiler_params=params(),
         name="down",
-    )(held, first, second)
+    )(second, first, held)
     gathered = lax.all_to_all(chunks, axes, 0, 0, tiled=True)
     rows_total = CELLS * size_x
     columns = max(LANES, CELLS * size_y) // LANES

time: 29.7 us -> 29.6 us (level)
  no operation moved by 1% of the time
where the time goes in v4:
time: 29.6 us; the launch traced here: 29.4 us
  blocking collectives  12.4 us (42%)
  starting transfers between devices  6.3 us (21%)
  Pallas kernels  6.16 us (21%)
  waiting for transfers between devices  3.87 us (13%)
  between operations  0.68 us (2%)
    all_to_all x1, blocking collectives, per_device(): gathered = lax.all_to_all(chunks, axes, 0, 0, tiled=True)  12.4 us
    ppermute x1, starting transfers between devices, per_device(): second = lax.ppermute(second, axes, routes[3])  3.21 us
    ppermute x1, starting transfers between devices, per_device(): first = lax.ppermute(first, axes, routes[0])  3.09 us
    pallas_call x1, Pallas kernels, per_device(): pl.pallas_call(functools.partial(up_kernel, size_x, size_y), out_shape=ja...  2.7 us
    pallas_call x1, Pallas kernels, per_device(): pl.pallas_call(functools.partial(down_kernel, size_y, devices), out_shape...  2.23 us
    ppermute x1, waiting for transfers between devices, per_device(): second = lax.ppermute(second, axes, routes[3])  1.98 us
    ppermute x1, waiting for transfers between devices, per_device(): first = lax.ppermute(first, axes, routes[0])  1.89 us
    pallas_call x1, Pallas kernels, per_device(): pl.pallas_call(bands_kernel, out_shape=(held_shape, band, band), in_specs...  0.97 us
  transfers between devices with their start and end apart: 4, of which 2 were waited for; matrix products, arithmetic and copies ran while one was open for 0% of the time, Pallas kernels for 0%

profile of v4, /device:TPU:0, one launch (start us, length us, event | category | flops | bytes accessed | tf_op | source)
XLA Modules:
  0.0 29.4 jit_solution(17774221226288556197)
XLA Ops:
  0.7 1.0 %bands.1 = (f32[4,184,128]{2,1,0:T(8,128)S(1)}, f32[64,128]{1,0:T(8,128)S(1)}, f32[64,128]{1,0:T(8,128)S(1)}) custom-call(s32[1,1]{1,0:T(1,128)S(6)} %copy.7.wet, f32[2,128,128]{2,1,0:T(8,128)} %right_side.1, f32[128,128]{1,0:T(8,128)} %shift_coef.1, f32[128,128]{1,0:T(8,128)} %viscosity.1), custom_call_target="tpu_custom_call" | custom-call | tf_op jit(solution)/shard_map/bands/pallas_call | solution.py:661
  1.6 3.1 %collective-permute-start = (f32[64,128]{1,0:T(8,128)S(1)}, f32[64,128]{1,0:T(8,128)S(1)}, u32[]{:S(2)}, u32[]{:S(2)}) collective-permute-start(f32[64,128]{1,0:T(8,128)S(1)} %get-tuple-element.17), channel_id=1, source_target_pairs={{0,8},{1,9},{2,10},{3,11},{4,12},{5,13},{6,14},{7,15},{8,0},{9,1},... | collective-permute-start | bytes 98312 | tf_op jit(solution)/shard_map/ppermute | solution.py:677
  4.7 0.0 collective-permute-start.1
  4.7 1.9 %collective-permute-done.got_first = f32[64,128]{1,0:T(8,128)S(1)} collective-permute-done((f32[64,128]{1,0:T(8,128)S(1)}, f32[64,128]{1,0:T(8,128)S(1)}, u32[]{:S(2)}, u32[]{:S(2)}) %collective-permute-start) | collective-permute-done | bytes 32800 | tf_op jit(solution)/shard_map/ppermute | solution.py:677
  6.6 0.0 collective-permute-done.1.got_second
  6.6 0.2 strips.1
  6.9 3.2 %collective-permute-start.2 = (f32[80,128]{1,0:T(8,128)S(1)}, f32[80,128]{1,0:T(8,128)S(1)}, u32[]{:S(2)}, u32[]{:S(2)}) collective-permute-start(f32[80,128]{1,0:T(8,128)S(1)} %get-tuple-element.19), channel_id=1, source_target_pairs={{0,8},{1,2},{2,1},{3,4},{4,3},{5,6},{6,5},{7,15},{8,0},{9,10},{10,... | collective-permute-start | bytes 122888 | tf_op jit(solution)/shard_map/ppermute | solution.py:688
  10.1 0.0 collective-permute-start.3
  10.1 2.0 %collective-permute-done.2.got_second = f32[80,128]{1,0:T(8,128)S(1)} collective-permute-done((f32[80,128]{1,0:T(8,128)S(1)}, f32[80,128]{1,0:T(8,128)S(1)}, u32[]{:S(2)}, u32[]{:S(2)}) %collective-permute-start.2) | collective-permute-done | bytes 40992 | tf_op jit(solution)/shard_map/ppermute | solution.py:688
  12.1 0.0 collective-permute-done.3.got_first
  12.1 2.2 %down.1 = (f32[128,128]{1,0:T(8,128)S(1)}, f32[10,184,128]{2,1,0:T(8,128)S(1)}, f32[10,104,128]{2,1,0:T(8,128)S(1)}, f32[10,64,128]{2,1,0:T(8,128)S(1)}, f32[16,48,128]{2,1,0:T(8,128)S(1)}) custom-call(f32[80,128]{1,0:T(8,128)S(1)} %collective-permute-done.2.got_second, f32[80,128]{1,0:T(8,128)S(1)} %collective-permute-done.3.got_first, ...), custom_call_target="tpu_custom_call" | custom-call | tf_op jit(solution)/shard_map/down/pallas_call | solution.py:694
  14.3 12.4 %all_to_all.11 = f32[32,4,128]{2,1,0:T(4,128)S(1)} all-to-all(f32[32,4,128]{2,1,0:T(4,128)S(1)} %bitcast.3), channel_id=1, replica_groups=mesh['gx'=4,'gy'=8] {'gx','gy'}, dimensions={0} | all-to-all | bytes 131072 | tf_op jit(solution)/shard_map/all_to_all | solution.py:708
  26.7 2.7 %up.1 = f32[2,128,128]{2,1,0:T(8,128)} custom-call(f32[128,128]{1,0:T(8,128)S(1)} %bitcast.2, f32[10,184,128]{2,1,0:T(8,128)S(1)} %get-tuple-element.23.state0, f32[10,104,128]{2,1,0:T(8,128)S(1)} %get-tuple-element.24.state1, f32[10,64,128]{2,1,0:T(8,128)S(1)} %get-tuple-element.25.state2, f32[16,48,128]{2,1,0:T(8,128)S(1)} %get-tuple-element.26.state3), custom_call_target="tpu_custom_call" | custom-call | tf_op jit(solution)/shard_map/up/pallas_call | solution.py:711
Async XLA Ops:
  1.6 5.0 %collective-permute-start = (f32[64,128]{1,0:T(8,128)S(1)}, f32[64,128]{1,0:T(8,128)S(1)}, u32[]{:S(2)}, u32[]{:S(2)}) collective-permute-start(f32[64,128]{1,0:T(8,128)S(1)} %get-tuple-element.17), channel_id=1, source_target_pairs={{0,8},{1,9},{2,10},{3,11},{4,12},{5,13},{6,14},{7,15},{8,0},{9,1},... | collective-permute-start | bytes 98312 | tf_op jit(solution)/shard_map/ppermute | solution.py:677
  4.7 1.9 %collective-permute-start.1 = (f32[64,128]{1,0:T(8,128)S(1)}, f32[64,128]{1,0:T(8,128)S(1)}, u32[]{:S(2)}, u32[]{:S(2)}) collective-permute-start(f32[64,128]{1,0:T(8,128)S(1)} %get-tuple-element.18), channel_id=1, source_target_pairs={{0,1},{1,0},{2,3},{3,2},{4,5},{5,4},{6,7},{7,6},{8,16},{9,17},{10,... | collective-permute-start | bytes 98312 | tf_op jit(solution)/shard_map/ppermute | solution.py:676
  6.9 5.2 %collective-permute-start.2 = (f32[80,128]{1,0:T(8,128)S(1)}, f32[80,128]{1,0:T(8,128)S(1)}, u32[]{:S(2)}, u32[]{:S(2)}) collective-permute-start(f32[80,128]{1,0:T(8,128)S(1)} %get-tuple-element.19), channel_id=1, source_target_pairs={{0,8},{1,2},{2,1},{3,4},{4,3},{5,6},{6,5},{7,15},{8,0},{9,10},{10,... | collective-permute-start | bytes 122888 | tf_op jit(solution)/shard_map/ppermute | solution.py:688
  10.1 2.0 %collective-permute-start.3 = (f32[80,128]{1,0:T(8,128)S(1)}, f32[80,128]{1,0:T(8,128)S(1)}, u32[]{:S(2)}, u32[]{:S(2)}) collective-permute-start(f32[80,128]{1,0:T(8,128)S(1)} %get-tuple-element.20), channel_id=1, source_target_pairs={{0,1},{1,0},{2,3},{3,2},{4,5},{5,4},{6,7},{7,6},{8,9},{9,8},{10,11... | collective-permute-start | bytes 122888 | tf_op jit(solution)/shard_map/ppermute | solution.py:689

commit v5 on v4

--- a/solution.py
+++ b/solution.py
@@ -31,7 +31,6 @@
 F32 = jnp.float32
 VMEM_LIMIT = 48 * 1024 * 1024
 
-EVEN, ODD, LEFT_ODD, RIGHT_EVEN = range(4)
 SWEPT, CENTRE, SIDE, ACROSS = 0, 4, 6, 8
 STATE = 10
 ITERATE, WEIGHT = 10, 14
@@ -73,50 +72,86 @@
             out[field * HALO : (field + 1) * HALO, :] = value if field == 2 else value * wetness
 
 
-def strips_kernel(size_x, wet, before_held, got_first, got_second, held, first, second):
+def rim_place(half, lane):
+    to_left = ((lane >> 3) & 1) == half
+    q = jnp.where(to_left, lane, (lane - (56 + 8 * half)) & (LANES - 1)) >> 4
+    cell = 2 * (lane & 7) + (q & 1) + jnp.where(to_left, 0, LANES - HALO)
+    return to_left, q >> 1, cell
+
+
+def strips_kernel(size_x, wet, held, got_first, got_second, first, second):
     index_x = lax.axis_index("gx")
     odd_x = index_x % 2 == 1
     odd_y = lax.axis_index("gy") % 2 == 1
     wetness = wet[0, 0].astype(F32)
     above = (index_x > 0).astype(F32)
     below = (index_x < size_x - 1).astype(F32)
-    for field in range(4):
-        rows = slice(field * HALO, (field + 1) * HALO)
-        one, two = got_first[rows, :], got_second[rows, :]
-        before = jnp.where(odd_x, one, two)
-        after = jnp.where(odd_x, two, one)
-        if field == 3:
-            before, after = before * above, after * below
-        held[field, GUARD:TOP, :] = before
-        if field != 2:
-            held[field, TOP:LOW, :] = before_held[field, TOP:LOW, :] * wetness
-        held[field, LOW : LOW + HALO, :] = after
     lane = iota(1)
+    rim_tiles = HALO // SUB
+
+    def piece(field, tile):
+        if rim_tiles <= tile < TILES[0] - rim_tiles:
+            row = GUARD + SUB * tile
+            return held[field, row : row + SUB, :]
+        top = tile < rim_tiles
+        row = field * HALO + SUB * (tile if top else tile - (TILES[0] - rim_tiles))
+        one, two = got_first[row : row + SUB, :], got_second[row : row + SUB, :]
+        return jnp.where(odd_x, one, two) if top else jnp.where(odd_x, two, one)
+
+    places = [rim_place(half, lane) for half in range(2)]
     for tile in range(HALF_TILES):
-        left = right = None
+        found = []
         for half in range(2):
-            row = GUARD + SUB * (tile + half * HALF_TILES)
+            to_left, owner, cell = places[half]
+            at = tile + half * HALF_TILES
+            value = None
             for field in range(4):
-                value = held[field, row : row + SUB, :]
-                place = HALF * half + HALO * field
-                other = HALF * (1 - half) + HALO * field
-                to_left = lane_roll(value, place)
-                to_right = lane_roll(value, other - (LANES - HALO))
-                if left is None:
-                    left, right = to_left, to_right
-                else:
-                    left = jnp.where(lane >= place, to_left, left)
-                    right = jnp.where((lane >= other) & (lane < other + HALO), to_right, right)
+                part = lane_take(piece(field, at), cell)
+                value = part if value is None else jnp.where(owner == field, part, value)
+            if rim_tiles <= at < TILES[0] - rim_tiles:
+                value = value * jnp.where(owner == 2, 1.0, wetness)
+            else:
+                value = value * jnp.where(owner == 3, above if at < rim_tiles else below, 1.0)
+            found.append(value)
+        left = jnp.where(places[0][0], found[0], found[1])
+        right = jnp.where(places[0][0], found[1], found[0])
         rows = slice(SUB * tile, SUB * tile + SUB)
         first[rows, :] = jnp.where(odd_y, left, right)
         second[rows, :] = jnp.where(odd_y, right, left)
 
 
+def halves_kernel(size_x, wet, held, got_first, got_second, fields):
+    index_x = lax.axis_index("gx")
+    odd_x = index_x % 2 == 1
+    wetness = wet[0, 0].astype(F32)
+    above = (index_x > 0).astype(F32)
+    below = (index_x < size_x - 1).astype(F32)
+    lane = iota(1)
+    rim_tiles = HALO // SUB
+    for tile in range(TILES[0]):
+        row = GUARD + SUB * tile
+        for field in range(4):
+            if rim_tiles <= tile < TILES[0] - rim_tiles:
+                value = held[field, row : row + SUB, :]
+                if field != 2:
+                    value = value * wetness
+            else:
+                top = tile < rim_tiles
+                at = field * HALO + SUB * (tile if top else tile - (TILES[0] - rim_tiles))
+                one, two = got_first[at : at + SUB, :], got_second[at : at + SUB, :]
+                value = jnp.where(odd_x, one, two) if top else jnp.where(odd_x, two, one)
+                if field == 3:
+                    value = value * (above if top else below)
+            for parity in range(2):
+                fields[2 * field + parity, row : row + SUB, :] = lane_take(
+                    value, (2 * lane + parity) & (LANES - 1)
+                )
+
+
 def down_kernel(size_y, devices, got_second, got_first, held, chunks, *refs):
     states, refs = refs[:LOCAL], refs[LOCAL:]
-    fields, refs = refs[:LOCAL], refs[LOCAL:]
+    viscous, refs = refs[:LOCAL], refs[LOCAL:]
     iterates, refs = refs[:LOCAL], refs[LOCAL:]
-    faces, refs = refs[:LOCAL], refs[LOCAL:]
     sums, ring = refs[:LOCAL], refs[LOCAL]
     index_y = lax.axis_index("gy")
     odd_y = index_y % 2 == 1
@@ -126,103 +161,95 @@
     )
     odd_row = (sub & 1) == 1
     inner = lane < HALF
-
-    spread = 2 * lane
-    for tile in range(HALF_TILES):
-        rows = slice(SUB * tile, SUB * tile + SUB)
-        one, two = got_first[rows, :], got_second[rows, :]
-        after = jnp.where(odd_y, two, one)
-        before = jnp.where(odd_y, one, two)
-        for half in range(2):
-            row = GUARD + SUB * (tile + half * HALF_TILES)
-            rims = jnp.where(inner, after, before) if half == 0 else jnp.where(inner, before, after)
-            base = jnp.where((lane < 96) == (half == 0), 0, HALF) + 2 * (lane & 7)
-            for field in range(4):
-                own = held[field, row : row + SUB, :]
-                for parity in range(2):
-                    mine = lane_take(own, (spread + parity) & (LANES - 1))
-                    rim = lane_take(rims, base + (HALO * field + parity))
-                    if field == 3:
-                        rim = rim * side_ok
-                    fields[0][2 * field + parity, row : row + SUB, :] = jnp.where(inner, mine, rim)
-
-    def source_slot(level, comp, kind):
-        return 2 * comp + kind if level == 0 else 4 * comp + kind
-
-    def iterate_slot(level, comp, kind):
-        return 2 * comp + kind if level == 0 else 4 * comp + kind
-
-    for level in range(LOCAL):
-        field, iterate, face, state, summed = (
-            fields[level],
-            iterates[level],
-            faces[level],
-            states[level],
-            sums[level],
+    even_block = ((lane >> 3) & 1) == 0
+
+    def finest(tile):
+        half, at = divmod(tile, HALF_TILES)
+        one, two = (r[SUB * at : SUB * at + SUB, :] for r in (got_first, got_second))
+        after, before = jnp.where(odd_y, two, one), jnp.where(odd_y, one, two)
+        rims = jnp.where(even_block, after, before) if half == 0 else jnp.where(
+            even_block, before, after
         )
-        reaction_at, viscous_at = (4, 6) if level == 0 else (8, 10)
-        for tile in range(TILES[level]):
-            row = GUARD + SUB * tile
-            rows = slice(row, row + SUB)
-            here = [tile_at(field, viscous_at + p, row) for p in range(2)]
+        row = GUARD + SUB * tile
+        values = []
+        for slot in range(8):
+            rim = lane_roll(rims, HALF - 16 * slot - 8 * half)
+            if slot >= 4:
+                rim = jnp.where(side_ok > 0, rim, 1.0 if slot < 6 else 0.0)
+            values.append(jnp.where(inner, held[slot, row : row + SUB, :], rim))
+        return [values[0:2], values[2:4]], values[4:6], values[6:8]
+
+    def paired(ref, slot, start):
+        return (
+            ref[slot, pl.ds(start, SUB, stride=2), :] + ref[slot, pl.ds(start + 1, SUB, stride=2), :]
+        )
+
+    takes = [(2 * lane + offset) & (LANES - 1) for offset in (0, 1, -1, 2)]
+
+    def coarser(level):
+        def load(tile):
+            start = GUARD + 2 * SUB * tile
+            ref = sums[level - 1]
+            reaction = 0.25 * paired(ref, 2, start)
+            viscosity = 0.0625 * paired(ref, 3, start)
+            sources = [0.25 * paired(ref, comp, start) for comp in range(2)]
+            return (
+                [[lane_take(s, t) for t in takes] for s in sources],
+                [lane_take(reaction, t) for t in takes[:2]],
+                [lane_take(viscosity, t) for t in takes],
+            )
+
+        return load
+
+    def faces(level, row, fields):
+        sources, reaction, here = fields
+        if level == 0:
+            left_odd, right_even = lane_roll(here[1], 1), lane_roll(here[0], -1)
+        else:
+            left_odd, right_even = here[2:]
+        middle = jnp.minimum(here[0], here[1])
+        outer = [jnp.minimum(here[0], left_odd), jnp.minimum(here[1], right_even)]
+        north, south, weights = [], [], []
+        for p in range(2):
+            north.append(jnp.minimum(here[p], tile_at(viscous[level], p, row - 1)))
+            south.append(jnp.minimum(here[p], tile_at(viscous[level], p, row + 1)))
+            weights.append(OMEGA / (reaction[p] + ((middle + outer[p]) + (north[p] + south[p]))))
+        if level > 0:
+            weights += [lane_roll(weights[1], 1), lane_roll(weights[0], -1)]
+        swept = [[w * s for w, s in zip(weights, source)] for source in sources]
+        for comp in range(2):
+            for p in range(2):
+                iterates[level][2 * comp + p, row : row + SUB, :] = swept[comp][p]
+        return sources, middle, outer, north, south, weights, swept
+
+    def residual(level, row, values):
+        sources, middle, outer, north, south, weights, swept = values
+        state, iterate = states[level], iterates[level]
+        rows = slice(row, row + SUB)
+        kept = level > 0 or TOP <= row < LOW
+        for comp in range(2):
+            here = swept[comp][:2]
             if level == 0:
-                left_odd, right_even = lane_roll(here[1], 1), lane_roll(here[0], -1)
+                beyond = [lane_roll(here[1], 1), lane_roll(here[0], -1)]
             else:
-                left_odd = tile_at(field, viscous_at + LEFT_ODD, row)
-                right_even = tile_at(field, viscous_at + RIGHT_EVEN, row)
-            middle = jnp.minimum(here[0], here[1])
-            outer = [jnp.minimum(here[0], left_odd), jnp.minimum(here[1], right_even)]
-            face[0, rows, :] = middle
-            weights = []
+                beyond = swept[comp][2:]
+            total = None
             for p in range(2):
-                north = jnp.minimum(here[p], tile_at(field, viscous_at + p, row - 1))
-                south = jnp.minimum(here[p], tile_at(field, viscous_at + p, row + 1))
-                diagonal = tile_at(field, reaction_at + p, row) + (
-                    (middle + outer[p]) + (north + south)
+                slot = 2 * comp + p
+                around = middle * here[1 - p] + outer[p] * beyond[p]
+                around = around + (
+                    south[p] * tile_at(iterate, slot, row + 1)
+                    + north[p] * tile_at(iterate, slot, row - 1)
                 )
-                weights.append(OMEGA / diagonal)
-                face[1 + p, rows, :] = outer[p]
-                face[3 + p, rows, :] = south
-                face[5 + p, rows, :] = weights[p]
-            if level > 0:
-                weights += [lane_roll(weights[1], 1), lane_roll(weights[0], -1)]
-            for comp in range(2):
-                for kind, weight in enumerate(weights):
-                    iterate[iterate_slot(level, comp, kind), rows, :] = weight * tile_at(
-                        field, source_slot(level, comp, kind), row
-                    )
-        for tile in range(TILES[level]):
-            row = GUARD + SUB * tile
-            rows = slice(row, row + SUB)
-            middle = face[0, rows, :]
-            outer = [face[1 + p, rows, :] for p in range(2)]
-            south = [face[3 + p, rows, :] for p in range(2)]
-            north = [tile_at(face, 3 + p, row - 1) for p in range(2)]
-            weights = [face[5 + p, rows, :] for p in range(2)]
-            for comp in range(2):
-                here = [tile_at(iterate, iterate_slot(level, comp, p), row) for p in range(2)]
-                if level == 0:
-                    beyond = [lane_roll(here[1], 1), lane_roll(here[0], -1)]
-                else:
-                    beyond = [
-                        tile_at(iterate, iterate_slot(level, comp, kind), row)
-                        for kind in (LEFT_ODD, RIGHT_EVEN)
-                    ]
-                total = None
-                for p in range(2):
-                    slot = iterate_slot(level, comp, p)
-                    around = middle * here[1 - p] + outer[p] * beyond[p]
-                    around = around + (
-                        south[p] * tile_at(iterate, slot, row + 1)
-                        + north[p] * tile_at(iterate, slot, row - 1)
-                    )
-                    left = KEEP * tile_at(field, source_slot(level, comp, p), row) + around
-                    state[SWEPT + 2 * comp + p, rows, :] = here[p] + weights[p] * left
-                    if level == LOCAL - 1:
-                        ring[2 * comp + p, rows, :] = left
-                        state[ITERATE + 2 * comp + p, rows, :] = here[p]
-                    total = left if total is None else total + left
-                summed[comp, rows, :] = total
+                left = KEEP * sources[comp][p] + around
+                if kept:
+                    state[SWEPT + slot, rows, :] = here[p] + weights[p] * left
+                if level == LOCAL - 1:
+                    ring[slot, rows, :] = left
+                    state[ITERATE + slot, rows, :] = here[p]
+                total = left if total is None else total + left
+            sums[level][comp, rows, :] = total
+        if kept:
             for p in range(2):
                 within = jnp.where(odd_row, north[p], south[p])
                 across = jnp.where(odd_row, south[p], north[p])
@@ -232,72 +259,61 @@
                 if level == LOCAL - 1:
                     state[WEIGHT + p, rows, :] = weights[p]
 
-        def pairs(ref, slot, start):
-            return (
-                ref[slot, pl.ds(start, SUB, stride=2), :]
-                + ref[slot, pl.ds(start + 1, SUB, stride=2), :]
+    for level in range(LOCAL):
+        load = finest if level == 0 else coarser(level)
+        loaded, swept = {}, {}
+        for turn in range(TILES[level] + 2):
+            if turn < TILES[level]:
+                row = GUARD + SUB * turn
+                loaded[turn] = load(turn)
+                _, reaction, here = loaded[turn]
+                for p in range(2):
+                    viscous[level][p, row : row + SUB, :] = here[p]
+                sums[level][2, row : row + SUB, :] = reaction[0] + reaction[1]
+                sums[level][3, row : row + SUB, :] = here[0] + here[1]
+            if 0 <= turn - 1 < TILES[level]:
+                row = GUARD + SUB * (turn - 1)
+                swept[turn - 1] = faces(level, row, loaded.pop(turn - 1))
+            if turn >= 2:
+                residual(level, GUARD + SUB * (turn - 2), swept.pop(turn - 2))
+
+    start = GUARD + RIM[LOCAL - 1]
+    column = lane & (SUB - 1)
+    own = [
+        lane_take(scale * paired(sums[LOCAL - 1], slot, start), column)
+        for slot, scale in enumerate((0.25, 0.25, 0.25, 0.0625))
+    ]
+    chosen = ((lane >> 3) & (SUB - 1)) == sub
+    edge = (lane >> 4) & 3
+    place = lane & 15
+
+    def packed(value):
+        return jnp.sum(value, axis=0, keepdims=True)
+
+    def joined(a, b):
+        return packed(jnp.where(chosen, jnp.where(inner, a, b), 0.0))
+
+    rims = jnp.zeros((SUB, LANES), F32)
+    for p in range(2):
+        index = jnp.where(edge < 2, column, 0 if p == 0 else SUB - 1)
+        for part in range(2):
+            along = (edge == part) & ((place >> 3) == p) & (sub == (0 if part == 0 else SUB - 1))
+            up = (edge == 2 + p) & (place == sub + SUB * part)
+            row = start + SUB * part
+            value = jnp.where(
+                inner,
+                lane_take(tile_at(ring, p, row), index),
+                lane_take(tile_at(ring, 2 + p, row), index),
             )
-
-        def coefficient(at, start):
-            return pairs(field, at, start) + pairs(field, at + 1, start)
-
-        if level < LOCAL - 1:
-            coarse = fields[level + 1]
-            takes = [(spread + offset) & (LANES - 1) for offset in (0, 1, -1, 2)]
-            for tile in range(TILES[level + 1]):
-                start = GUARD + 2 * SUB * tile
-                rows = slice(GUARD + SUB * tile, GUARD + SUB * tile + SUB)
-                viscous = 0.0625 * coefficient(viscous_at, start)
-                reaction = 0.25 * coefficient(reaction_at, start)
-                for kind in range(4):
-                    coarse[10 + kind, rows, :] = lane_take(viscous, takes[kind])
-                for kind in range(2):
-                    coarse[8 + kind, rows, :] = lane_take(reaction, takes[kind])
-                for comp in range(2):
-                    source = 0.25 * pairs(summed, comp, start)
-                    for kind in range(4):
-                        coarse[4 * comp + kind, rows, :] = lane_take(source, takes[kind])
-            continue
-
-        start = GUARD + RIM[level]
-        column = lane & (SUB - 1)
-        own = [
-            lane_take(0.25 * pairs(summed, 0, start), column),
-            lane_take(0.25 * pairs(summed, 1, start), column),
-            lane_take(0.25 * coefficient(reaction_at, start), column),
-            lane_take(0.0625 * coefficient(viscous_at, start), column),
-        ]
-        chosen = ((lane >> 3) & (SUB - 1)) == sub
-        edge = (lane >> 4) & 3
-        place = lane & 15
-
-        def packed(value):
-            return jnp.sum(value, axis=0, keepdims=True)
-
-        def joined(a, b):
-            return packed(jnp.where(chosen, jnp.where(inner, a, b), 0.0))
-
-        rims = jnp.zeros((SUB, LANES), F32)
-        for part in range(2):
-            for p in range(2):
-                index = jnp.where(edge < 2, column, 0 if p == 0 else SUB - 1)
-                along = (edge == part) & ((place >> 3) == p) & (sub == (0 if part == 0 else SUB - 1))
-                up = (edge == 2 + p) & (place == sub + SUB * part)
-                row = start + SUB * part
-                value = jnp.where(
-                    inner,
-                    lane_take(tile_at(ring, p, row), index),
-                    lane_take(tile_at(ring, 2 + p, row), index),
-                )
-                rims = jnp.where(along | up, value, rims)
-        kind = sub % CHUNK
-        tile = jnp.where(
-            kind == 0,
-            joined(own[0], own[1]),
-            jnp.where(kind == 1, joined(own[2], own[3]), jnp.where(kind == 2, packed(rims), 0.0)),
-        )
-        for block in range(CHUNK * devices // SUB):
-            chunks[SUB * block : SUB * block + SUB, :] = tile
+            rims = jnp.where(along | up, value, rims)
+    kind = sub % CHUNK
+    tile = jnp.where(
+        kind == 0,
+        joined(own[0], own[1]),
+        jnp.where(kind == 1, joined(own[2], own[3]), jnp.where(kind == 2, packed(rims), 0.0)),
+    )
+    for block in range(CHUNK * devices // SUB):
+        chunks[SUB * block : SUB * block + SUB, :] = tile
 
 
 def coarse_solve(fields, rows_total, cols_total):
@@ -676,15 +692,24 @@
     second = lax.ppermute(second, axes, routes[1])
     first = lax.ppermute(first, axes, routes[0])
     strip = jax.ShapeDtypeStruct((MESSAGE, LANES), F32)
-    held, first, second = pl.pallas_call(
+    got = (first, second)
+    first, second = pl.pallas_call(
         functools.partial(strips_kernel, size_x),
-        out_shape=(held_shape, strip, strip),
+        out_shape=(strip, strip),
         in_specs=[SMEM_SPEC] + [VMEM_SPEC] * 3,
-        out_specs=(VMEM_SPEC,) * 3,
-        input_output_aliases={1: 0},
+        out_specs=(VMEM_SPEC,) * 2,
         compiler_params=params(),
         name="strips",
-    )(wet_tiles, held, first, second)
+    )(wet_tiles, held, *got)
+    fields = pl.pallas_call(
+        functools.partial(halves_kernel, size_x),
+        out_shape=pltpu.VMEM((8, HELD[0], LANES), F32),
+        in_specs=[SMEM_SPEC] + [VMEM_SPEC] * 3,
+        out_specs=VMEM_SPEC,
+        cost_estimate=pl.CostEstimate(flops=1 << 20, bytes_accessed=1 << 21, transcendentals=0),
+        compiler_params=params(),
+        name="halves",
+    )(wet_tiles, held, *got)
     second = lax.ppermute(second, axes, routes[3])
     first = lax.ppermute(first, axes, routes[2])
 
@@ -697,14 +722,13 @@
         + tuple(buffers([STATE, STATE, STATE, STATE + 6])),
         in_specs=[VMEM_SPEC] * 3,
         out_specs=(VMEM_SPEC,) * (1 + LOCAL),
-        scratch_shapes=buffers([8, 14, 14, 14])
-        + buffers([4, 8, 8, 8])
-        + buffers([7] * 4)
-        + buffers([2] * 4)
+        scratch_shapes=buffers([2] * 4)
+        + buffers([4] * 4)
+        + buffers([4] * 4)
         + [pltpu.VMEM((4, HELD[3], LANES), F32)],
         compiler_params=params(),
         name="down",
-    )(second, first, held)
+    )(second, first, fields)
     gathered = lax.all_to_all(chunks, axes, 0, 0, tiled=True)
     rows_total = CELLS * size_x
     columns = max(LANES, CELLS * size_y) // LANES

time: 29.6 us -> 29.9 us (1.010)
  Pallas kernels: 6.16 us -> 6.72 us
    pallas_call x1, Pallas kernels: 2.23 us -> 2.58 us  [per_device(): pl.pallas_call(functools.partial(down_kernel, size_y, devices), out_shape...]
  transfers between devices with their start and end apart: 4 -> 4, of which waited for: 2 -> 2; matrix products, arithmetic and copies ran while one was open for 0% -> 0% of each run, Pallas kernels for 0% -> 1%
where the time goes in v5:
time: 29.9 us; the launch traced here: 29.7 us
  blocking collectives  12.4 us (41%)
  Pallas kernels  6.72 us (22%)
  starting transfers between devices  6.3 us (21%)
  waiting for transfers between devices  3.63 us (12%)
  between operations  0.68 us (2%)
    all_to_all x1, blocking collectives, per_device(): gathered = lax.all_to_all(chunks, axes, 0, 0, tiled=True)  12.4 us
    ppermute x1, starting transfers between devices, per_device(): second = lax.ppermute(second, axes, routes[3])  3.21 us
    ppermute x1, starting transfers between devices, per_device(): first = lax.ppermute(first, axes, routes[0])  3.09 us
    pallas_call x1, Pallas kernels, per_device(): pl.pallas_call(functools.partial(up_kernel, size_x, size_y), out_shape=ja...  2.7 us
    pallas_call x1, Pallas kernels, per_device(): pl.pallas_call(functools.partial(down_kernel, size_y, devices), out_shape...  2.58 us
    ppermute x1, waiting for transfers between devices, per_device(): first = lax.ppermute(first, axes, routes[0])  1.89 us
    ppermute x1, waiting for transfers between devices, per_device(): second = lax.ppermute(second, axes, routes[3])  1.73 us
    pallas_call x1, Pallas kernels, per_device(): pl.pallas_call(bands_kernel, out_shape=(held_shape, band, band), in_specs...  0.97 us
  transfers between devices with their start and end apart: 4, of which 2 were waited for; matrix products, arithmetic and copies ran while one was open for 0% of the time, Pallas kernels for 1%

profile of v5, /device:TPU:0, one launch (start us, length us, event | category | flops | bytes accessed | tf_op | source)
XLA Modules:
  0.0 29.7 jit_solution(6800842480072054290)
XLA Ops:
  0.7 1.0 %bands.1 = (f32[4,184,128]{2,1,0:T(8,128)S(1)}, f32[64,128]{1,0:T(8,128)S(1)}, f32[64,128]{1,0:T(8,128)S(1)}) custom-call(s32[1,1]{1,0:T(1,128)S(6)} %copy.5.wet, f32[2,128,128]{2,1,0:T(8,128)} %right_side.1, f32[128,128]{1,0:T(8,128)} %shift_coef.1, f32[128,128]{1,0:T(8,128)} %viscosity.1), custom_call_target="tpu_custom_call" | custom-call | tf_op jit(solution)/shard_map/bands/pallas_call | solution.py:677
  1.6 3.1 %collective-permute-start = (f32[64,128]{1,0:T(8,128)S(1)}, f32[64,128]{1,0:T(8,128)S(1)}, u32[]{:S(2)}, u32[]{:S(2)}) collective-permute-start(f32[64,128]{1,0:T(8,128)S(1)} %get-tuple-element.16), channel_id=1, source_target_pairs={{0,8},{1,9},{2,10},{3,11},{4,12},{5,13},{6,14},{7,15},{8,0},{9,1},... | collective-permute-start | bytes 98312 | tf_op jit(solution)/shard_map/ppermute | solution.py:693
  4.7 0.0 collective-permute-start.1
  4.7 1.9 %collective-permute-done.got_first = f32[64,128]{1,0:T(8,128)S(1)} collective-permute-done((f32[64,128]{1,0:T(8,128)S(1)}, f32[64,128]{1,0:T(8,128)S(1)}, u32[]{:S(2)}, u32[]{:S(2)}) %collective-permute-start) | collective-permute-done | bytes 32800 | tf_op jit(solution)/shard_map/ppermute | solution.py:693
  6.6 0.0 collective-permute-done.1.got_second
  6.6 0.2 strips.1
  6.8 3.2 %collective-permute-start.2 = (f32[80,128]{1,0:T(8,128)S(1)}, f32[80,128]{1,0:T(8,128)S(1)}, u32[]{:S(2)}, u32[]{:S(2)}) collective-permute-start(f32[80,128]{1,0:T(8,128)S(1)} %get-tuple-element.18), channel_id=1, source_target_pairs={{0,8},{1,2},{2,1},{3,4},{4,3},{5,6},{6,5},{7,15},{8,0},{9,10},{10,... | collective-permute-start | bytes 122888 | tf_op jit(solution)/shard_map/ppermute | solution.py:713
  10.1 0.0 collective-permute-start.3
  10.1 0.2 halves.1.held
  10.3 1.7 %collective-permute-done.2.got_second = f32[80,128]{1,0:T(8,128)S(1)} collective-permute-done((f32[80,128]{1,0:T(8,128)S(1)}, f32[80,128]{1,0:T(8,128)S(1)}, u32[]{:S(2)}, u32[]{:S(2)}) %collective-permute-start.2) | collective-permute-done | bytes 40992 | tf_op jit(solution)/shard_map/ppermute | solution.py:713
  12.0 0.0 collective-permute-done.3.got_first
  12.0 2.6 %down.1 = (f32[128,128]{1,0:T(8,128)S(1)}, f32[10,184,128]{2,1,0:T(8,128)S(1)}, f32[10,104,128]{2,1,0:T(8,128)S(1)}, f32[10,64,128]{2,1,0:T(8,128)S(1)}, f32[16,48,128]{2,1,0:T(8,128)S(1)}) custom-call(f32[80,128]{1,0:T(8,128)S(1)} %collective-permute-done.2.got_second, f32[80,128]{1,0:T(8,128)S(1)} %collective-permute-done.3.got_first, ...), custom_call_target="tpu_custom_call" | custom-call | tf_op jit(solution)/shard_map/down/pallas_call | solution.py:719
  14.6 12.4 %all_to_all.11 = f32[32,4,128]{2,1,0:T(4,128)S(1)} all-to-all(f32[32,4,128]{2,1,0:T(4,128)S(1)} %bitcast.3), channel_id=1, replica_groups=mesh['gx'=4,'gy'=8] {'gx','gy'}, dimensions={0} | all-to-all | bytes 131072 | tf_op jit(solution)/shard_map/all_to_all | solution.py:732
  27.0 2.7 %up.1 = f32[2,128,128]{2,1,0:T(8,128)} custom-call(f32[128,128]{1,0:T(8,128)S(1)} %bitcast.2, f32[10,184,128]{2,1,0:T(8,128)S(1)} %get-tuple-element.21.state0, f32[10,104,128]{2,1,0:T(8,128)S(1)} %get-tuple-element.22.state1, f32[10,64,128]{2,1,0:T(8,128)S(1)} %get-tuple-element.23.state2, f32[16,48,128]{2,1,0:T(8,128)S(1)} %get-tuple-element.24.state3), custom_call_target="tpu_custom_call" | custom-call | tf_op jit(solution)/shard_map/up/pallas_call | solution.py:735
Async XLA Ops:
  1.6 5.0 %collective-permute-start = (f32[64,128]{1,0:T(8,128)S(1)}, f32[64,128]{1,0:T(8,128)S(1)}, u32[]{:S(2)}, u32[]{:S(2)}) collective-permute-start(f32[64,128]{1,0:T(8,128)S(1)} %get-tuple-element.16), channel_id=1, source_target_pairs={{0,8},{1,9},{2,10},{3,11},{4,12},{5,13},{6,14},{7,15},{8,0},{9,1},... | collective-permute-start | bytes 98312 | tf_op jit(solution)/shard_map/ppermute | solution.py:693
  4.7 1.9 %collective-permute-start.1 = (f32[64,128]{1,0:T(8,128)S(1)}, f32[64,128]{1,0:T(8,128)S(1)}, u32[]{:S(2)}, u32[]{:S(2)}) collective-permute-start(f32[64,128]{1,0:T(8,128)S(1)} %get-tuple-element.17), channel_id=1, source_target_pairs={{0,1},{1,0},{2,3},{3,2},{4,5},{5,4},{6,7},{7,6},{8,16},{9,17},{10,... | collective-permute-start | bytes 98312 | tf_op jit(solution)/shard_map/ppermute | solution.py:692
  6.8 5.2 %collective-permute-start.2 = (f32[80,128]{1,0:T(8,128)S(1)}, f32[80,128]{1,0:T(8,128)S(1)}, u32[]{:S(2)}, u32[]{:S(2)}) collective-permute-start(f32[80,128]{1,0:T(8,128)S(1)} %get-tuple-element.18), channel_id=1, source_target_pairs={{0,8},{1,2},{2,1},{3,4},{4,3},{5,6},{6,5},{7,15},{8,0},{9,10},{10,... | collective-permute-start | bytes 122888 | tf_op jit(solution)/shard_map/ppermute | solution.py:713
  10.1 2.0 %collective-permute-start.3 = (f32[80,128]{1,0:T(8,128)S(1)}, f32[80,128]{1,0:T(8,128)S(1)}, u32[]{:S(2)}, u32[]{:S(2)}) collective-permute-start(f32[80,128]{1,0:T(8,128)S(1)} %get-tuple-element.19), channel_id=1, source_target_pairs={{0,1},{1,0},{2,3},{3,2},{4,5},{5,4},{6,7},{7,6},{8,9},{9,8},{10,11... | collective-permute-start | bytes 122888 | tf_op jit(solution)/shard_map/ppermute | solution.py:714

commit v6 on v5

--- a/solution.py
+++ b/solution.py
@@ -151,8 +151,11 @@
 def down_kernel(size_y, devices, got_second, got_first, held, chunks, *refs):
     states, refs = refs[:LOCAL], refs[LOCAL:]
     viscous, refs = refs[:LOCAL], refs[LOCAL:]
+    reactions, refs = refs[:LOCAL], refs[LOCAL:]
+    sources, refs = refs[:LOCAL], refs[LOCAL:]
+    weights, refs = refs[:LOCAL], refs[LOCAL:]
     iterates, refs = refs[:LOCAL], refs[LOCAL:]
-    sums, ring = refs[:LOCAL], refs[LOCAL]
+    sums, (outers, ring) = refs[:LOCAL], refs[LOCAL:]
     index_y = lax.axis_index("gy")
     odd_y = index_y % 2 == 1
     lane, sub = iota(1), iota(0)
@@ -163,21 +166,27 @@
     inner = lane < HALF
     even_block = ((lane >> 3) & 1) == 0
 
-    def finest(tile):
-        half, at = divmod(tile, HALF_TILES)
+    def tiles(level):
+        return [GUARD + SUB * tile for tile in range(TILES[level])]
+
+    def put(ref, slot, row, value):
+        ref[slot, row : row + SUB, :] = value
+
+    def rims(row, slots):
+        half, at = divmod((row - GUARD) // SUB, HALF_TILES)
         one, two = (r[SUB * at : SUB * at + SUB, :] for r in (got_first, got_second))
         after, before = jnp.where(odd_y, two, one), jnp.where(odd_y, one, two)
-        rims = jnp.where(even_block, after, before) if half == 0 else jnp.where(
-            even_block, before, after
-        )
-        row = GUARD + SUB * tile
+        if half == 0:
+            both = jnp.where(even_block, after, before)
+        else:
+            both = jnp.where(even_block, before, after)
         values = []
-        for slot in range(8):
-            rim = lane_roll(rims, HALF - 16 * slot - 8 * half)
+        for slot in slots:
+            rim = lane_roll(both, HALF - 16 * slot - 8 * half)
             if slot >= 4:
                 rim = jnp.where(side_ok > 0, rim, 1.0 if slot < 6 else 0.0)
-            values.append(jnp.where(inner, held[slot, row : row + SUB, :], rim))
-        return [values[0:2], values[2:4]], values[4:6], values[6:8]
+            values.append(jnp.where(inner, tile_at(held, slot, row), rim))
+        return values
 
     def paired(ref, slot, start):
         return (
@@ -186,96 +195,151 @@
 
     takes = [(2 * lane + offset) & (LANES - 1) for offset in (0, 1, -1, 2)]
 
-    def coarser(level):
-        def load(tile):
-            start = GUARD + 2 * SUB * tile
-            ref = sums[level - 1]
-            reaction = 0.25 * paired(ref, 2, start)
-            viscosity = 0.0625 * paired(ref, 3, start)
-            sources = [0.25 * paired(ref, comp, start) for comp in range(2)]
-            return (
-                [[lane_take(s, t) for t in takes] for s in sources],
-                [lane_take(reaction, t) for t in takes[:2]],
-                [lane_take(viscosity, t) for t in takes],
-            )
-
-        return load
-
-    def faces(level, row, fields):
-        sources, reaction, here = fields
+    def coefficients(level):
+        for row in tiles(level):
+            if level == 0:
+                values = rims(row, (4, 5, 6, 7))
+                reaction, viscosity = values[:2], values[2:]
+            else:
+                start = GUARD + 2 * (row - GUARD)
+                ref = sums[level - 1]
+                value = 0.0625 * paired(ref, 3, start)
+                viscosity = [lane_take(value, t) for t in takes]
+                value = 0.25 * paired(ref, 2, start)
+                reaction = [lane_take(value, t) for t in takes[:2]]
+            for slot, value in enumerate(viscosity):
+                put(viscous[level], slot, row, value)
+            for slot, value in enumerate(reaction):
+                put(reactions[level], slot, row, value)
+            put(sums[level], 2, row, reaction[0] + reaction[1])
+            put(sums[level], 3, row, viscosity[0] + viscosity[1])
+
+    def faces(level, row):
+        here = [tile_at(viscous[level], p, row) for p in range(2)]
+        north = [jnp.minimum(here[p], tile_at(viscous[level], p, row - 1)) for p in range(2)]
+        south = [jnp.minimum(here[p], tile_at(viscous[level], p, row + 1)) for p in range(2)]
+        return here, jnp.minimum(here[0], here[1]), north, south
+
+    def outside(level, row, here):
         if level == 0:
-            left_odd, right_even = lane_roll(here[1], 1), lane_roll(here[0], -1)
+            beyond = [lane_roll(here[1], 1), lane_roll(here[0], -1)]
         else:
-            left_odd, right_even = here[2:]
-        middle = jnp.minimum(here[0], here[1])
-        outer = [jnp.minimum(here[0], left_odd), jnp.minimum(here[1], right_even)]
-        north, south, weights = [], [], []
-        for p in range(2):
-            north.append(jnp.minimum(here[p], tile_at(viscous[level], p, row - 1)))
-            south.append(jnp.minimum(here[p], tile_at(viscous[level], p, row + 1)))
-            weights.append(OMEGA / (reaction[p] + ((middle + outer[p]) + (north[p] + south[p]))))
-        if level > 0:
-            weights += [lane_roll(weights[1], 1), lane_roll(weights[0], -1)]
-        swept = [[w * s for w, s in zip(weights, source)] for source in sources]
-        for comp in range(2):
+            beyond = [tile_at(viscous[level], 2 + p, row) for p in range(2)]
+        return [jnp.minimum(h, b) for h, b in zip(here, beyond)]
+
+    def weigh(level):
+        for row in tiles(level):
+            here, middle, north, south = faces(level, row)
+            outer = outside(level, row, here)
+            found = []
             for p in range(2):
-                iterates[level][2 * comp + p, row : row + SUB, :] = swept[comp][p]
-        return sources, middle, outer, north, south, weights, swept
-
-    def residual(level, row, values):
-        sources, middle, outer, north, south, weights, swept = values
-        state, iterate = states[level], iterates[level]
-        rows = slice(row, row + SUB)
-        kept = level > 0 or TOP <= row < LOW
-        for comp in range(2):
-            here = swept[comp][:2]
+                diagonal = tile_at(reactions[level], p, row) + (
+                    (middle + outer[p]) + (north[p] + south[p])
+                )
+                found.append(OMEGA / diagonal)
+                if level == 0:
+                    put(outers, p, row, outer[p])
+            if level > 0:
+                found += [lane_roll(found[1], 1), lane_roll(found[0], -1)]
+            for slot, value in enumerate(found):
+                put(weights[level], slot, row, value)
+
+    def take_sources(level):
+        for row in tiles(level):
             if level == 0:
-                beyond = [lane_roll(here[1], 1), lane_roll(here[0], -1)]
+                found = rims(row, (0, 1, 2, 3))
             else:
-                beyond = swept[comp][2:]
-            total = None
-            for p in range(2):
-                slot = 2 * comp + p
-                around = middle * here[1 - p] + outer[p] * beyond[p]
-                around = around + (
-                    south[p] * tile_at(iterate, slot, row + 1)
-                    + north[p] * tile_at(iterate, slot, row - 1)
-                )
-                left = KEEP * sources[comp][p] + around
-                if kept:
-                    state[SWEPT + slot, rows, :] = here[p] + weights[p] * left
-                if level == LOCAL - 1:
-                    ring[slot, rows, :] = left
-                    state[ITERATE + slot, rows, :] = here[p]
-                total = left if total is None else total + left
-            sums[level][comp, rows, :] = total
-        if kept:
-            for p in range(2):
-                within = jnp.where(odd_row, north[p], south[p])
-                across = jnp.where(odd_row, south[p], north[p])
-                state[CENTRE + p, rows, :] = KEEP + weights[p] * (middle + within)
-                state[SIDE + p, rows, :] = weights[p] * outer[p]
-                state[ACROSS + p, rows, :] = weights[p] * across
-                if level == LOCAL - 1:
-                    state[WEIGHT + p, rows, :] = weights[p]
-
-    for level in range(LOCAL):
-        load = finest if level == 0 else coarser(level)
-        loaded, swept = {}, {}
-        for turn in range(TILES[level] + 2):
-            if turn < TILES[level]:
-                row = GUARD + SUB * turn
-                loaded[turn] = load(turn)
-                _, reaction, here = loaded[turn]
+                start = GUARD + 2 * (row - GUARD)
+                values = [0.25 * paired(sums[level - 1], comp, start) for comp in range(2)]
+                found = [lane_take(value, t) for value in values for t in takes]
+            for slot, value in enumerate(found):
+                put(sources[level], slot, row, value)
+
+    def kinds(level):
+        return 2 if level == 0 else 4
+
+    def first_sweep(level):
+        for row in tiles(level):
+            for comp in range(2):
                 for p in range(2):
-                    viscous[level][p, row : row + SUB, :] = here[p]
-                sums[level][2, row : row + SUB, :] = reaction[0] + reaction[1]
-                sums[level][3, row : row + SUB, :] = here[0] + here[1]
-            if 0 <= turn - 1 < TILES[level]:
-                row = GUARD + SUB * (turn - 1)
-                swept[turn - 1] = faces(level, row, loaded.pop(turn - 1))
-            if turn >= 2:
-                residual(level, GUARD + SUB * (turn - 2), swept.pop(turn - 2))
+                    put(
+                        iterates[level],
+                        2 * comp + p,
+                        row,
+                        tile_at(weights[level], p, row)
+                        * tile_at(sources[level], kinds(level) * comp + p, row),
+                    )
+
+    def residual(level):
+        state, iterate, weight, source = (
+            states[level],
+            iterates[level],
+            weights[level],
+            sources[level],
+        )
+        for row in tiles(level):
+            _, middle, north, south = faces(level, row)
+            if level == 0:
+                outer = [tile_at(outers, p, row) for p in range(2)]
+            else:
+                outer = outside(level, row, [tile_at(viscous[level], p, row) for p in range(2)])
+            scale = [tile_at(weight, p, row) for p in range(2)]
+            kept = level > 0 or TOP <= row < LOW
+            for comp in range(2):
+                here = [tile_at(iterate, 2 * comp + p, row) for p in range(2)]
+                if level == 0:
+                    beyond = [lane_roll(here[1], 1), lane_roll(here[0], -1)]
+                else:
+                    beyond = [
+                        tile_at(weight, 2 + p, row) * tile_at(source, 4 * comp + 2 + p, row)
+                        for p in range(2)
+                    ]
+                total = None
+                for p in range(2):
+                    slot = 2 * comp + p
+                    around = middle * here[1 - p] + outer[p] * beyond[p]
+                    around = around + (
+                        south[p] * tile_at(iterate, slot, row + 1)
+                        + north[p] * tile_at(iterate, slot, row - 1)
+                    )
+                    left = KEEP * tile_at(source, kinds(level) * comp + p, row) + around
+                    if kept:
+                        put(state, SWEPT + slot, row, here[p] + scale[p] * left)
+                    if level == LOCAL - 1:
+                        put(ring, slot, row, left)
+                        put(state, ITERATE + slot, row, here[p])
+                    total = left if total is None else total + left
+                put(sums[level], comp, row, total)
+            if kept:
+                for p in range(2):
+                    within = jnp.where(odd_row, north[p], south[p])
+                    across = jnp.where(odd_row, south[p], north[p])
+                    put(state, CENTRE + p, row, KEEP + scale[p] * (middle + within))
+                    put(state, SIDE + p, row, scale[p] * outer[p])
+                    put(state, ACROSS + p, row, scale[p] * across)
+                    if level == LOCAL - 1:
+                        put(state, WEIGHT + p, row, scale[p])
+
+    coefficients(0)
+    take_sources(0)
+    weigh(0)
+    coefficients(1)
+    first_sweep(0)
+    residual(0)
+    weigh(1)
+    coefficients(2)
+    take_sources(1)
+    weigh(2)
+    coefficients(3)
+    first_sweep(1)
+    residual(1)
+    take_sources(2)
+    weigh(3)
+    first_sweep(2)
+    residual(2)
+    take_sources(3)
+    first_sweep(3)
+    residual(3)
 
     start = GUARD + RIM[LOCAL - 1]
     column = lane & (SUB - 1)
@@ -722,10 +786,13 @@
         + tuple(buffers([STATE, STATE, STATE, STATE + 6])),
         in_specs=[VMEM_SPEC] * 3,
         out_specs=(VMEM_SPEC,) * (1 + LOCAL),
-        scratch_shapes=buffers([2] * 4)
+        scratch_shapes=buffers([2, 4, 4, 4])
+        + buffers([2] * 4)
+        + buffers([4, 8, 8, 8])
+        + buffers([2, 4, 4, 4])
         + buffers([4] * 4)
         + buffers([4] * 4)
-        + [pltpu.VMEM((4, HELD[3], LANES), F32)],
+        + [pltpu.VMEM((2, HELD[0], LANES), F32), pltpu.VMEM((4, HELD[3], LANES), F32)],
         compiler_params=params(),
         name="down",
     )(second, first, fields)

time: 29.9 us -> 28.7 us (0.960)
  Pallas kernels: 6.72 us -> 5.53 us
    pallas_call x1, Pallas kernels: 2.58 us -> 1.39 us  [per_device(): pl.pallas_call(functools.partial(down_kernel, size_y, devices), out_shape...]
where the time goes in v6:
time: 28.7 us; the launch traced here: 28.5 us
  blocking collectives  12.4 us (43%)
  starting transfers between devices  6.3 us (22%)
  Pallas kernels  5.53 us (19%)
  waiting for transfers between devices  3.63 us (13%)
  between operations  0.68 us (2%)
    all_to_all x1, blocking collectives, per_device(): gathered = lax.all_to_all(chunks, axes, 0, 0, tiled=True)  12.4 us
    ppermute x1, starting transfers between devices, per_device(): second = lax.ppermute(second, axes, routes[3])  3.21 us
    ppermute x1, starting transfers between devices, per_device(): first = lax.ppermute(first, axes, routes[0])  3.09 us
    pallas_call x1, Pallas kernels, per_device(): pl.pallas_call(functools.partial(up_kernel, size_x, size_y), out_shape=ja...  2.7 us
    ppermute x1, waiting for transfers between devices, per_device(): first = lax.ppermute(first, axes, routes[0])  1.89 us
    ppermute x1, waiting for transfers between devices, per_device(): second = lax.ppermute(second, axes, routes[3])  1.73 us
    pallas_call x1, Pallas kernels, per_device(): pl.pallas_call(functools.partial(down_kernel, size_y, devices), out_shape...  1.39 us
    pallas_call x1, Pallas kernels, per_device(): pl.pallas_call(bands_kernel, out_shape=(held_shape, band, band), in_specs...  0.97 us
  transfers between devices with their start and end apart: 4, of which 2 were waited for; matrix products, arithmetic and copies ran while one was open for 0% of the time, Pallas kernels for 1%

profile of v6, /device:TPU:0, one launch (start us, length us, event | category | flops | bytes accessed | tf_op | source)
XLA Modules:
  0.0 28.5 jit_solution(7235420575963429567)
XLA Ops:
  0.7 1.0 %bands.1 = (f32[4,184,128]{2,1,0:T(8,128)S(1)}, f32[64,128]{1,0:T(8,128)S(1)}, f32[64,128]{1,0:T(8,128)S(1)}) custom-call(s32[1,1]{1,0:T(1,128)S(6)} %copy.5.wet, f32[2,128,128]{2,1,0:T(8,128)} %right_side.1, f32[128,128]{1,0:T(8,128)} %shift_coef.1, f32[128,128]{1,0:T(8,128)} %viscosity.1), custom_call_target="tpu_custom_call" | custom-call | tf_op jit(solution)/shard_map/bands/pallas_call | solution.py:741
  1.6 3.1 %collective-permute-start = (f32[64,128]{1,0:T(8,128)S(1)}, f32[64,128]{1,0:T(8,128)S(1)}, u32[]{:S(2)}, u32[]{:S(2)}) collective-permute-start(f32[64,128]{1,0:T(8,128)S(1)} %get-tuple-element.16), channel_id=1, source_target_pairs={{0,8},{1,9},{2,10},{3,11},{4,12},{5,13},{6,14},{7,15},{8,0},{9,1},... | collective-permute-start | bytes 98312 | tf_op jit(solution)/shard_map/ppermute | solution.py:757
  4.7 0.0 collective-permute-start.1
  4.7 1.9 %collective-permute-done.got_first = f32[64,128]{1,0:T(8,128)S(1)} collective-permute-done((f32[64,128]{1,0:T(8,128)S(1)}, f32[64,128]{1,0:T(8,128)S(1)}, u32[]{:S(2)}, u32[]{:S(2)}) %collective-permute-start) | collective-permute-done | bytes 32800 | tf_op jit(solution)/shard_map/ppermute | solution.py:757
  6.6 0.0 collective-permute-done.1.got_second
  6.6 0.2 strips.1
  6.8 3.2 %collective-permute-start.2 = (f32[80,128]{1,0:T(8,128)S(1)}, f32[80,128]{1,0:T(8,128)S(1)}, u32[]{:S(2)}, u32[]{:S(2)}) collective-permute-start(f32[80,128]{1,0:T(8,128)S(1)} %get-tuple-element.18), channel_id=1, source_target_pairs={{0,8},{1,2},{2,1},{3,4},{4,3},{5,6},{6,5},{7,15},{8,0},{9,10},{10,... | collective-permute-start | bytes 122888 | tf_op jit(solution)/shard_map/ppermute | solution.py:777
  10.1 0.0 collective-permute-start.3
  10.1 0.2 halves.1.held
  10.3 1.7 %collective-permute-done.2.got_second = f32[80,128]{1,0:T(8,128)S(1)} collective-permute-done((f32[80,128]{1,0:T(8,128)S(1)}, f32[80,128]{1,0:T(8,128)S(1)}, u32[]{:S(2)}, u32[]{:S(2)}) %collective-permute-start.2) | collective-permute-done | bytes 40992 | tf_op jit(solution)/shard_map/ppermute | solution.py:777
  12.0 0.0 collective-permute-done.3.got_first
  12.0 1.4 %down.1 = (f32[128,128]{1,0:T(8,128)S(1)}, f32[10,184,128]{2,1,0:T(8,128)S(1)}, f32[10,104,128]{2,1,0:T(8,128)S(1)}, f32[10,64,128]{2,1,0:T(8,128)S(1)}, f32[16,48,128]{2,1,0:T(8,128)S(1)}) custom-call(f32[80,128]{1,0:T(8,128)S(1)} %collective-permute-done.2.got_second, f32[80,128]{1,0:T(8,128)S(1)} %collective-permute-done.3.got_first, ...), custom_call_target="tpu_custom_call" | custom-call | tf_op jit(solution)/shard_map/down/pallas_call | solution.py:783
  13.4 12.4 %all_to_all.11 = f32[32,4,128]{2,1,0:T(4,128)S(1)} all-to-all(f32[32,4,128]{2,1,0:T(4,128)S(1)} %bitcast.3), channel_id=1, replica_groups=mesh['gx'=4,'gy'=8] {'gx','gy'}, dimensions={0} | all-to-all | bytes 131072 | tf_op jit(solution)/shard_map/all_to_all | solution.py:799
  25.8 2.7 %up.1 = f32[2,128,128]{2,1,0:T(8,128)} custom-call(f32[128,128]{1,0:T(8,128)S(1)} %bitcast.2, f32[10,184,128]{2,1,0:T(8,128)S(1)} %get-tuple-element.21.state0, f32[10,104,128]{2,1,0:T(8,128)S(1)} %get-tuple-element.22.state1, f32[10,64,128]{2,1,0:T(8,128)S(1)} %get-tuple-element.23.state2, f32[16,48,128]{2,1,0:T(8,128)S(1)} %get-tuple-element.24.state3), custom_call_target="tpu_custom_call" | custom-call | tf_op jit(solution)/shard_map/up/pallas_call | solution.py:802
Async XLA Ops:
  1.6 5.0 %collective-permute-start = (f32[64,128]{1,0:T(8,128)S(1)}, f32[64,128]{1,0:T(8,128)S(1)}, u32[]{:S(2)}, u32[]{:S(2)}) collective-permute-start(f32[64,128]{1,0:T(8,128)S(1)} %get-tuple-element.16), channel_id=1, source_target_pairs={{0,8},{1,9},{2,10},{3,11},{4,12},{5,13},{6,14},{7,15},{8,0},{9,1},... | collective-permute-start | bytes 98312 | tf_op jit(solution)/shard_map/ppermute | solution.py:757
  4.7 1.9 %collective-permute-start.1 = (f32[64,128]{1,0:T(8,128)S(1)}, f32[64,128]{1,0:T(8,128)S(1)}, u32[]{:S(2)}, u32[]{:S(2)}) collective-permute-start(f32[64,128]{1,0:T(8,128)S(1)} %get-tuple-element.17), channel_id=1, source_target_pairs={{0,1},{1,0},{2,3},{3,2},{4,5},{5,4},{6,7},{7,6},{8,16},{9,17},{10,... | collective-permute-start | bytes 98312 | tf_op jit(solution)/shard_map/ppermute | solution.py:756
  6.8 5.2 %collective-permute-start.2 = (f32[80,128]{1,0:T(8,128)S(1)}, f32[80,128]{1,0:T(8,128)S(1)}, u32[]{:S(2)}, u32[]{:S(2)}) collective-permute-start(f32[80,128]{1,0:T(8,128)S(1)} %get-tuple-element.18), channel_id=1, source_target_pairs={{0,8},{1,2},{2,1},{3,4},{4,3},{5,6},{6,5},{7,15},{8,0},{9,10},{10,... | collective-permute-start | bytes 122888 | tf_op jit(solution)/shard_map/ppermute | solution.py:777
  10.1 2.0 %collective-permute-start.3 = (f32[80,128]{1,0:T(8,128)S(1)}, f32[80,128]{1,0:T(8,128)S(1)}, u32[]{:S(2)}, u32[]{:S(2)}) collective-permute-start(f32[80,128]{1,0:T(8,128)S(1)} %get-tuple-element.19), channel_id=1, source_target_pairs={{0,1},{1,0},{2,3},{3,2},{4,5},{5,4},{6,7},{7,6},{8,9},{9,8},{10,11... | collective-permute-start | bytes 122888 | tf_op jit(solution)/shard_map/ppermute | solution.py:778

commit v7 on v6

--- a/solution.py
+++ b/solution.py
@@ -347,15 +347,17 @@
         lane_take(scale * paired(sums[LOCAL - 1], slot, start), column)
         for slot, scale in enumerate((0.25, 0.25, 0.25, 0.0625))
     ]
-    chosen = ((lane >> 3) & (SUB - 1)) == sub
+    turned = ((lane >> 3) - index_y) & 15
+    chosen = (turned & (SUB - 1)) == sub
+
+    def packed(value):
+        return jnp.sum(value, axis=0, keepdims=True)
+
+    def joined(a, b):
+        return packed(jnp.where(chosen, jnp.where(turned < SUB, a, b), 0.0))
+
     edge = (lane >> 4) & 3
     place = lane & 15
-
-    def packed(value):
-        return jnp.sum(value, axis=0, keepdims=True)
-
-    def joined(a, b):
-        return packed(jnp.where(chosen, jnp.where(inner, a, b), 0.0))
 
     rims = jnp.zeros((SUB, LANES), F32)
     for p in range(2):
@@ -371,203 +373,308 @@
             )
             rims = jnp.where(along | up, value, rims)
     kind = sub % CHUNK
+    parts = [joined(own[0], own[1]), joined(own[2], own[2]), packed(rims), joined(own[3], own[3])]
     tile = jnp.where(
-        kind == 0,
-        joined(own[0], own[1]),
-        jnp.where(kind == 1, joined(own[2], own[3]), jnp.where(kind == 2, packed(rims), 0.0)),
+        kind < 2,
+        jnp.where(kind == 0, parts[0], parts[1]),
+        jnp.where(kind == 2, parts[2], parts[3]),
     )
     for block in range(CHUNK * devices // SUB):
         chunks[SUB * block : SUB * block + SUB, :] = tile
 
 
-def coarse_solve(fields, rows_total, cols_total):
-    shape = fields[0].shape
-    width = shape[1]
-    row, lane = iota(0, shape), iota(1, shape)
-
-    def along(value, amount):
-        return pltpu.roll(value, amount % width, 1)
-
-    def down(value, amount):
-        return pltpu.roll(value, amount % shape[0], 0)
-
-    sources = fields[:2]
-    reaction = jnp.where(lane < cols_total, fields[2], 1.0)
-    viscous = fields[3]
-    stored = []
-    for level in range(COARSE):
-        step = 1 << level
-        odd_lane, odd_row = (lane & step) != 0, (row & step) != 0
-
-        def paired(value):
-            return (
-                jnp.where(odd_lane, along(value, step), value),
-                jnp.where(odd_lane, value, along(value, -step)),
+def write(buffer, slot, rows, value):
+    for column in range(buffer.shape[1]):
+        buffer[slot, column, rows, :] = value[:, LANES * column : LANES * column + LANES]
+
+
+def read(buffer, slot, rows):
+    parts = [buffer[slot, column, rows, :] for column in range(buffer.shape[1])]
+    return parts[0] if len(parts) == 1 else jnp.concatenate(parts, 1)
+
+
+class Coarse:
+    def __init__(self, step, row_step, rows, cols_total, width):
+        self.step, self.row_step = step, row_step
+        self.shape = (rows, width)
+        lane, row = iota(1, self.shape), iota(0, self.shape)
+        column = lane & (cols_total - 1)
+        self.odd_lane, self.odd_row = (lane & step) != 0, (row & row_step) != 0
+        self.leftmost = column < 2 * step
+        self.rightmost = column >= cols_total - 2 * step
+        self.top, self.bottom = row < row_step, row >= rows - row_step
+
+    def along(self, value, amount):
+        return pltpu.roll(value, amount % self.shape[1], 1)
+
+    def down(self, value, amount):
+        return pltpu.roll(value, amount % self.shape[0], 0)
+
+    def paired(self, value):
+        return (
+            jnp.where(self.odd_lane, self.along(value, self.step), value),
+            jnp.where(self.odd_lane, value, self.along(value, -self.step)),
+        )
+
+    def outside(self, value):
+        return (
+            jnp.where(
+                self.odd_lane, self.along(value, 2 * self.step), self.along(value, self.step)
+            ),
+            jnp.where(
+                self.odd_lane, self.along(value, -self.step), self.along(value, -2 * self.step)
+            ),
+        )
+
+    def coefficients(self, viscous, reaction):
+        here, reactions, beyond = self.paired(viscous), self.paired(reaction), self.outside(viscous)
+        self.middle = jnp.minimum(here[0], here[1])
+        self.outer = [
+            jnp.minimum(here[0], jnp.where(self.leftmost, 0.0, beyond[0])),
+            jnp.minimum(here[1], jnp.where(self.rightmost, 0.0, beyond[1])),
+        ]
+        self.north, self.south, self.weights = [], [], []
+        for p in range(2):
+            above = jnp.where(self.top, 0.0, self.down(here[p], self.row_step))
+            below = jnp.where(self.bottom, 0.0, self.down(here[p], -self.row_step))
+            self.north.append(jnp.minimum(here[p], above))
+            self.south.append(jnp.minimum(here[p], below))
+            diagonal = reactions[p] + (
+                (self.middle + self.outer[p]) + (self.north[p] + self.south[p])
             )
-
-        def outside(value):
-            return (
-                jnp.where(odd_lane, along(value, 2 * step), along(value, step)),
-                jnp.where(odd_lane, along(value, -step), along(value, -2 * step)),
+            self.weights.append(OMEGA / diagonal)
+        return here[0] + here[1], reactions[0] + reactions[1]
+
+    def weigh(self):
+        self.weights_beyond = (
+            self.along(self.weights[1], 2 * self.step),
+            self.along(self.weights[0], -2 * self.step),
+        )
+
+    def take(self, source):
+        self.values, self.values_beyond = self.paired(source), self.outside(source)
+
+    def residual(self):
+        x = [w * s for w, s in zip(self.weights, self.values)]
+        x_beyond = [w * s for w, s in zip(self.weights_beyond, self.values_beyond)]
+        total, self.swept = None, []
+        for p in range(2):
+            around = self.middle * x[1 - p] + self.outer[p] * x_beyond[p]
+            around = around + (
+                self.south[p] * self.down(x[p], -self.row_step)
+                + self.north[p] * self.down(x[p], self.row_step)
             )
-
-        here, reactions = paired(viscous), paired(reaction)
-        beyond = outside(viscous)
-        beyond = (
-            jnp.where(lane < 2 * step, 0.0, beyond[0]),
-            jnp.where(lane < cols_total - 2 * step, beyond[1], 0.0),
-        )
-        middle = jnp.minimum(here[0], here[1])
-        outer = [jnp.minimum(a, b) for a, b in zip(here, beyond)]
-        north, south, weights = [], [], []
+            left = KEEP * self.values[p] + around
+            self.swept.append(x[p] + self.weights[p] * left)
+            total = left if total is None else total + left
+        return total
+
+    def corrected(self, here, beyond, across):
+        parts = []
         for p in range(2):
-            above = jnp.where(row < step, 0.0, down(here[p], step))
-            below = jnp.where(row < rows_total - step, down(here[p], -step), 0.0)
-            north.append(jnp.minimum(here[p], above))
-            south.append(jnp.minimum(here[p], below))
-            diagonal = reactions[p] + ((middle + outer[p]) + (north[p] + south[p]))
-            weights.append(OMEGA / diagonal)
-        weights_beyond = (along(weights[1], 2 * step), along(weights[0], -2 * step))
-        swept, remaining = [], []
-        for source in sources:
-            values, values_beyond = paired(source), outside(source)
-            x = [w * s for w, s in zip(weights, values)]
-            x_beyond = [w * s for w, s in zip(weights_beyond, values_beyond)]
-            total = None
-            for p in range(2):
-                around = middle * x[1 - p] + outer[p] * x_beyond[p]
-                around = around + (south[p] * down(x[p], -step) + north[p] * down(x[p], step))
-                left = KEEP * values[p] + around
-                swept.append(x[p] + weights[p] * left)
-                total = left if total is None else total + left
-            remaining.append(total)
-        centre, side, across = [], [], []
-        for p in range(2):
-            within = jnp.where(odd_row, north[p], south[p])
-            out = jnp.where(odd_row, south[p], north[p])
-            centre.append(KEEP + weights[p] * (middle + within))
-            side.append(weights[p] * outer[p])
-            across.append(weights[p] * out)
-        stored.append((step, odd_lane, odd_row, swept, centre, side, across))
-
-        def folded(value, scale):
-            return scale * (value + jnp.where(odd_row, down(value, step), down(value, -step)))
-
-        sources = [folded(total, 0.25) for total in remaining]
-        reaction = folded(reactions[0] + reactions[1], 0.25)
-        viscous = folded(here[0] + here[1], 0.0625)
-
+            within = jnp.where(self.odd_row, self.north[p], self.south[p])
+            out = jnp.where(self.odd_row, self.south[p], self.north[p])
+            weight = self.weights[p]
+            centre = KEEP + weight * (self.middle + within)
+            parts.append(
+                (self.swept[p] + centre * here)
+                + ((weight * self.outer[p]) * beyond[p] + (weight * out) * across)
+            )
+        return jnp.where(self.odd_lane, parts[1], parts[0])
+
+
+def coarse_solve(grid, buffer, rows_total, cols_total, width, meanwhile):
+    columns = width // LANES
+
+    def whole(slot):
+        return jnp.concatenate([grid[slot, c] for c in range(columns)], 1) if columns > 1 else grid[slot, 0]
+
+    levels, rows, row_step = [], rows_total, 1
+    for index in range(COARSE + 1):
+        levels.append(Coarse(1 << index, row_step, rows, cols_total, width))
+        if rows > SUB:
+            rows //= 2
+        else:
+            row_step *= 2
+
+    def folded(index, value, slot, scale):
+        level = levels[index]
+        rows = level.shape[0]
+        if levels[index + 1].shape[0] == rows:
+            other = jnp.where(
+                level.odd_row, level.down(value, level.row_step), level.down(value, -level.row_step)
+            )
+            return scale * (value + other)
+        write(buffer, slot, slice(0, rows), value)
+        first, second = [pl.ds(begin, rows // 2, stride=2) for begin in range(2)]
+        return scale * (read(buffer, slot, first) + read(buffer, slot, second))
+
+    def opened(index, value):
+        level = levels[index]
+        rows = level.shape[0]
+        if value.shape[0] == rows:
+            return value, jnp.where(
+                level.odd_row, level.down(value, -level.row_step), level.down(value, level.row_step)
+            )
+        half = rows // 2
+        blank = jnp.zeros((SUB, width), F32)
+        for begin in range(2):
+            write(buffer, 0, pl.ds(begin, half, stride=2), value)
+        write(buffer, 1, slice(SUB, 2 * SUB), blank)
+        write(buffer, 1, slice(rows, rows + SUB), blank)
+        for begin in (SUB + 2, SUB - 1):
+            write(buffer, 1, pl.ds(begin, half, stride=2), value)
+        return read(buffer, 0, slice(0, rows)), read(buffer, 1, slice(SUB, SUB + rows))
+
+    viscous, reaction, source = [None] * 5, [None] * 5, [None] * 5
+    viscous[0], reaction[0], source[0] = whole(2), whole(1), whole(0)
+
+    def coefficients(index):
+        pair, reactions = levels[index].coefficients(viscous[index], reaction[index])
+        viscous[index + 1] = folded(index, pair, 0, 0.0625)
+        reaction[index + 1] = folded(index, reactions, 1, 0.25)
+
+    def residual(index):
+        source[index + 1] = folded(index, levels[index].residual(), 2, 0.25)
+
+    last = levels[COARSE]
     block = 1 << COARSE
-    rows_left, cols_left = rows_total // block, cols_total // block
-    cells = [(i, j) for i in range(rows_left) for j in range(cols_left)]
-
-    def spread_cells(value):
-        found = {}
-        for i, j in cells:
-            column, place = divmod(block * j, LANES)
-            tile = value[block * i : block * i + SUB, LANES * column : LANES * column + LANES]
-            found[i, j] = lane_take(tile, jnp.full((SUB, LANES), place, jnp.int32))
+    cols_left = cols_total // block
+    rows_left = last.shape[0]
+    lane = iota(1, (rows_left, LANES))
+    groups = 1 if cols_total < LANES else 2
+    per_group = columns // groups
+
+    def spread(value):
+        found = []
+        for group in range(groups):
+            for j in range(cols_left):
+                column, place = divmod(block * j, LANES)
+                column += group * per_group
+                if groups == 1:
+                    place = place + (lane & (LANES - cols_total))
+                else:
+                    place = jnp.full((rows_left, LANES), place, jnp.int32)
+                found.append(lane_take(value[:, LANES * column : LANES * column + LANES], place))
         return found
 
-    source_cells = [spread_cells(s) for s in sources]
-    reaction_cells, viscous_cells = spread_cells(reaction), spread_cells(viscous)
-    pulls, weight_cells = {}, {}
-    for i, j in cells:
-        near = [c for c in ((i - 1, j), (i + 1, j), (i, j - 1), (i, j + 1)) if c in viscous_cells]
-        links = [(c, jnp.minimum(viscous_cells[i, j], viscous_cells[c])) for c in near]
-        diagonal = reaction_cells[i, j] + sum(c for _, c in links)
-        weight_cells[i, j] = OMEGA / diagonal
-        pulls[i, j] = [(c, weight_cells[i, j] * link) for c, link in links]
-    solved = []
-    for comp in range(2):
-        pushed = {c: weight_cells[c] * source_cells[comp][c] for c in cells}
-        values = pushed
-        for _ in range(COARSE_SWEEPS - 1):
-            values = {
-                c: (KEEP * values[c] + pushed[c])
-                + sum(pull * values[other] for other, pull in pulls[c])
-                for c in cells
-            }
-        solved.append(values)
-
-    def laid(values, di, dj):
-        tiles = []
-        nothing = jnp.zeros((SUB, LANES), F32)
-        for tile in range(shape[0] // SUB):
-            i = SUB * tile // block
-            if di:
-                i += 1 if (SUB * tile // (block // 2)) % 2 else -1
-            columns = []
-            for column in range(width // LANES):
-                place = iota(1) // block + column * (LANES // block)
-                value = nothing
-                for j in range(cols_left):
-                    if (i, j) in values and column * LANES <= (j - dj) * block < (column + 1) * LANES:
-                        value = jnp.where(place == j - dj, values[i, j], value)
-                columns.append(value)
-            tiles.append(columns[0] if len(columns) == 1 else jnp.concatenate(columns, 1))
-        return jnp.concatenate(tiles, 0)
-
-    corrections = None
-    for step, odd_lane, odd_row, swept, centre, side, across in reversed(stored):
+    def flat(values, group, j):
+        return values[group * cols_left + j]
+
+    levels[0].take(source[0])
+    coefficients(0)
+    coefficients(1)
+    levels[0].weigh()
+    coefficients(2)
+    levels[1].weigh()
+    residual(0)
+    levels[1].take(source[1])
+    coefficients(3)
+    levels[2].weigh()
+    residual(1)
+    levels[2].take(source[2])
+    meanwhile()
+    levels[3].weigh()
+    viscous_columns, reaction_columns = spread(viscous[4]), spread(reaction[4])
+    residual(2)
+    levels[3].take(source[3])
+
+    top, bottom = last.top[:, :LANES], last.bottom[:, :LANES]
+    pulls, weights = [], []
+    for group in range(groups):
+        for j in range(cols_left):
+            here = flat(viscous_columns, group, j)
+            above = jnp.where(top, 0.0, last.down(here, last.row_step))
+            below = jnp.where(bottom, 0.0, last.down(here, -last.row_step))
+            links = [jnp.minimum(here, above), jnp.minimum(here, below)]
+            links += [
+                jnp.minimum(here, flat(viscous_columns, group, other))
+                for other in (j - 1, j + 1)
+                if 0 <= other < cols_left
+            ]
+            weight = OMEGA / (flat(reaction_columns, group, j) + sum(links))
+            weights.append(weight)
+            pulls.append([weight * link for link in links])
+    residual(3)
+    pushed = [w * s for w, s in zip(weights, spread(source[4]))]
+    values = pushed
+    for _ in range(COARSE_SWEEPS - 1):
+        following = []
+        for group in range(groups):
+            for j in range(cols_left):
+                at = group * cols_left + j
+                here, pull = values[at], pulls[at]
+                total = (KEEP * here + pushed[at]) + (
+                    pull[0] * last.down(here, last.row_step)
+                    + pull[1] * last.down(here, -last.row_step)
+                )
+                sides = [other for other in (j - 1, j + 1) if 0 <= other < cols_left]
+                for link, other in zip(pull[2:], sides):
+                    total = total + link * flat(values, group, other)
+                following.append(total)
+        values = following
+
+    def laid(shift):
         found = []
-        for comp in range(2):
-            if corrections is None:
-                here = laid(solved[comp], 0, 0)
-                beyond = [laid(solved[comp], 0, -1), laid(solved[comp], 0, 1)]
-                out = laid(solved[comp], 1, 0)
-            else:
-                here = corrections[comp]
-                beyond = [along(here, 2 * step), along(here, -2 * step)]
-                out = jnp.where(odd_row, down(here, -step), down(here, step))
-            parts = [
-                (swept[2 * comp + p] + centre[p] * here) + (side[p] * beyond[p] + across[p] * out)
-                for p in range(2)
-            ]
-            found.append(jnp.where(odd_lane, parts[1], parts[0]))
-        corrections = found
-    return corrections
+        for column in range(columns):
+            group = column // per_group
+            place = ((lane & (cols_total - 1)) if groups == 1 else lane) // block
+            place = place + (column % per_group) * (LANES // block)
+            value = jnp.zeros((rows_left, LANES), F32)
+            for j in range(cols_left):
+                value = jnp.where(place == j + shift, flat(values, group, j), value)
+            found.append(value)
+        return found[0] if columns == 1 else jnp.concatenate(found, 1)
+
+    index = COARSE - 1
+    here, across = opened(index, laid(0))
+    beyond = [opened(index, laid(shift))[0] for shift in (1, -1)]
+    correction = levels[index].corrected(here, beyond, across)
+    for index in range(COARSE - 2, -1, -1):
+        level, next_level = levels[index], levels[index + 1]
+        sides = [next_level.along(correction, 2 * level.step), next_level.along(correction, -2 * level.step)]
+        here, across = opened(index, correction)
+        beyond = [opened_sides(level, buffer, side) for side in sides]
+        correction = level.corrected(here, beyond, across)
+    return correction
+
+
+def opened_sides(level, buffer, value):
+    rows = level.shape[0]
+    if value.shape[0] == rows:
+        return value
+    for begin in range(2):
+        write(buffer, 2, pl.ds(begin, rows // 2, stride=2), value)
+    return read(buffer, 2, slice(0, rows))
 
 
 def up_kernel(size_x, size_y, gathered, state0, state1, state2, state3, out, *refs):
-    grid, whole, swept3, corr1, corr2, corr3, merged0, merged1, merged2 = refs
+    grid, buffer, whole, window, swept3, corr1, corr2, corr3, merged0, merged1, merged2 = refs
     index_x, index_y = lax.axis_index("gx"), lax.axis_index("gy")
     rows_total, cols_total = CELLS * size_x, CELLS * size_y
-    width = max(LANES, cols_total)
+    width = 2 * cols_total
     columns = width // LANES
     per_column = LANES // CELLS
     lane, sub = iota(1), iota(0)
 
-    tall = iota(1, (2 * size_x, LANES))
+    tall = iota(1, (size_x, LANES)) // CELLS
+    modulus = min(size_y, per_column)
     for column in range(columns):
-        targets = [[jnp.zeros((2 * size_x, LANES), F32)] * CELLS for _ in range(2)]
-        for place in range(min(per_column, size_y - column * per_column)):
-            j = column * per_column + place
-            chunk = jnp.concatenate(
-                [
-                    gathered[pl.ds(CHUNK * j + h, size_x, stride=CHUNK * size_y), :]
-                    for h in range(2)
-                ],
-                0,
-            )
-            mine = (tall // CELLS) == place
-            turns = {}
-            for half in range(2):
-                for r in range(CELLS):
-                    shift = (CELLS * (place - r) - half * HALF) % LANES
-                    if shift not in turns:
-                        turns[shift] = lane_roll(chunk, shift)
-                    targets[half][r] = jnp.where(mine, turns[shift], targets[half][r])
-        for half in range(2):
+        comp = column // (columns // 2) if columns > 1 else 0
+        first = (column % (columns // 2)) * per_column if columns > 1 else 0
+        for slot, kind in ((2, 3), (1, 1), (0, 0)):
+            chunks = [
+                gathered[pl.ds(CHUNK * (first + j) + kind, size_x, stride=CHUNK * size_y), :]
+                for j in range(modulus)
+            ]
             for r in range(CELLS):
-                for h in range(2):
-                    grid[2 * h + half, column, pl.ds(r, size_x, stride=CELLS), :] = targets[half][r][
-                        h * size_x : (h + 1) * size_x
-                    ]
-    fields = [
-        jnp.concatenate([grid[f, c] for c in range(columns)], 1) if columns > 1 else grid[f, 0]
-        for f in range(4)
-    ]
+                turn = r + CELLS * comp
+                value = chunks[0]
+                for j in range(1, modulus):
+                    value = jnp.where(((tall - turn) & (modulus - 1)) == j, chunks[j], value)
+                grid[slot, column, pl.ds(r, size_x, stride=CELLS), :] = lane_roll(
+                    value, -CELLS * turn
+                )
 
     def ring_row(dx, dy):
         i = jnp.clip(index_x + dx, 0, size_x - 1)
@@ -576,54 +683,58 @@
             gathered[pl.ds(CHUNK * (i * size_y + j) + 2, 1), :], (SUB, LANES)
         )
 
-    beside = {
-        (dx, dy): ring_row(dx, dy) for dx in (-1, 0, 1) for dy in (-1, 0, 1) if dx or dy
-    }
     start = GUARD + RIM[3]
-    for comp in range(2):
-        base = comp * HALF
-        for p in range(2):
-            slot = 2 * comp + p
-            end = 7 if p else 0
-            corner_lane = LANES - 1 if p else SUB
-            dy = -1 if p else 1
-            for tile in range(2):
-                at = start + SUB * tile
-                index = base + (48 if p else 32) + SUB * tile + sub
-                ringed = lane_take(beside[0, dy], index)
-                swept = jnp.where(
-                    lane == corner_lane,
-                    tile_at(state3, ITERATE + slot, at) + tile_at(state3, WEIGHT + p, at) * ringed,
-                    tile_at(state3, SWEPT + slot, at),
-                )
-                swept3[slot, at : at + SUB, :] = swept
-            for dx, at, edge in ((-1, start - 1, 16), (1, start + 2 * SUB, 0)):
-                index = base + edge + 8 * p
-                ringed = jnp.where(
-                    lane == corner_lane,
-                    lane_take(beside[dx, dy], jnp.full((SUB, LANES), index + end, jnp.int32)),
-                    lane_take(beside[dx, 0], index + (lane & 7)),
-                )
-                rows = slice(at, at + 1)
-                swept3[slot, rows, :] = (
-                    state3[ITERATE + slot, rows, :] + state3[WEIGHT + p, rows, :] * ringed[0:1]
-                )
-
-    corrections = coarse_solve(fields, rows_total, cols_total)
-
+
+    def complete_ring():
+        beside = {
+            (dx, dy): ring_row(dx, dy) for dx in (-1, 0, 1) for dy in (-1, 0, 1) if dx or dy
+        }
+        for comp in range(2):
+            base = comp * HALF
+            for p in range(2):
+                slot = 2 * comp + p
+                end = 7 if p else 0
+                corner_lane = LANES - 1 if p else SUB
+                dy = -1 if p else 1
+                for tile in range(2):
+                    at = start + SUB * tile
+                    index = base + (48 if p else 32) + SUB * tile + sub
+                    ringed = lane_take(beside[0, dy], index)
+                    swept = jnp.where(
+                        lane == corner_lane,
+                        tile_at(state3, ITERATE + slot, at)
+                        + tile_at(state3, WEIGHT + p, at) * ringed,
+                        tile_at(state3, SWEPT + slot, at),
+                    )
+                    swept3[slot, at : at + SUB, :] = swept
+                for dx, at, edge in ((-1, start - 1, 16), (1, start + 2 * SUB, 0)):
+                    index = base + edge + 8 * p
+                    ringed = jnp.where(
+                        lane == corner_lane,
+                        lane_take(beside[dx, dy], jnp.full((SUB, LANES), index + end, jnp.int32)),
+                        lane_take(beside[dx, 0], index + (lane & 7)),
+                    )
+                    rows = slice(at, at + 1)
+                    swept3[slot, rows, :] = (
+                        state3[ITERATE + slot, rows, :] + state3[WEIGHT + p, rows, :] * ringed[0:1]
+                    )
+
+    correction = coarse_solve(grid, buffer, rows_total, cols_total, width, complete_ring)
+
+    whole[GUARD : GUARD + rows_total, :] = correction
+    whole[0:GUARD, :] = jnp.zeros((GUARD, width), F32)
+    whole[GUARD + rows_total :, :] = jnp.zeros((2 * SUB, width), F32)
+    near_rows = whole[pl.ds(pl.multiple_of(CELLS * index_x, SUB), 3 * SUB), :]
     for comp in range(2):
         for kind in range(3):
-            shift = (width - CELLS * index_y + (0, -1, 1)[kind] + width) % width
-            turned = pltpu.roll(corrections[comp], shift, 1)
+            shift = (2 * width - cols_total * comp - CELLS * index_y + (0, -1, 1)[kind]) % width
+            turned = pltpu.roll(near_rows, shift, 1)
             if columns > 1:
-                tall_lane = iota(1, (rows_total, LANES))
+                tall_lane = iota(1, (3 * SUB, LANES))
                 turned = jnp.where(
                     tall_lane < HALF, turned[:, :LANES], turned[:, width - LANES :]
                 )
-            slot = 3 * comp + kind
-            whole[slot, 2 * GUARD : 2 * GUARD + rows_total, :] = turned
-            whole[slot, 0 : 2 * GUARD, :] = jnp.zeros((2 * GUARD, LANES), F32)
-            whole[slot, 2 * GUARD + rows_total :, :] = jnp.zeros((3 * SUB, LANES), F32)
+            window[3 * comp + kind, 0 : 3 * SUB, :] = turned
 
     def swept_rows(ref, level, coarse_row, parity, here, beyond, across, comp):
         at = pl.ds(GUARD + RIM[level] + 2 * coarse_row + parity, SUB, stride=2)
@@ -634,16 +745,13 @@
             for p in range(2)
         ]
 
-    base = pl.multiple_of(CELLS * index_x, SUB)
     for comp in range(2):
-        window = [whole[3 * comp + kind, pl.ds(base, 6 * SUB), :] for kind in range(3)]
         for tile in range(2):
             first = SUB * tile - 1
-            at = 2 * GUARD + first
-            here, right, left = [w[at : at + SUB] for w in window]
+            at = GUARD + first
+            here, right, left = [tile_at(window, 3 * comp + kind, at) for kind in range(3)]
             for parity in range(2):
-                shifted = at + (1 if parity else -1)
-                across = window[0][shifted : shifted + SUB]
+                across = tile_at(window, 3 * comp, at + (1 if parity else -1))
                 found = swept_rows(swept3, 3, first, parity, here, (left, right), across, comp)
                 rows = pl.ds(GUARD + RIM[3] + 2 * first + parity, SUB, stride=2)
                 for p in range(2):
@@ -798,15 +906,17 @@
     )(second, first, fields)
     gathered = lax.all_to_all(chunks, axes, 0, 0, tiled=True)
     rows_total = CELLS * size_x
-    columns = max(LANES, CELLS * size_y) // LANES
+    width = 2 * CELLS * size_y
     return pl.pallas_call(
         functools.partial(up_kernel, size_x, size_y),
         out_shape=jax.ShapeDtypeStruct((2, LANES, LANES), F32),
         in_specs=[VMEM_SPEC] * (1 + LOCAL),
         out_specs=VMEM_SPEC,
         scratch_shapes=[
-            pltpu.VMEM((4, columns, rows_total, LANES), F32),
-            pltpu.VMEM((6, rows_total + 5 * SUB, LANES), F32),
+            pltpu.VMEM((3, width // LANES, rows_total, LANES), F32),
+            pltpu.VMEM((3, width // LANES, rows_total + 3 * SUB, LANES), F32),
+            pltpu.VMEM((rows_total + 3 * SUB, width), F32),
+            pltpu.VMEM((6, 5 * SUB, LANES), F32),
             pltpu.VMEM((4, HELD[3], LANES), F32),
         ]
         + [pltpu.VMEM((4, HELD[level], LANES), F32) for level in (1, 2, 3)]

time: 28.7 us -> 28.3 us (0.986)
  Pallas kernels: 5.53 us -> 5.18 us
    pallas_call x1, Pallas kernels: 2.7 us -> 2.34 us  [per_device(): pl.pallas_call(functools.partial(up_kernel, size_x, size_y), out_shape=ja...]
where the time goes in v7:
time: 28.3 us; the launch traced here: 28.2 us
  blocking collectives  12.4 us (44%)
  starting transfers between devices  6.3 us (22%)
  Pallas kernels  5.18 us (18%)
  waiting for transfers between devices  3.63 us (13%)
  between operations  0.68 us (2%)
    all_to_all x1, blocking collectives, per_device(): gathered = lax.all_to_all(chunks, axes, 0, 0, tiled=True)  12.4 us
    ppermute x1, starting transfers between devices, per_device(): second = lax.ppermute(second, axes, routes[3])  3.21 us
    ppermute x1, starting transfers between devices, per_device(): first = lax.ppermute(first, axes, routes[0])  3.09 us
    pallas_call x1, Pallas kernels, per_device(): pl.pallas_call(functools.partial(up_kernel, size_x, size_y), out_shape=ja...  2.34 us
    ppermute x1, waiting for transfers between devices, per_device(): first = lax.ppermute(first, axes, routes[0])  1.89 us
    ppermute x1, waiting for transfers between devices, per_device(): second = lax.ppermute(second, axes, routes[3])  1.73 us
    pallas_call x1, Pallas kernels, per_device(): pl.pallas_call(functools.partial(down_kernel, size_y, devices), out_shape...  1.4 us
    pallas_call x1, Pallas kernels, per_device(): pl.pallas_call(bands_kernel, out_shape=(held_shape, band, band), in_specs...  0.97 us
  transfers between devices with their start and end apart: 4, of which 2 were waited for; matrix products, arithmetic and copies ran while one was open for 0% of the time, Pallas kernels for 1%

profile of v7, /device:TPU:0, one launch (start us, length us, event | category | flops | bytes accessed | tf_op | source)
XLA Modules:
  0.0 28.2 jit_solution(2444171536987736233)
XLA Ops:
  0.7 1.0 %bands.1 = (f32[4,184,128]{2,1,0:T(8,128)S(1)}, f32[64,128]{1,0:T(8,128)S(1)}, f32[64,128]{1,0:T(8,128)S(1)}) custom-call(s32[1,1]{1,0:T(1,128)S(6)} %copy.5.wet, f32[2,128,128]{2,1,0:T(8,128)} %right_side.1, f32[128,128]{1,0:T(8,128)} %shift_coef.1, f32[128,128]{1,0:T(8,128)} %viscosity.1), custom_call_target="tpu_custom_call" | custom-call | tf_op jit(solution)/shard_map/bands/pallas_call | solution.py:849
  1.6 3.1 %collective-permute-start = (f32[64,128]{1,0:T(8,128)S(1)}, f32[64,128]{1,0:T(8,128)S(1)}, u32[]{:S(2)}, u32[]{:S(2)}) collective-permute-start(f32[64,128]{1,0:T(8,128)S(1)} %get-tuple-element.16), channel_id=1, source_target_pairs={{0,8},{1,9},{2,10},{3,11},{4,12},{5,13},{6,14},{7,15},{8,0},{9,1},... | collective-permute-start | bytes 98312 | tf_op jit(solution)/shard_map/ppermute | solution.py:865
  4.7 0.0 collective-permute-start.1
  4.7 1.9 %collective-permute-done.got_first = f32[64,128]{1,0:T(8,128)S(1)} collective-permute-done((f32[64,128]{1,0:T(8,128)S(1)}, f32[64,128]{1,0:T(8,128)S(1)}, u32[]{:S(2)}, u32[]{:S(2)}) %collective-permute-start) | collective-permute-done | bytes 32800 | tf_op jit(solution)/shard_map/ppermute | solution.py:865
  6.6 0.0 collective-permute-done.1.got_second
  6.6 0.2 strips.1
  6.8 3.2 %collective-permute-start.2 = (f32[80,128]{1,0:T(8,128)S(1)}, f32[80,128]{1,0:T(8,128)S(1)}, u32[]{:S(2)}, u32[]{:S(2)}) collective-permute-start(f32[80,128]{1,0:T(8,128)S(1)} %get-tuple-element.18), channel_id=1, source_target_pairs={{0,8},{1,2},{2,1},{3,4},{4,3},{5,6},{6,5},{7,15},{8,0},{9,10},{10,... | collective-permute-start | bytes 122888 | tf_op jit(solution)/shard_map/ppermute | solution.py:885
  10.1 0.0 collective-permute-start.3
  10.1 0.2 halves.1.held
  10.3 1.7 %collective-permute-done.2.got_second = f32[80,128]{1,0:T(8,128)S(1)} collective-permute-done((f32[80,128]{1,0:T(8,128)S(1)}, f32[80,128]{1,0:T(8,128)S(1)}, u32[]{:S(2)}, u32[]{:S(2)}) %collective-permute-start.2) | collective-permute-done | bytes 40992 | tf_op jit(solution)/shard_map/ppermute | solution.py:885
  12.0 0.0 collective-permute-done.3.got_first
  12.0 1.4 %down.1 = (f32[128,128]{1,0:T(8,128)S(1)}, f32[10,184,128]{2,1,0:T(8,128)S(1)}, f32[10,104,128]{2,1,0:T(8,128)S(1)}, f32[10,64,128]{2,1,0:T(8,128)S(1)}, f32[16,48,128]{2,1,0:T(8,128)S(1)}) custom-call(f32[80,128]{1,0:T(8,128)S(1)} %collective-permute-done.2.got_second, f32[80,128]{1,0:T(8,128)S(1)} %collective-permute-done.3.got_first, ...), custom_call_target="tpu_custom_call" | custom-call | tf_op jit(solution)/shard_map/down/pallas_call | solution.py:891
  13.4 12.4 %all_to_all.11 = f32[32,4,128]{2,1,0:T(4,128)S(1)} all-to-all(f32[32,4,128]{2,1,0:T(4,128)S(1)} %bitcast.3), channel_id=1, replica_groups=mesh['gx'=4,'gy'=8] {'gx','gy'}, dimensions={0} | all-to-all | bytes 131072 | tf_op jit(solution)/shard_map/all_to_all | solution.py:907
  25.8 2.3 %up.1 = f32[2,128,128]{2,1,0:T(8,128)} custom-call(f32[128,128]{1,0:T(8,128)S(1)} %bitcast.2, f32[10,184,128]{2,1,0:T(8,128)S(1)} %get-tuple-element.21.state0, f32[10,104,128]{2,1,0:T(8,128)S(1)} %get-tuple-element.22.state1, f32[10,64,128]{2,1,0:T(8,128)S(1)} %get-tuple-element.23.state2, f32[16,48,128]{2,1,0:T(8,128)S(1)} %get-tuple-element.24.state3), custom_call_target="tpu_custom_call" | custom-call | tf_op jit(solution)/shard_map/up/pallas_call | solution.py:910
Async XLA Ops:
  1.6 5.0 %collective-permute-start = (f32[64,128]{1,0:T(8,128)S(1)}, f32[64,128]{1,0:T(8,128)S(1)}, u32[]{:S(2)}, u32[]{:S(2)}) collective-permute-start(f32[64,128]{1,0:T(8,128)S(1)} %get-tuple-element.16), channel_id=1, source_target_pairs={{0,8},{1,9},{2,10},{3,11},{4,12},{5,13},{6,14},{7,15},{8,0},{9,1},... | collective-permute-start | bytes 98312 | tf_op jit(solution)/shard_map/ppermute | solution.py:865
  4.7 1.9 %collective-permute-start.1 = (f32[64,128]{1,0:T(8,128)S(1)}, f32[64,128]{1,0:T(8,128)S(1)}, u32[]{:S(2)}, u32[]{:S(2)}) collective-permute-start(f32[64,128]{1,0:T(8,128)S(1)} %get-tuple-element.17), channel_id=1, source_target_pairs={{0,1},{1,0},{2,3},{3,2},{4,5},{5,4},{6,7},{7,6},{8,16},{9,17},{10,... | collective-permute-start | bytes 98312 | tf_op jit(solution)/shard_map/ppermute | solution.py:864
  6.8 5.2 %collective-permute-start.2 = (f32[80,128]{1,0:T(8,128)S(1)}, f32[80,128]{1,0:T(8,128)S(1)}, u32[]{:S(2)}, u32[]{:S(2)}) collective-permute-start(f32[80,128]{1,0:T(8,128)S(1)} %get-tuple-element.18), channel_id=1, source_target_pairs={{0,8},{1,2},{2,1},{3,4},{4,3},{5,6},{6,5},{7,15},{8,0},{9,10},{10,... | collective-permute-start | bytes 122888 | tf_op jit(solution)/shard_map/ppermute | solution.py:885
  10.1 2.0 %collective-permute-start.3 = (f32[80,128]{1,0:T(8,128)S(1)}, f32[80,128]{1,0:T(8,128)S(1)}, u32[]{:S(2)}, u32[]{:S(2)}) collective-permute-start(f32[80,128]{1,0:T(8,128)S(1)} %get-tuple-element.19), channel_id=1, source_target_pairs={{0,1},{1,0},{2,3},{3,2},{4,5},{5,4},{6,7},{7,6},{8,9},{9,8},{10,11... | collective-permute-start | bytes 122888 | tf_op jit(solution)/shard_map/ppermute | solution.py:886

commit v8 on v7

--- a/solution.py
+++ b/solution.py
@@ -79,7 +79,7 @@
     return to_left, q >> 1, cell
 
 
-def strips_kernel(size_x, wet, held, got_first, got_second, first, second):
+def strips_kernel(size_x, wet, got_second, got_first, held, first, second):
     index_x = lax.axis_index("gx")
     odd_x = index_x % 2 == 1
     odd_y = lax.axis_index("gy") % 2 == 1
@@ -120,7 +120,7 @@
         second[rows, :] = jnp.where(odd_y, right, left)
 
 
-def halves_kernel(size_x, wet, held, got_first, got_second, fields):
+def halves_kernel(size_x, wet, got_second, got_first, held, fields):
     index_x = lax.axis_index("gx")
     odd_x = index_x % 2 == 1
     wetness = wet[0, 0].astype(F32)
@@ -864,7 +864,7 @@
     second = lax.ppermute(second, axes, routes[1])
     first = lax.ppermute(first, axes, routes[0])
     strip = jax.ShapeDtypeStruct((MESSAGE, LANES), F32)
-    got = (first, second)
+    got = (second, first)
     first, second = pl.pallas_call(
         functools.partial(strips_kernel, size_x),
         out_shape=(strip, strip),
@@ -872,7 +872,7 @@
         out_specs=(VMEM_SPEC,) * 2,
         compiler_params=params(),
         name="strips",
-    )(wet_tiles, held, *got)
+    )(wet_tiles, *got, held)
     fields = pl.pallas_call(
         functools.partial(halves_kernel, size_x),
         out_shape=pltpu.VMEM((8, HELD[0], LANES), F32),
@@ -881,7 +881,7 @@
         cost_estimate=pl.CostEstimate(flops=1 << 20, bytes_accessed=1 << 21, transcendentals=0),
         compiler_params=params(),
         name="halves",
-    )(wet_tiles, held, *got)
+    )(wet_tiles, *got, held)
     second = lax.ppermute(second, axes, routes[3])
     first = lax.ppermute(first, axes, routes[2])
 

time: 28.3 us -> 27.9 us (0.986)
  blocking collectives: 12.4 us -> 11.4 us
  starting transfers between devices: 6.3 us -> 6.76 us
    ppermute x1, starting transfers between devices: 3.21 us -> 2.09 us  [per_device(): second = lax.ppermute(second, axes, routes[3])]
    ppermute x1, starting transfers between devices: 3.09 us -> 4.15 us  [per_device(): first = lax.ppermute(first, axes, routes[0])]
    all_to_all x1, blocking collectives: 12.4 us -> 11.4 us  [per_device(): gathered = lax.all_to_all(chunks, axes, 0, 0, tiled=True)]
    ppermute x1, starting transfers between devices: 0.01 us -> 0.52 us  [per_device(): second = lax.ppermute(second, axes, routes[1])]
where the time goes in v8:
time: 27.9 us; the launch traced here: 27.7 us
  blocking collectives  11.4 us (41%)
  starting transfers between devices  6.76 us (24%)
  Pallas kernels  5.18 us (19%)
  waiting for transfers between devices  3.63 us (13%)
  between operations  0.68 us (2%)
    all_to_all x1, blocking collectives, per_device(): gathered = lax.all_to_all(chunks, axes, 0, 0, tiled=True)  11.4 us
    ppermute x1, starting transfers between devices, per_device(): first = lax.ppermute(first, axes, routes[0])  4.15 us
    pallas_call x1, Pallas kernels, per_device(): pl.pallas_call(functools.partial(up_kernel, size_x, size_y), out_shape=ja...  2.34 us
    ppermute x1, starting transfers between devices, per_device(): second = lax.ppermute(second, axes, routes[3])  2.09 us
    ppermute x1, waiting for transfers between devices, per_device(): first = lax.ppermute(first, axes, routes[0])  1.89 us
    ppermute x1, waiting for transfers between devices, per_device(): second = lax.ppermute(second, axes, routes[3])  1.73 us
    pallas_call x1, Pallas kernels, per_device(): pl.pallas_call(functools.partial(down_kernel, size_y, devices), out_shape...  1.4 us
    pallas_call x1, Pallas kernels, per_device(): pl.pallas_call(bands_kernel, out_shape=(held_shape, band, band), in_specs...  0.97 us
  transfers between devices with their start and end apart: 4, of which 2 were waited for; matrix products, arithmetic and copies ran while one was open for 0% of the time, Pallas kernels for 1%

profile of v8, /device:TPU:0, one launch (start us, length us, event | category | flops | bytes accessed | tf_op | source)
XLA Modules:
  0.0 27.7 jit_solution(13183585677769520373)
XLA Ops:
  0.7 1.0 %bands.1 = (f32[4,184,128]{2,1,0:T(8,128)S(1)}, f32[64,128]{1,0:T(8,128)S(1)}, f32[64,128]{1,0:T(8,128)S(1)}) custom-call(s32[1,1]{1,0:T(1,128)S(6)} %copy.5.wet, f32[2,128,128]{2,1,0:T(8,128)} %right_side.1, f32[128,128]{1,0:T(8,128)} %shift_coef.1, f32[128,128]{1,0:T(8,128)} %viscosity.1), custom_call_target="tpu_custom_call" | custom-call | tf_op jit(solution)/shard_map/bands/pallas_call | solution.py:849
  1.6 0.5 %collective-permute-start = (f32[64,128]{1,0:T(8,128)S(1)}, f32[64,128]{1,0:T(8,128)S(1)}, u32[]{:S(2)}, u32[]{:S(2)}) collective-permute-start(f32[64,128]{1,0:T(8,128)S(1)} %get-tuple-element.15), channel_id=1, source_target_pairs={{0,1},{1,0},{2,3},{3,2},{4,5},{5,4},{6,7},{7,6},{8,16},{9,17},{10,... | collective-permute-start | bytes 98312 | tf_op jit(solution)/shard_map/ppermute | solution.py:864
  2.2 4.1 %collective-permute-start.1 = (f32[64,128]{1,0:T(8,128)S(1)}, f32[64,128]{1,0:T(8,128)S(1)}, u32[]{:S(2)}, u32[]{:S(2)}) collective-permute-start(f32[64,128]{1,0:T(8,128)S(1)} %get-tuple-element.16), channel_id=1, source_target_pairs={{0,8},{1,9},{2,10},{3,11},{4,12},{5,13},{6,14},{7,15},{8,0},{9,1},... | collective-permute-start | bytes 98312 | tf_op jit(solution)/shard_map/ppermute | solution.py:865
  6.3 0.0 collective-permute-done.got_second
  6.3 1.9 %collective-permute-done.1.got_first = f32[64,128]{1,0:T(8,128)S(1)} collective-permute-done((f32[64,128]{1,0:T(8,128)S(1)}, f32[64,128]{1,0:T(8,128)S(1)}, u32[]{:S(2)}, u32[]{:S(2)}) %collective-permute-start.1) | collective-permute-done | bytes 32800 | tf_op jit(solution)/shard_map/ppermute | solution.py:865
  8.2 0.2 strips.1
  8.4 2.1 %collective-permute-start.2 = (f32[80,128]{1,0:T(8,128)S(1)}, f32[80,128]{1,0:T(8,128)S(1)}, u32[]{:S(2)}, u32[]{:S(2)}) collective-permute-start(f32[80,128]{1,0:T(8,128)S(1)} %get-tuple-element.18), channel_id=1, source_target_pairs={{0,8},{1,2},{2,1},{3,4},{4,3},{5,6},{6,5},{7,15},{8,0},{9,10},{10,... | collective-permute-start | bytes 122888 | tf_op jit(solution)/shard_map/ppermute | solution.py:885
  10.5 0.0 collective-permute-start.3
  10.5 0.2 halves.1.held
  10.8 1.7 %collective-permute-done.2.got_second = f32[80,128]{1,0:T(8,128)S(1)} collective-permute-done((f32[80,128]{1,0:T(8,128)S(1)}, f32[80,128]{1,0:T(8,128)S(1)}, u32[]{:S(2)}, u32[]{:S(2)}) %collective-permute-start.2) | collective-permute-done | bytes 40992 | tf_op jit(solution)/shard_map/ppermute | solution.py:885
  12.5 0.0 collective-permute-done.3.got_first
  12.5 1.4 %down.1 = (f32[128,128]{1,0:T(8,128)S(1)}, f32[10,184,128]{2,1,0:T(8,128)S(1)}, f32[10,104,128]{2,1,0:T(8,128)S(1)}, f32[10,64,128]{2,1,0:T(8,128)S(1)}, f32[16,48,128]{2,1,0:T(8,128)S(1)}) custom-call(f32[80,128]{1,0:T(8,128)S(1)} %collective-permute-done.2.got_second, f32[80,128]{1,0:T(8,128)S(1)} %collective-permute-done.3.got_first, ...), custom_call_target="tpu_custom_call" | custom-call | tf_op jit(solution)/shard_map/down/pallas_call | solution.py:891
  13.9 11.4 %all_to_all.11 = f32[32,4,128]{2,1,0:T(4,128)S(1)} all-to-all(f32[32,4,128]{2,1,0:T(4,128)S(1)} %bitcast.3), channel_id=1, replica_groups=mesh['gx'=4,'gy'=8] {'gx','gy'}, dimensions={0} | all-to-all | bytes 131072 | tf_op jit(solution)/shard_map/all_to_all | solution.py:907
  25.3 2.3 %up.1 = f32[2,128,128]{2,1,0:T(8,128)} custom-call(f32[128,128]{1,0:T(8,128)S(1)} %bitcast.2, f32[10,184,128]{2,1,0:T(8,128)S(1)} %get-tuple-element.21.state0, f32[10,104,128]{2,1,0:T(8,128)S(1)} %get-tuple-element.22.state1, f32[10,64,128]{2,1,0:T(8,128)S(1)} %get-tuple-element.23.state2, f32[16,48,128]{2,1,0:T(8,128)S(1)} %get-tuple-element.24.state3), custom_call_target="tpu_custom_call" | custom-call | tf_op jit(solution)/shard_map/up/pallas_call | solution.py:910
Async XLA Ops:
  1.6 4.7 %collective-permute-start = (f32[64,128]{1,0:T(8,128)S(1)}, f32[64,128]{1,0:T(8,128)S(1)}, u32[]{:S(2)}, u32[]{:S(2)}) collective-permute-start(f32[64,128]{1,0:T(8,128)S(1)} %get-tuple-element.15), channel_id=1, source_target_pairs={{0,1},{1,0},{2,3},{3,2},{4,5},{5,4},{6,7},{7,6},{8,16},{9,17},{10,... | collective-permute-start | bytes 98312 | tf_op jit(solution)/shard_map/ppermute | solution.py:864
  2.2 6.0 %collective-permute-start.1 = (f32[64,128]{1,0:T(8,128)S(1)}, f32[64,128]{1,0:T(8,128)S(1)}, u32[]{:S(2)}, u32[]{:S(2)}) collective-permute-start(f32[64,128]{1,0:T(8,128)S(1)} %get-tuple-element.16), channel_id=1, source_target_pairs={{0,8},{1,9},{2,10},{3,11},{4,12},{5,13},{6,14},{7,15},{8,0},{9,1},... | collective-permute-start | bytes 98312 | tf_op jit(solution)/shard_map/ppermute | solution.py:865
  8.4 4.1 %collective-permute-start.2 = (f32[80,128]{1,0:T(8,128)S(1)}, f32[80,128]{1,0:T(8,128)S(1)}, u32[]{:S(2)}, u32[]{:S(2)}) collective-permute-start(f32[80,128]{1,0:T(8,128)S(1)} %get-tuple-element.18), channel_id=1, source_target_pairs={{0,8},{1,2},{2,1},{3,4},{4,3},{5,6},{6,5},{7,15},{8,0},{9,10},{10,... | collective-permute-start | bytes 122888 | tf_op jit(solution)/shard_map/ppermute | solution.py:885
  10.5 2.0 %collective-permute-start.3 = (f32[80,128]{1,0:T(8,128)S(1)}, f32[80,128]{1,0:T(8,128)S(1)}, u32[]{:S(2)}, u32[]{:S(2)}) collective-permute-start(f32[80,128]{1,0:T(8,128)S(1)} %get-tuple-element.19), channel_id=1, source_target_pairs={{0,1},{1,0},{2,3},{3,2},{4,5},{5,4},{6,7},{7,6},{8,9},{9,8},{10,11... | collective-permute-start | bytes 122888 | tf_op jit(solution)/shard_map/ppermute | solution.py:886

commit v9 on v8

--- a/solution.py
+++ b/solution.py
@@ -426,30 +426,41 @@
             ),
         )
 
+    def farther(self, value):
+        return (
+            jnp.where(
+                self.odd_lane, self.along(value, 3 * self.step), self.along(value, 2 * self.step)
+            ),
+            jnp.where(
+                self.odd_lane, self.along(value, -2 * self.step), self.along(value, -3 * self.step)
+            ),
+        )
+
+    def rows_beside(self, here):
+        above = jnp.where(self.top, 0.0, self.down(here, self.row_step))
+        below = jnp.where(self.bottom, 0.0, self.down(here, -self.row_step))
+        return jnp.minimum(here, above), jnp.minimum(here, below)
+
     def coefficients(self, viscous, reaction):
-        here, reactions, beyond = self.paired(viscous), self.paired(reaction), self.outside(viscous)
+        here, beyond, far = self.paired(viscous), self.outside(viscous), self.farther(viscous)
+        reactions, reactions_beyond = self.paired(reaction), self.outside(reaction)
+        edges = (self.leftmost, self.rightmost)
         self.middle = jnp.minimum(here[0], here[1])
-        self.outer = [
-            jnp.minimum(here[0], jnp.where(self.leftmost, 0.0, beyond[0])),
-            jnp.minimum(here[1], jnp.where(self.rightmost, 0.0, beyond[1])),
-        ]
-        self.north, self.south, self.weights = [], [], []
+        self.outer, self.north, self.south = [], [], []
+        self.weights, self.weights_beyond = [], []
         for p in range(2):
-            above = jnp.where(self.top, 0.0, self.down(here[p], self.row_step))
-            below = jnp.where(self.bottom, 0.0, self.down(here[p], -self.row_step))
-            self.north.append(jnp.minimum(here[p], above))
-            self.south.append(jnp.minimum(here[p], below))
-            diagonal = reactions[p] + (
-                (self.middle + self.outer[p]) + (self.north[p] + self.south[p])
-            )
+            outer = jnp.minimum(here[p], jnp.where(edges[p], 0.0, beyond[p]))
+            north, south = self.rows_beside(here[p])
+            diagonal = reactions[p] + ((self.middle + outer) + (north + south))
             self.weights.append(OMEGA / diagonal)
+            self.outer.append(outer)
+            self.north.append(north)
+            self.south.append(south)
+            next_outer = jnp.minimum(beyond[p], far[p])
+            north, south = self.rows_beside(beyond[p])
+            diagonal = reactions_beyond[p] + ((outer + next_outer) + (north + south))
+            self.weights_beyond.append(OMEGA / diagonal)
         return here[0] + here[1], reactions[0] + reactions[1]
-
-    def weigh(self):
-        self.weights_beyond = (
-            self.along(self.weights[1], 2 * self.step),
-            self.along(self.weights[0], -2 * self.step),
-        )
 
     def take(self, source):
         self.values, self.values_beyond = self.paired(source), self.outside(source)
@@ -469,18 +480,29 @@
             total = left if total is None else total + left
         return total
 
-    def corrected(self, here, beyond, across):
+    def prepare(self):
         parts = []
         for p in range(2):
             within = jnp.where(self.odd_row, self.north[p], self.south[p])
             out = jnp.where(self.odd_row, self.south[p], self.north[p])
             weight = self.weights[p]
             centre = KEEP + weight * (self.middle + within)
-            parts.append(
-                (self.swept[p] + centre * here)
-                + ((weight * self.outer[p]) * beyond[p] + (weight * out) * across)
-            )
-        return jnp.where(self.odd_lane, parts[1], parts[0])
+            parts.append((self.swept[p], centre, weight * self.outer[p], weight * out))
+        self.parts = parts
+        self.left_parts = [self.along(value, 2 * self.step) for value in parts[1]]
+        self.right_parts = [self.along(value, -2 * self.step) for value in parts[0]]
+
+    def corrected(self, here, left, right):
+        def swept(part, own, side):
+            return (part[0] + part[1] * own[0]) + (part[2] * side[0] + part[3] * own[1])
+
+        even, odd = swept(self.parts[0], here, left), swept(self.parts[1], here, right)
+        before, after = swept(self.left_parts, left, here), swept(self.right_parts, right, here)
+        return (
+            jnp.where(self.odd_lane, odd, even),
+            jnp.where(self.odd_lane, even, before),
+            jnp.where(self.odd_lane, after, odd),
+        )
 
 
 def coarse_solve(grid, buffer, rows_total, cols_total, width, meanwhile):
@@ -509,7 +531,7 @@
         first, second = [pl.ds(begin, rows // 2, stride=2) for begin in range(2)]
         return scale * (read(buffer, slot, first) + read(buffer, slot, second))
 
-    def opened(index, value):
+    def opened(index, value, slot):
         level = levels[index]
         rows = level.shape[0]
         if value.shape[0] == rows:
@@ -519,12 +541,12 @@
         half = rows // 2
         blank = jnp.zeros((SUB, width), F32)
         for begin in range(2):
-            write(buffer, 0, pl.ds(begin, half, stride=2), value)
-        write(buffer, 1, slice(SUB, 2 * SUB), blank)
-        write(buffer, 1, slice(rows, rows + SUB), blank)
+            write(buffer, slot, pl.ds(begin, half, stride=2), value)
+        write(buffer, slot + 1, slice(SUB, 2 * SUB), blank)
+        write(buffer, slot + 1, slice(rows, rows + SUB), blank)
         for begin in (SUB + 2, SUB - 1):
-            write(buffer, 1, pl.ds(begin, half, stride=2), value)
-        return read(buffer, 0, slice(0, rows)), read(buffer, 1, slice(SUB, SUB + rows))
+            write(buffer, slot + 1, pl.ds(begin, half, stride=2), value)
+        return read(buffer, slot, slice(0, rows)), read(buffer, slot + 1, slice(SUB, SUB + rows))
 
     viscous, reaction, source = [None] * 5, [None] * 5, [None] * 5
     viscous[0], reaction[0], source[0] = whole(2), whole(1), whole(0)
@@ -564,20 +586,15 @@
     levels[0].take(source[0])
     coefficients(0)
     coefficients(1)
-    levels[0].weigh()
-    coefficients(2)
-    levels[1].weigh()
     residual(0)
     levels[1].take(source[1])
-    coefficients(3)
-    levels[2].weigh()
+    coefficients(2)
     residual(1)
     levels[2].take(source[2])
-    meanwhile()
-    levels[3].weigh()
-    viscous_columns, reaction_columns = spread(viscous[4]), spread(reaction[4])
+    coefficients(3)
     residual(2)
     levels[3].take(source[3])
+    viscous_columns, reaction_columns = spread(viscous[4]), spread(reaction[4])
 
     top, bottom = last.top[:, :LANES], last.bottom[:, :LANES]
     pulls, weights = [], []
@@ -597,6 +614,9 @@
             pulls.append([weight * link for link in links])
     residual(3)
     pushed = [w * s for w, s in zip(weights, spread(source[4]))]
+    meanwhile()
+    for index in range(COARSE - 1, -1, -1):
+        levels[index].prepare()
     values = pushed
     for _ in range(COARSE_SWEEPS - 1):
         following = []
@@ -626,26 +646,12 @@
             found.append(value)
         return found[0] if columns == 1 else jnp.concatenate(found, 1)
 
-    index = COARSE - 1
-    here, across = opened(index, laid(0))
-    beyond = [opened(index, laid(shift))[0] for shift in (1, -1)]
-    correction = levels[index].corrected(here, beyond, across)
-    for index in range(COARSE - 2, -1, -1):
-        level, next_level = levels[index], levels[index + 1]
-        sides = [next_level.along(correction, 2 * level.step), next_level.along(correction, -2 * level.step)]
-        here, across = opened(index, correction)
-        beyond = [opened_sides(level, buffer, side) for side in sides]
-        correction = level.corrected(here, beyond, across)
-    return correction
-
-
-def opened_sides(level, buffer, value):
-    rows = level.shape[0]
-    if value.shape[0] == rows:
-        return value
-    for begin in range(2):
-        write(buffer, 2, pl.ds(begin, rows // 2, stride=2), value)
-    return read(buffer, 2, slice(0, rows))
+    corrections = [laid(shift) for shift in (0, 1, -1)]
+    for index in range(COARSE - 1, -1, -1):
+        corrections = levels[index].corrected(
+            *[opened(index, value, 2 * at) for at, value in enumerate(corrections)]
+        )
+    return corrections
 
 
 def up_kernel(size_x, size_y, gathered, state0, state1, state2, state3, out, *refs):
@@ -719,16 +725,18 @@
                         state3[ITERATE + slot, rows, :] + state3[WEIGHT + p, rows, :] * ringed[0:1]
                     )
 
-    correction = coarse_solve(grid, buffer, rows_total, cols_total, width, complete_ring)
-
-    whole[GUARD : GUARD + rows_total, :] = correction
-    whole[0:GUARD, :] = jnp.zeros((GUARD, width), F32)
-    whole[GUARD + rows_total :, :] = jnp.zeros((2 * SUB, width), F32)
-    near_rows = whole[pl.ds(pl.multiple_of(CELLS * index_x, SUB), 3 * SUB), :]
+    corrections = coarse_solve(grid, buffer, rows_total, cols_total, width, complete_ring)
+
+    blank = jnp.zeros((SUB, width), F32)
+    for kind, correction in enumerate(corrections):
+        whole[kind, GUARD : GUARD + rows_total, :] = correction
+        whole[kind, 0:GUARD, :] = blank
+        whole[kind, GUARD + rows_total : GUARD + rows_total + SUB, :] = blank
+    near_rows = pl.ds(pl.multiple_of(CELLS * index_x, SUB), 3 * SUB)
     for comp in range(2):
+        shift = (2 * width - cols_total * comp - CELLS * index_y) % width
         for kind in range(3):
-            shift = (2 * width - cols_total * comp - CELLS * index_y + (0, -1, 1)[kind]) % width
-            turned = pltpu.roll(near_rows, shift, 1)
+            turned = pltpu.roll(whole[kind, near_rows, :], shift, 1)
             if columns > 1:
                 tall_lane = iota(1, (3 * SUB, LANES))
                 turned = jnp.where(
@@ -749,7 +757,7 @@
         for tile in range(2):
             first = SUB * tile - 1
             at = GUARD + first
-            here, right, left = [tile_at(window, 3 * comp + kind, at) for kind in range(3)]
+            here, left, right = [tile_at(window, 3 * comp + kind, at) for kind in range(3)]
             for parity in range(2):
                 across = tile_at(window, 3 * comp, at + (1 if parity else -1))
                 found = swept_rows(swept3, 3, first, parity, here, (left, right), across, comp)
@@ -914,8 +922,8 @@
         out_specs=VMEM_SPEC,
         scratch_shapes=[
             pltpu.VMEM((3, width // LANES, rows_total, LANES), F32),
-            pltpu.VMEM((3, width // LANES, rows_total + 3 * SUB, LANES), F32),
-            pltpu.VMEM((rows_total + 3 * SUB, width), F32),
+            pltpu.VMEM((6, width // LANES, rows_total + 3 * SUB, LANES), F32),
+            pltpu.VMEM((3, rows_total + 2 * SUB, width), F32),
             pltpu.VMEM((6, 5 * SUB, LANES), F32),
             pltpu.VMEM((4, HELD[3], LANES), F32),
         ]

time: 27.9 us -> 27.6 us (0.989)
  no operation moved by 1% of the time
where the time goes in v9:
time: 27.6 us; the launch traced here: 27.4 us
  blocking collectives  11.4 us (41%)
  starting transfers between devices  6.76 us (24%)
  Pallas kernels  4.94 us (18%)
  waiting for transfers between devices  3.63 us (13%)
  between operations  0.68 us (2%)
    all_to_all x1, blocking collectives, per_device(): gathered = lax.all_to_all(chunks, axes, 0, 0, tiled=True)  11.4 us
    ppermute x1, starting transfers between devices, per_device(): first = lax.ppermute(first, axes, routes[0])  4.15 us
    pallas_call x1, Pallas kernels, per_device(): pl.pallas_call(functools.partial(up_kernel, size_x, size_y), out_shape=ja...  2.11 us
    ppermute x1, starting transfers between devices, per_device(): second = lax.ppermute(second, axes, routes[3])  2.09 us
    ppermute x1, waiting for transfers between devices, per_device(): first = lax.ppermute(first, axes, routes[0])  1.89 us
    ppermute x1, waiting for transfers between devices, per_device(): second = lax.ppermute(second, axes, routes[3])  1.73 us
    pallas_call x1, Pallas kernels, per_device(): pl.pallas_call(functools.partial(down_kernel, size_y, devices), out_shape...  1.4 us
    pallas_call x1, Pallas kernels, per_device(): pl.pallas_call(bands_kernel, out_shape=(held_shape, band, band), in_specs...  0.97 us
  transfers between devices with their start and end apart: 4, of which 2 were waited for; matrix products, arithmetic and copies ran while one was open for 0% of the time, Pallas kernels for 1%

profile of v9, /device:TPU:0, one launch (start us, length us, event | category | flops | bytes accessed | tf_op | source)
XLA Modules:
  0.0 27.4 jit_solution(13714347489141813585)
XLA Ops:
  0.7 1.0 %bands.1 = (f32[4,184,128]{2,1,0:T(8,128)S(1)}, f32[64,128]{1,0:T(8,128)S(1)}, f32[64,128]{1,0:T(8,128)S(1)}) custom-call(s32[1,1]{1,0:T(1,128)S(6)} %copy.5.wet, f32[2,128,128]{2,1,0:T(8,128)} %right_side.1, f32[128,128]{1,0:T(8,128)} %shift_coef.1, f32[128,128]{1,0:T(8,128)} %viscosity.1), custom_call_target="tpu_custom_call" | custom-call | tf_op jit(solution)/shard_map/bands/pallas_call | solution.py:857
  1.6 0.5 %collective-permute-start = (f32[64,128]{1,0:T(8,128)S(1)}, f32[64,128]{1,0:T(8,128)S(1)}, u32[]{:S(2)}, u32[]{:S(2)}) collective-permute-start(f32[64,128]{1,0:T(8,128)S(1)} %get-tuple-element.15), channel_id=1, source_target_pairs={{0,1},{1,0},{2,3},{3,2},{4,5},{5,4},{6,7},{7,6},{8,16},{9,17},{10,... | collective-permute-start | bytes 98312 | tf_op jit(solution)/shard_map/ppermute | solution.py:872
  2.2 4.1 %collective-permute-start.1 = (f32[64,128]{1,0:T(8,128)S(1)}, f32[64,128]{1,0:T(8,128)S(1)}, u32[]{:S(2)}, u32[]{:S(2)}) collective-permute-start(f32[64,128]{1,0:T(8,128)S(1)} %get-tuple-element.16), channel_id=1, source_target_pairs={{0,8},{1,9},{2,10},{3,11},{4,12},{5,13},{6,14},{7,15},{8,0},{9,1},... | collective-permute-start | bytes 98312 | tf_op jit(solution)/shard_map/ppermute | solution.py:873
  6.3 0.0 collective-permute-done.got_second
  6.3 1.9 %collective-permute-done.1.got_first = f32[64,128]{1,0:T(8,128)S(1)} collective-permute-done((f32[64,128]{1,0:T(8,128)S(1)}, f32[64,128]{1,0:T(8,128)S(1)}, u32[]{:S(2)}, u32[]{:S(2)}) %collective-permute-start.1) | collective-permute-done | bytes 32800 | tf_op jit(solution)/shard_map/ppermute | solution.py:873
  8.2 0.2 strips.1
  8.4 2.1 %collective-permute-start.2 = (f32[80,128]{1,0:T(8,128)S(1)}, f32[80,128]{1,0:T(8,128)S(1)}, u32[]{:S(2)}, u32[]{:S(2)}) collective-permute-start(f32[80,128]{1,0:T(8,128)S(1)} %get-tuple-element.18), channel_id=1, source_target_pairs={{0,8},{1,2},{2,1},{3,4},{4,3},{5,6},{6,5},{7,15},{8,0},{9,10},{10,... | collective-permute-start | bytes 122888 | tf_op jit(solution)/shard_map/ppermute | solution.py:893
  10.5 0.0 collective-permute-start.3
  10.5 0.2 halves.1.held
  10.8 1.7 %collective-permute-done.2.got_second = f32[80,128]{1,0:T(8,128)S(1)} collective-permute-done((f32[80,128]{1,0:T(8,128)S(1)}, f32[80,128]{1,0:T(8,128)S(1)}, u32[]{:S(2)}, u32[]{:S(2)}) %collective-permute-start.2) | collective-permute-done | bytes 40992 | tf_op jit(solution)/shard_map/ppermute | solution.py:893
  12.5 0.0 collective-permute-done.3.got_first
  12.5 1.4 %down.1 = (f32[128,128]{1,0:T(8,128)S(1)}, f32[10,184,128]{2,1,0:T(8,128)S(1)}, f32[10,104,128]{2,1,0:T(8,128)S(1)}, f32[10,64,128]{2,1,0:T(8,128)S(1)}, f32[16,48,128]{2,1,0:T(8,128)S(1)}) custom-call(f32[80,128]{1,0:T(8,128)S(1)} %collective-permute-done.2.got_second, f32[80,128]{1,0:T(8,128)S(1)} %collective-permute-done.3.got_first, ...), custom_call_target="tpu_custom_call" | custom-call | tf_op jit(solution)/shard_map/down/pallas_call | solution.py:899
  13.9 11.4 %all_to_all.11 = f32[32,4,128]{2,1,0:T(4,128)S(1)} all-to-all(f32[32,4,128]{2,1,0:T(4,128)S(1)} %bitcast.3), channel_id=1, replica_groups=mesh['gx'=4,'gy'=8] {'gx','gy'}, dimensions={0} | all-to-all | bytes 131072 | tf_op jit(solution)/shard_map/all_to_all | solution.py:915
  25.3 2.1 %up.1 = f32[2,128,128]{2,1,0:T(8,128)} custom-call(f32[128,128]{1,0:T(8,128)S(1)} %bitcast.2, f32[10,184,128]{2,1,0:T(8,128)S(1)} %get-tuple-element.21.state0, f32[10,104,128]{2,1,0:T(8,128)S(1)} %get-tuple-element.22.state1, f32[10,64,128]{2,1,0:T(8,128)S(1)} %get-tuple-element.23.state2, f32[16,48,128]{2,1,0:T(8,128)S(1)} %get-tuple-element.24.state3), custom_call_target="tpu_custom_call" | custom-call | tf_op jit(solution)/shard_map/up/pallas_call | solution.py:918
Async XLA Ops:
  1.6 4.7 %collective-permute-start = (f32[64,128]{1,0:T(8,128)S(1)}, f32[64,128]{1,0:T(8,128)S(1)}, u32[]{:S(2)}, u32[]{:S(2)}) collective-permute-start(f32[64,128]{1,0:T(8,128)S(1)} %get-tuple-element.15), channel_id=1, source_target_pairs={{0,1},{1,0},{2,3},{3,2},{4,5},{5,4},{6,7},{7,6},{8,16},{9,17},{10,... | collective-permute-start | bytes 98312 | tf_op jit(solution)/shard_map/ppermute | solution.py:872
  2.2 6.0 %collective-permute-start.1 = (f32[64,128]{1,0:T(8,128)S(1)}, f32[64,128]{1,0:T(8,128)S(1)}, u32[]{:S(2)}, u32[]{:S(2)}) collective-permute-start(f32[64,128]{1,0:T(8,128)S(1)} %get-tuple-element.16), channel_id=1, source_target_pairs={{0,8},{1,9},{2,10},{3,11},{4,12},{5,13},{6,14},{7,15},{8,0},{9,1},... | collective-permute-start | bytes 98312 | tf_op jit(solution)/shard_map/ppermute | solution.py:873
  8.4 4.1 %collective-permute-start.2 = (f32[80,128]{1,0:T(8,128)S(1)}, f32[80,128]{1,0:T(8,128)S(1)}, u32[]{:S(2)}, u32[]{:S(2)}) collective-permute-start(f32[80,128]{1,0:T(8,128)S(1)} %get-tuple-element.18), channel_id=1, source_target_pairs={{0,8},{1,2},{2,1},{3,4},{4,3},{5,6},{6,5},{7,15},{8,0},{9,10},{10,... | collective-permute-start | bytes 122888 | tf_op jit(solution)/shard_map/ppermute | solution.py:893
  10.5 2.0 %collective-permute-start.3 = (f32[80,128]{1,0:T(8,128)S(1)}, f32[80,128]{1,0:T(8,128)S(1)}, u32[]{:S(2)}, u32[]{:S(2)}) collective-permute-start(f32[80,128]{1,0:T(8,128)S(1)} %get-tuple-element.19), channel_id=1, source_target_pairs={{0,1},{1,0},{2,3},{3,2},{4,5},{5,4},{6,7},{7,6},{8,9},{9,8},{10,11... | collective-permute-start | bytes 122888 | tf_op jit(solution)/shard_map/ppermute | solution.py:894

commit v10 on v9

--- a/solution.py
+++ b/solution.py
@@ -99,10 +99,10 @@
         return jnp.where(odd_x, one, two) if top else jnp.where(odd_x, two, one)
 
     places = [rim_place(half, lane) for half in range(2)]
-    for tile in range(HALF_TILES):
-        found = []
-        for half in range(2):
-            to_left, owner, cell = places[half]
+    found = {}
+    for half in range(2):
+        _, owner, cell = places[half]
+        for tile in range(HALF_TILES):
             at = tile + half * HALF_TILES
             value = None
             for field in range(4):
@@ -112,9 +112,10 @@
                 value = value * jnp.where(owner == 2, 1.0, wetness)
             else:
                 value = value * jnp.where(owner == 3, above if at < rim_tiles else below, 1.0)
-            found.append(value)
-        left = jnp.where(places[0][0], found[0], found[1])
-        right = jnp.where(places[0][0], found[1], found[0])
+            found[half, tile] = value
+    for tile in range(HALF_TILES):
+        left = jnp.where(places[0][0], found[0, tile], found[1, tile])
+        right = jnp.where(places[0][0], found[1, tile], found[0, tile])
         rows = slice(SUB * tile, SUB * tile + SUB)
         first[rows, :] = jnp.where(odd_y, left, right)
         second[rows, :] = jnp.where(odd_y, right, left)
@@ -196,21 +197,35 @@
     takes = [(2 * lane + offset) & (LANES - 1) for offset in (0, 1, -1, 2)]
 
     def coefficients(level):
-        for row in tiles(level):
-            if level == 0:
+        if level == 0:
+            for row in tiles(level):
                 values = rims(row, (4, 5, 6, 7))
-                reaction, viscosity = values[:2], values[2:]
-            else:
-                start = GUARD + 2 * (row - GUARD)
-                ref = sums[level - 1]
-                value = 0.0625 * paired(ref, 3, start)
-                viscosity = [lane_take(value, t) for t in takes]
-                value = 0.25 * paired(ref, 2, start)
-                reaction = [lane_take(value, t) for t in takes[:2]]
-            for slot, value in enumerate(viscosity):
-                put(viscous[level], slot, row, value)
-            for slot, value in enumerate(reaction):
-                put(reactions[level], slot, row, value)
+                for slot, value in enumerate(values[:2]):
+                    put(reactions[level], slot, row, value)
+                for slot, value in enumerate(values[2:]):
+                    put(viscous[level], slot, row, value)
+                put(sums[level], 2, row, values[0] + values[1])
+                put(sums[level], 3, row, values[2] + values[3])
+            return
+        ref = sums[level - 1]
+        loaded = {
+            row: [
+                scale * paired(ref, slot, GUARD + 2 * (row - GUARD))
+                for slot, scale in ((2, 0.25), (3, 0.0625))
+            ]
+            for row in tiles(level)
+        }
+        found = {row: ([], []) for row in loaded}
+        for kind, index in enumerate(takes):
+            for row, (reaction, viscosity) in loaded.items():
+                value = lane_take(viscosity, index)
+                put(viscous[level], kind, row, value)
+                found[row][1].append(value)
+                if kind < 2:
+                    value = lane_take(reaction, index)
+                    put(reactions[level], kind, row, value)
+                    found[row][0].append(value)
+        for row, (reaction, viscosity) in found.items():
             put(sums[level], 2, row, reaction[0] + reaction[1])
             put(sums[level], 3, row, viscosity[0] + viscosity[1])
 
@@ -245,15 +260,22 @@
                 put(weights[level], slot, row, value)
 
     def take_sources(level):
-        for row in tiles(level):
-            if level == 0:
-                found = rims(row, (0, 1, 2, 3))
-            else:
-                start = GUARD + 2 * (row - GUARD)
-                values = [0.25 * paired(sums[level - 1], comp, start) for comp in range(2)]
-                found = [lane_take(value, t) for value in values for t in takes]
-            for slot, value in enumerate(found):
-                put(sources[level], slot, row, value)
+        if level == 0:
+            for row in tiles(level):
+                for slot, value in enumerate(rims(row, (0, 1, 2, 3))):
+                    put(sources[level], slot, row, value)
+            return
+        loaded = {
+            row: [
+                0.25 * paired(sums[level - 1], comp, GUARD + 2 * (row - GUARD))
+                for comp in range(2)
+            ]
+            for row in tiles(level)
+        }
+        for kind, index in enumerate(takes):
+            for row, values in loaded.items():
+                for comp in range(2):
+                    put(sources[level], 4 * comp + kind, row, lane_take(values[comp], index))
 
     def kinds(level):
         return 2 if level == 0 else 4
@@ -567,8 +589,8 @@
     groups = 1 if cols_total < LANES else 2
     per_group = columns // groups
 
-    def spread(value):
-        found = []
+    def spread(*arrays):
+        found = [[] for _ in arrays]
         for group in range(groups):
             for j in range(cols_left):
                 column, place = divmod(block * j, LANES)
@@ -577,7 +599,9 @@
                     place = place + (lane & (LANES - cols_total))
                 else:
                     place = jnp.full((rows_left, LANES), place, jnp.int32)
-                found.append(lane_take(value[:, LANES * column : LANES * column + LANES], place))
+                for value, columns_found in zip(arrays, found):
+                    tile = value[:, LANES * column : LANES * column + LANES]
+                    columns_found.append(lane_take(tile, place))
         return found
 
     def flat(values, group, j):
@@ -594,7 +618,7 @@
     coefficients(3)
     residual(2)
     levels[3].take(source[3])
-    viscous_columns, reaction_columns = spread(viscous[4]), spread(reaction[4])
+    viscous_columns, reaction_columns = spread(viscous[4], reaction[4])
 
     top, bottom = last.top[:, :LANES], last.bottom[:, :LANES]
     pulls, weights = [], []
@@ -613,7 +637,7 @@
             weights.append(weight)
             pulls.append([weight * link for link in links])
     residual(3)
-    pushed = [w * s for w, s in zip(weights, spread(source[4]))]
+    pushed = [w * s for w, s in zip(weights, spread(source[4])[0])]
     meanwhile()
     for index in range(COARSE - 1, -1, -1):
         levels[index].prepare()
@@ -774,22 +798,28 @@
         corr, state, whole_rows = corrs[coarse], (state0, state1, state2)[level], merged[level]
         count = (LANES >> coarse) + 2
         origin = GUARD + RIM[coarse]
-        sides = {}
-        for tile in range(-(-count // SUB)):
-            at = origin - 1 + SUB * tile
-            for comp in range(2):
-                even, odd = tile_at(corr, 2 * comp, at), tile_at(corr, 2 * comp + 1, at)
-                even_here, odd_here = lane_take(even, near), lane_take(odd, near)
-                even_next = lane_take(even, (near + 1) & (LANES - 1))
-                odd_last = lane_take(odd, (near - 1) & (LANES - 1))
-                here = jnp.where(odd_lane, odd_here, even_here)
-                whole_rows[3 * comp, at : at + SUB, :] = here
-                whole_rows[3 * comp + 1, at : at + SUB, :] = jnp.where(
-                    odd_lane, even_next, odd_here
-                )
-                whole_rows[3 * comp + 2, at : at + SUB, :] = jnp.where(
-                    odd_lane, even_here, odd_last
-                )
+        places = [
+            (comp, origin - 1 + SUB * tile)
+            for tile in range(-(-count // SUB))
+            for comp in range(2)
+        ]
+        pairs = {
+            (comp, at): (tile_at(corr, 2 * comp, at), tile_at(corr, 2 * comp + 1, at))
+            for comp, at in places
+        }
+        moved = {
+            place: [lane_take(even, near), lane_take(odd, near)]
+            for place, (even, odd) in pairs.items()
+        }
+        for place, (even, _) in pairs.items():
+            moved[place].append(lane_take(even, (near + 1) & (LANES - 1)))
+        for place, (_, odd) in pairs.items():
+            moved[place].append(lane_take(odd, (near - 1) & (LANES - 1)))
+        for (comp, at), (even_here, odd_here, even_next, odd_last) in moved.items():
+            rows = slice(at, at + SUB)
+            whole_rows[3 * comp, rows, :] = jnp.where(odd_lane, odd_here, even_here)
+            whole_rows[3 * comp + 1, rows, :] = jnp.where(odd_lane, even_next, odd_here)
+            whole_rows[3 * comp + 2, rows, :] = jnp.where(odd_lane, even_here, odd_last)
         if level > 0:
             first, tiles = -1, -(-count // SUB)
         else:

time: 27.6 us -> 27.2 us (0.986)
  Pallas kernels: 4.94 us -> 4.55 us
where the time goes in v10:
time: 27.2 us; the launch traced here: 27.1 us
  blocking collectives  11.4 us (42%)
  starting transfers between devices  6.76 us (25%)
  Pallas kernels  4.55 us (17%)
  waiting for transfers between devices  3.63 us (13%)
  between operations  0.68 us (2%)
    all_to_all x1, blocking collectives, per_device(): gathered = lax.all_to_all(chunks, axes, 0, 0, tiled=True)  11.4 us
    ppermute x1, starting transfers between devices, per_device(): first = lax.ppermute(first, axes, routes[0])  4.15 us
    ppermute x1, starting transfers between devices, per_device(): second = lax.ppermute(second, axes, routes[3])  2.09 us
    pallas_call x1, Pallas kernels, per_device(): pl.pallas_call(functools.partial(up_kernel, size_x, size_y), out_shape=ja...  2 us
    ppermute x1, waiting for transfers between devices, per_device(): first = lax.ppermute(first, axes, routes[0])  1.89 us
    ppermute x1, waiting for transfers between devices, per_device(): second = lax.ppermute(second, axes, routes[3])  1.73 us
    pallas_call x1, Pallas kernels, per_device(): pl.pallas_call(functools.partial(down_kernel, size_y, devices), out_shape...  1.17 us
    pallas_call x1, Pallas kernels, per_device(): pl.pallas_call(bands_kernel, out_shape=(held_shape, band, band), in_specs...  0.97 us
  transfers between devices with their start and end apart: 4, of which 2 were waited for; matrix products, arithmetic and copies ran while one was open for 0% of the time, Pallas kernels for 1%

profile of v10, /device:TPU:0, one launch (start us, length us, event | category | flops | bytes accessed | tf_op | source)
XLA Modules:
  0.0 27.1 jit_solution(1993739552021133901)
XLA Ops:
  0.7 1.0 %bands.1 = (f32[4,184,128]{2,1,0:T(8,128)S(1)}, f32[64,128]{1,0:T(8,128)S(1)}, f32[64,128]{1,0:T(8,128)S(1)}) custom-call(s32[1,1]{1,0:T(1,128)S(6)} %copy.5.wet, f32[2,128,128]{2,1,0:T(8,128)} %right_side.1, f32[128,128]{1,0:T(8,128)} %shift_coef.1, f32[128,128]{1,0:T(8,128)} %viscosity.1), custom_call_target="tpu_custom_call" | custom-call | tf_op jit(solution)/shard_map/bands/pallas_call | solution.py:887
  1.6 0.5 %collective-permute-start = (f32[64,128]{1,0:T(8,128)S(1)}, f32[64,128]{1,0:T(8,128)S(1)}, u32[]{:S(2)}, u32[]{:S(2)}) collective-permute-start(f32[64,128]{1,0:T(8,128)S(1)} %get-tuple-element.15), channel_id=1, source_target_pairs={{0,1},{1,0},{2,3},{3,2},{4,5},{5,4},{6,7},{7,6},{8,16},{9,17},{10,... | collective-permute-start | bytes 98312 | tf_op jit(solution)/shard_map/ppermute | solution.py:902
  2.2 4.1 %collective-permute-start.1 = (f32[64,128]{1,0:T(8,128)S(1)}, f32[64,128]{1,0:T(8,128)S(1)}, u32[]{:S(2)}, u32[]{:S(2)}) collective-permute-start(f32[64,128]{1,0:T(8,128)S(1)} %get-tuple-element.16), channel_id=1, source_target_pairs={{0,8},{1,9},{2,10},{3,11},{4,12},{5,13},{6,14},{7,15},{8,0},{9,1},... | collective-permute-start | bytes 98312 | tf_op jit(solution)/shard_map/ppermute | solution.py:903
  6.3 0.0 collective-permute-done.got_second
  6.3 1.9 %collective-permute-done.1.got_first = f32[64,128]{1,0:T(8,128)S(1)} collective-permute-done((f32[64,128]{1,0:T(8,128)S(1)}, f32[64,128]{1,0:T(8,128)S(1)}, u32[]{:S(2)}, u32[]{:S(2)}) %collective-permute-start.1) | collective-permute-done | bytes 32800 | tf_op jit(solution)/shard_map/ppermute | solution.py:903
  8.2 0.2 strips.1
  8.4 2.1 %collective-permute-start.2 = (f32[80,128]{1,0:T(8,128)S(1)}, f32[80,128]{1,0:T(8,128)S(1)}, u32[]{:S(2)}, u32[]{:S(2)}) collective-permute-start(f32[80,128]{1,0:T(8,128)S(1)} %get-tuple-element.18), channel_id=1, source_target_pairs={{0,8},{1,2},{2,1},{3,4},{4,3},{5,6},{6,5},{7,15},{8,0},{9,10},{10,... | collective-permute-start | bytes 122888 | tf_op jit(solution)/shard_map/ppermute | solution.py:923
  10.4 0.0 collective-permute-start.3
  10.5 0.2 halves.1.held
  10.7 1.7 %collective-permute-done.2.got_second = f32[80,128]{1,0:T(8,128)S(1)} collective-permute-done((f32[80,128]{1,0:T(8,128)S(1)}, f32[80,128]{1,0:T(8,128)S(1)}, u32[]{:S(2)}, u32[]{:S(2)}) %collective-permute-start.2) | collective-permute-done | bytes 40992 | tf_op jit(solution)/shard_map/ppermute | solution.py:923
  12.4 0.0 collective-permute-done.3.got_first
  12.4 1.2 %down.1 = (f32[128,128]{1,0:T(8,128)S(1)}, f32[10,184,128]{2,1,0:T(8,128)S(1)}, f32[10,104,128]{2,1,0:T(8,128)S(1)}, f32[10,64,128]{2,1,0:T(8,128)S(1)}, f32[16,48,128]{2,1,0:T(8,128)S(1)}) custom-call(f32[80,128]{1,0:T(8,128)S(1)} %collective-permute-done.2.got_second, f32[80,128]{1,0:T(8,128)S(1)} %collective-permute-done.3.got_first, ...), custom_call_target="tpu_custom_call" | custom-call | tf_op jit(solution)/shard_map/down/pallas_call | solution.py:929
  13.6 11.4 %all_to_all.11 = f32[32,4,128]{2,1,0:T(4,128)S(1)} all-to-all(f32[32,4,128]{2,1,0:T(4,128)S(1)} %bitcast.3), channel_id=1, replica_groups=mesh['gx'=4,'gy'=8] {'gx','gy'}, dimensions={0} | all-to-all | bytes 131072 | tf_op jit(solution)/shard_map/all_to_all | solution.py:945
  25.1 2.0 %up.1 = f32[2,128,128]{2,1,0:T(8,128)} custom-call(f32[128,128]{1,0:T(8,128)S(1)} %bitcast.2, f32[10,184,128]{2,1,0:T(8,128)S(1)} %get-tuple-element.21.state0, f32[10,104,128]{2,1,0:T(8,128)S(1)} %get-tuple-element.22.state1, f32[10,64,128]{2,1,0:T(8,128)S(1)} %get-tuple-element.23.state2, f32[16,48,128]{2,1,0:T(8,128)S(1)} %get-tuple-element.24.state3), custom_call_target="tpu_custom_call" | custom-call | tf_op jit(solution)/shard_map/up/pallas_call | solution.py:948
Async XLA Ops:
  1.6 4.7 %collective-permute-start = (f32[64,128]{1,0:T(8,128)S(1)}, f32[64,128]{1,0:T(8,128)S(1)}, u32[]{:S(2)}, u32[]{:S(2)}) collective-permute-start(f32[64,128]{1,0:T(8,128)S(1)} %get-tuple-element.15), channel_id=1, source_target_pairs={{0,1},{1,0},{2,3},{3,2},{4,5},{5,4},{6,7},{7,6},{8,16},{9,17},{10,... | collective-permute-start | bytes 98312 | tf_op jit(solution)/shard_map/ppermute | solution.py:902
  2.2 6.0 %collective-permute-start.1 = (f32[64,128]{1,0:T(8,128)S(1)}, f32[64,128]{1,0:T(8,128)S(1)}, u32[]{:S(2)}, u32[]{:S(2)}) collective-permute-start(f32[64,128]{1,0:T(8,128)S(1)} %get-tuple-element.16), channel_id=1, source_target_pairs={{0,8},{1,9},{2,10},{3,11},{4,12},{5,13},{6,14},{7,15},{8,0},{9,1},... | collective-permute-start | bytes 98312 | tf_op jit(solution)/shard_map/ppermute | solution.py:903
  8.4 4.1 %collective-permute-start.2 = (f32[80,128]{1,0:T(8,128)S(1)}, f32[80,128]{1,0:T(8,128)S(1)}, u32[]{:S(2)}, u32[]{:S(2)}) collective-permute-start(f32[80,128]{1,0:T(8,128)S(1)} %get-tuple-element.18), channel_id=1, source_target_pairs={{0,8},{1,2},{2,1},{3,4},{4,3},{5,6},{6,5},{7,15},{8,0},{9,10},{10,... | collective-permute-start | bytes 122888 | tf_op jit(solution)/shard_map/ppermute | solution.py:923
  10.4 2.0 %collective-permute-start.3 = (f32[80,128]{1,0:T(8,128)S(1)}, f32[80,128]{1,0:T(8,128)S(1)}, u32[]{:S(2)}, u32[]{:S(2)}) collective-permute-start(f32[80,128]{1,0:T(8,128)S(1)} %get-tuple-element.19), channel_id=1, source_target_pairs={{0,1},{1,0},{2,3},{3,2},{4,5},{5,4},{6,7},{7,6},{8,9},{9,8},{10,11... | collective-permute-start | bytes 122888 | tf_op jit(solution)/shard_map/ppermute | solution.py:924

commit v11 on v10

--- a/solution.py
+++ b/solution.py
@@ -52,24 +52,35 @@
     return ref[slot, row : row + SUB, :]
 
 
-def bands_kernel(wet, right_side, shift_coef, viscosity, held, first, second, sems):
+def bands_kernel(wet, right_side, shift_coef, viscosity, first, second, sems):
     odd = lax.axis_index("gx") % 2
     wetness = wet[0, 0].astype(F32)
-    own = pl.ds(TOP, LANES)
-    sources = (right_side.at[0], right_side.at[1], shift_coef, viscosity)
-    copies = [
-        pltpu.make_async_copy(sources[field], held.at[field, own, :], sems.at[field])
-        for field in range(4)
-    ]
+    bottom = LANES - HALO
+    copies = []
+    for slot, (start, out) in enumerate(((bottom - bottom * odd, first), (bottom * odd, second))):
+        rows = pl.ds(pl.multiple_of(start, SUB), HALO)
+        for kind, (source, target) in enumerate(
+            (
+                (right_side.at[:, rows, :], out.at[0:2]),
+                (shift_coef.at[rows, :], out.at[2]),
+                (viscosity.at[rows, :], out.at[3]),
+            )
+        ):
+            copies.append(pltpu.make_async_copy(source, target, sems.at[3 * slot + kind]))
     for copy in copies:
         copy.start()
-    bottom = LANES - HALO
-    starts = (TOP + bottom - bottom * odd, TOP + bottom * odd)
-    for field in range(4):
-        copies[field].wait()
-        for start, out in zip(starts, (first, second)):
-            value = held[field, pl.ds(pl.multiple_of(start, SUB), HALO), :]
-            out[field * HALO : (field + 1) * HALO, :] = value if field == 2 else value * wetness
+    for copy in copies:
+        copy.wait()
+    for out in (first, second):
+        for field in (0, 1, 3):
+            out[field] = out[field] * wetness
+
+
+def own_rows(right_side, shift_coef, viscosity, field, tile):
+    rows = slice(SUB * tile, SUB * tile + SUB)
+    if field < 2:
+        return right_side[field, rows, :]
+    return shift_coef[rows, :] if field == 2 else viscosity[rows, :]
 
 
 def rim_place(half, lane):
@@ -79,7 +90,9 @@
     return to_left, q >> 1, cell
 
 
-def strips_kernel(size_x, wet, got_second, got_first, held, first, second):
+def strips_kernel(
+    size_x, wet, got_second, got_first, right_side, shift_coef, viscosity, first, second
+):
     index_x = lax.axis_index("gx")
     odd_x = index_x % 2 == 1
     odd_y = lax.axis_index("gy") % 2 == 1
@@ -91,11 +104,10 @@
 
     def piece(field, tile):
         if rim_tiles <= tile < TILES[0] - rim_tiles:
-            row = GUARD + SUB * tile
-            return held[field, row : row + SUB, :]
+            return own_rows(right_side, shift_coef, viscosity, field, tile - rim_tiles)
         top = tile < rim_tiles
-        row = field * HALO + SUB * (tile if top else tile - (TILES[0] - rim_tiles))
-        one, two = got_first[row : row + SUB, :], got_second[row : row + SUB, :]
+        row = SUB * (tile if top else tile - (TILES[0] - rim_tiles))
+        one, two = tile_at(got_first, field, row), tile_at(got_second, field, row)
         return jnp.where(odd_x, one, two) if top else jnp.where(odd_x, two, one)
 
     places = [rim_place(half, lane) for half in range(2)]
@@ -121,7 +133,9 @@
         second[rows, :] = jnp.where(odd_y, right, left)
 
 
-def halves_kernel(size_x, wet, got_second, got_first, held, fields):
+def halves_kernel(
+    size_x, wet, got_second, got_first, right_side, shift_coef, viscosity, fields
+):
     index_x = lax.axis_index("gx")
     odd_x = index_x % 2 == 1
     wetness = wet[0, 0].astype(F32)
@@ -133,13 +147,13 @@
         row = GUARD + SUB * tile
         for field in range(4):
             if rim_tiles <= tile < TILES[0] - rim_tiles:
-                value = held[field, row : row + SUB, :]
+                value = own_rows(right_side, shift_coef, viscosity, field, tile - rim_tiles)
                 if field != 2:
                     value = value * wetness
             else:
                 top = tile < rim_tiles
-                at = field * HALO + SUB * (tile if top else tile - (TILES[0] - rim_tiles))
-                one, two = got_first[at : at + SUB, :], got_second[at : at + SUB, :]
+                at = SUB * (tile if top else tile - (TILES[0] - rim_tiles))
+                one, two = tile_at(got_first, field, at), tile_at(got_second, field, at)
                 value = jnp.where(odd_x, one, two) if top else jnp.where(odd_x, two, one)
                 if field == 3:
                     value = value * (above if top else below)
@@ -882,23 +896,17 @@
     axes = ("gx", "gy")
     devices = size_x * size_y
     routes = swap_routes(size_x, size_y)
-    band = jax.ShapeDtypeStruct((4 * HALO, LANES), F32)
-    held_shape = pltpu.VMEM((4, HELD[0], LANES), F32)
-    held, first, second = pl.pallas_call(
+    band = pltpu.VMEM((4, HALO, LANES), F32)
+    own = (right_side, shift_coef, viscosity)
+    first, second = pl.pallas_call(
         bands_kernel,
-        out_shape=(held_shape, band, band),
+        out_shape=(band, band),
         in_specs=[SMEM_SPEC] + [HBM_SPEC] * 3,
-        out_specs=(VMEM_SPEC,) * 3,
-        scratch_shapes=[pltpu.SemaphoreType.DMA((4,))],
+        out_specs=(VMEM_SPEC,) * 2,
+        scratch_shapes=[pltpu.SemaphoreType.DMA((6,))],
         compiler_params=params(),
         name="bands",
-    )(
-        wet_tiles,
-        *[
-            pltpu.with_memory_space_constraint(array, pltpu.HBM)
-            for array in (right_side, shift_coef, viscosity)
-        ],
-    )
+    )(wet_tiles, *[pltpu.with_memory_space_constraint(array, pltpu.HBM) for array in own])
     second = lax.ppermute(second, axes, routes[1])
     first = lax.ppermute(first, axes, routes[0])
     strip = jax.ShapeDtypeStruct((MESSAGE, LANES), F32)
@@ -906,20 +914,20 @@
     first, second = pl.pallas_call(
         functools.partial(strips_kernel, size_x),
         out_shape=(strip, strip),
-        in_specs=[SMEM_SPEC] + [VMEM_SPEC] * 3,
+        in_specs=[SMEM_SPEC] + [VMEM_SPEC] * 5,
         out_specs=(VMEM_SPEC,) * 2,
         compiler_params=params(),
         name="strips",
-    )(wet_tiles, *got, held)
+    )(wet_tiles, *got, *own)
     fields = pl.pallas_call(
         functools.partial(halves_kernel, size_x),
         out_shape=pltpu.VMEM((8, HELD[0], LANES), F32),
-        in_specs=[SMEM_SPEC] + [VMEM_SPEC] * 3,
+        in_specs=[SMEM_SPEC] + [VMEM_SPEC] * 5,
         out_specs=VMEM_SPEC,
         cost_estimate=pl.CostEstimate(flops=1 << 20, bytes_accessed=1 << 21, transcendentals=0),
         compiler_params=params(),
         name="halves",
-    )(wet_tiles, *got, held)
+    )(wet_tiles, *got, *own)
     second = lax.ppermute(second, axes, routes[3])
     first = lax.ppermute(first, axes, routes[2])
 

time: 27.2 us -> 27.3 us (level)
  no operation moved by 1% of the time
where the time goes in v11:
time: 27.3 us; the launch traced here: 27 us
  blocking collectives  11.4 us (42%)
  starting transfers between devices  6.76 us (25%)
  Pallas kernels  4.5 us (16%)
  waiting for transfers between devices  3.63 us (13%)
  between operations  0.71 us (3%)
    all_to_all x1, blocking collectives, per_device(): gathered = lax.all_to_all(chunks, axes, 0, 0, tiled=True)  11.4 us
    ppermute x1, starting transfers between devices, per_device(): first = lax.ppermute(first, axes, routes[0])  4.15 us
    ppermute x1, starting transfers between devices, per_device(): second = lax.ppermute(second, axes, routes[3])  2.09 us
    pallas_call x1, Pallas kernels, per_device(): pl.pallas_call(functools.partial(up_kernel, size_x, size_y), out_shape=ja...  2 us
    ppermute x1, waiting for transfers between devices, per_device(): first = lax.ppermute(first, axes, routes[0])  1.89 us
    ppermute x1, waiting for transfers between devices, per_device(): second = lax.ppermute(second, axes, routes[3])  1.73 us
    pallas_call x1, Pallas kernels, per_device(): pl.pallas_call(functools.partial(down_kernel, size_y, devices), out_shape...  1.17 us
    pallas_call x1, Pallas kernels, per_device(): pl.pallas_call(bands_kernel, out_shape=(band, band), in_specs=[SMEM_SPEC]...  0.92 us
  transfers between devices with their start and end apart: 4, of which 2 were waited for; matrix products, arithmetic and copies ran while one was open for 0% of the time, Pallas kernels for 1%

profile of v11, /device:TPU:0, one launch (start us, length us, event | category | flops | bytes accessed | tf_op | source)
XLA Modules:
  0.0 27.0 jit_solution(11452048281340965034)
XLA Ops:
  0.7 0.0 copy-start
  0.7 0.0 copy-start.1
  0.7 0.0 copy-start.2
  0.7 0.9 %bands.1 = (f32[4,16,128]{2,1,0:T(8,128)S(1)}, f32[4,16,128]{2,1,0:T(8,128)S(1)}) custom-call(s32[1,1]{1,0:T(1,128)S(6)} %copy.5.wet, f32[2,128,128]{2,1,0:T(8,128)} %right_side.5, f32[128,128]{1,0:T(8,128)} %shift_coef.5, f32[128,128]{1,0:T(8,128)} %viscosity.5), custom_call_target="tpu_custom_call" | custom-call | tf_op jit(solution)/shard_map/bands/pallas_call | solution.py:901
  1.6 0.5 %collective-permute-start = (f32[4,16,128]{2,1,0:T(8,128)S(1)}, f32[4,16,128]{2,1,0:T(8,128)S(1)}, u32[]{:S(2)}, u32[]{:S(2)}) collective-permute-start(f32[4,16,128]{2,1,0:T(8,128)S(1)} %get-tuple-element.14), channel_id=1, source_target_pairs={{0,1},{1,0},{2,3},{3,2},{4,5},{5,4},{6,7},{7,6},{8,16},{9,17},{10,... | collective-permute-start | bytes 98312 | tf_op jit(solution)/shard_map/ppermute | solution.py:910
  2.1 4.1 %collective-permute-start.1 = (f32[4,16,128]{2,1,0:T(8,128)S(1)}, f32[4,16,128]{2,1,0:T(8,128)S(1)}, u32[]{:S(2)}, u32[]{:S(2)}) collective-permute-start(f32[4,16,128]{2,1,0:T(8,128)S(1)} %get-tuple-element.15), channel_id=1, source_target_pairs={{0,8},{1,9},{2,10},{3,11},{4,12},{5,13},{6,14},{7,15},{8,0},{9,1},... | collective-permute-start | bytes 98312 | tf_op jit(solution)/shard_map/ppermute | solution.py:911
  6.3 0.0 collective-permute-done.got_second
  6.3 1.9 %collective-permute-done.1.got_first = f32[4,16,128]{2,1,0:T(8,128)S(1)} collective-permute-done((f32[4,16,128]{2,1,0:T(8,128)S(1)}, f32[4,16,128]{2,1,0:T(8,128)S(1)}, u32[]{:S(2)}, u32[]{:S(2)}) %collective-permute-start.1) | collective-permute-done | bytes 32800 | tf_op jit(solution)/shard_map/ppermute | solution.py:911
  8.2 0.0 copy-done
  8.2 0.0 copy-done.1
  8.2 0.0 copy-done.2
  8.2 0.2 strips.1
  8.3 2.1 %collective-permute-start.2 = (f32[80,128]{1,0:T(8,128)S(1)}, f32[80,128]{1,0:T(8,128)S(1)}, u32[]{:S(2)}, u32[]{:S(2)}) collective-permute-start(f32[80,128]{1,0:T(8,128)S(1)} %get-tuple-element.16), channel_id=1, source_target_pairs={{0,8},{1,2},{2,1},{3,4},{4,3},{5,6},{6,5},{7,15},{8,0},{9,10},{10,... | collective-permute-start | bytes 122888 | tf_op jit(solution)/shard_map/ppermute | solution.py:931
  10.4 0.0 collective-permute-start.3
  10.4 0.2 halves.1.held
  10.7 1.7 %collective-permute-done.2.got_second = f32[80,128]{1,0:T(8,128)S(1)} collective-permute-done((f32[80,128]{1,0:T(8,128)S(1)}, f32[80,128]{1,0:T(8,128)S(1)}, u32[]{:S(2)}, u32[]{:S(2)}) %collective-permute-start.2) | collective-permute-done | bytes 40992 | tf_op jit(solution)/shard_map/ppermute | solution.py:931
  12.4 0.0 collective-permute-done.3.got_first
  12.4 1.2 %down.1 = (f32[128,128]{1,0:T(8,128)S(1)}, f32[10,184,128]{2,1,0:T(8,128)S(1)}, f32[10,104,128]{2,1,0:T(8,128)S(1)}, f32[10,64,128]{2,1,0:T(8,128)S(1)}, f32[16,48,128]{2,1,0:T(8,128)S(1)}) custom-call(f32[80,128]{1,0:T(8,128)S(1)} %collective-permute-done.2.got_second, f32[80,128]{1,0:T(8,128)S(1)} %collective-permute-done.3.got_first, ...), custom_call_target="tpu_custom_call" | custom-call | tf_op jit(solution)/shard_map/down/pallas_call | solution.py:937
  13.6 11.4 %all_to_all.11 = f32[32,4,128]{2,1,0:T(4,128)S(1)} all-to-all(f32[32,4,128]{2,1,0:T(4,128)S(1)} %bitcast.3), channel_id=1, replica_groups=mesh['gx'=4,'gy'=8] {'gx','gy'}, dimensions={0} | all-to-all | bytes 131072 | tf_op jit(solution)/shard_map/all_to_all | solution.py:953
  25.0 2.0 %up.1 = f32[2,128,128]{2,1,0:T(8,128)} custom-call(f32[128,128]{1,0:T(8,128)S(1)} %bitcast.2, f32[10,184,128]{2,1,0:T(8,128)S(1)} %get-tuple-element.19.state0, f32[10,104,128]{2,1,0:T(8,128)S(1)} %get-tuple-element.20.state1, f32[10,64,128]{2,1,0:T(8,128)S(1)} %get-tuple-element.21.state2, f32[16,48,128]{2,1,0:T(8,128)S(1)} %get-tuple-element.22.state3), custom_call_target="tpu_custom_call" | custom-call | tf_op jit(solution)/shard_map/up/pallas_call | solution.py:956
Async XLA Ops:
  0.7 7.5 %copy-start = (f32[2,128,128]{2,1,0:T(8,128)S(1)}, f32[2,128,128]{2,1,0:T(8,128)}, u32[]{:S(2)}) copy-start(f32[2,128,128]{2,1,0:T(8,128)} %right_side.5) | copy-start | bytes 393220
  0.7 7.5 %copy-start.1 = (f32[128,128]{1,0:T(8,128)S(1)}, f32[128,128]{1,0:T(8,128)}, u32[]{:S(2)}) copy-start(f32[128,128]{1,0:T(8,128)} %shift_coef.5) | copy-start | bytes 196612
  0.7 7.5 %copy-start.2 = (f32[128,128]{1,0:T(8,128)S(1)}, f32[128,128]{1,0:T(8,128)}, u32[]{:S(2)}) copy-start(f32[128,128]{1,0:T(8,128)} %viscosity.5) | copy-start | bytes 196612
  1.6 4.7 %collective-permute-start = (f32[4,16,128]{2,1,0:T(8,128)S(1)}, f32[4,16,128]{2,1,0:T(8,128)S(1)}, u32[]{:S(2)}, u32[]{:S(2)}) collective-permute-start(f32[4,16,128]{2,1,0:T(8,128)S(1)} %get-tuple-element.14), channel_id=1, source_target_pairs={{0,1},{1,0},{2,3},{3,2},{4,5},{5,4},{6,7},{7,6},{8,16},{9,17},{10,... | collective-permute-start | bytes 98312 | tf_op jit(solution)/shard_map/ppermute | solution.py:910
  2.1 6.0 %collective-permute-start.1 = (f32[4,16,128]{2,1,0:T(8,128)S(1)}, f32[4,16,128]{2,1,0:T(8,128)S(1)}, u32[]{:S(2)}, u32[]{:S(2)}) collective-permute-start(f32[4,16,128]{2,1,0:T(8,128)S(1)} %get-tuple-element.15), channel_id=1, source_target_pairs={{0,8},{1,9},{2,10},{3,11},{4,12},{5,13},{6,14},{7,15},{8,0},{9,1},... | collective-permute-start | bytes 98312 | tf_op jit(solution)/shard_map/ppermute | solution.py:911
  8.3 4.1 %collective-permute-start.2 = (f32[80,128]{1,0:T(8,128)S(1)}, f32[80,128]{1,0:T(8,128)S(1)}, u32[]{:S(2)}, u32[]{:S(2)}) collective-permute-start(f32[80,128]{1,0:T(8,128)S(1)} %get-tuple-element.16), channel_id=1, source_target_pairs={{0,8},{1,2},{2,1},{3,4},{4,3},{5,6},{6,5},{7,15},{8,0},{9,10},{10,... | collective-permute-start | bytes 122888 | tf_op jit(solution)/shard_map/ppermute | solution.py:931
  10.4 2.0 %collective-permute-start.3 = (f32[80,128]{1,0:T(8,128)S(1)}, f32[80,128]{1,0:T(8,128)S(1)}, u32[]{:S(2)}, u32[]{:S(2)}) collective-permute-start(f32[80,128]{1,0:T(8,128)S(1)} %get-tuple-element.17), channel_id=1, source_target_pairs={{0,1},{1,0},{2,3},{3,2},{4,5},{5,4},{6,7},{7,6},{8,9},{9,8},{10,11... | collective-permute-start | bytes 122888 | tf_op jit(solution)/shard_map/ppermute | solution.py:932

commit v12 on v11

--- a/solution.py
+++ b/solution.py
@@ -28,6 +28,7 @@
 HALF_TILES = TILES[0] // 2
 MESSAGE = ROWS[0] // 2
 CHUNK = 4
+PIECES = (4, 8)
 F32 = jnp.float32
 VMEM_LIMIT = 48 * 1024 * 1024
 
@@ -693,7 +694,8 @@
 
 
 def up_kernel(size_x, size_y, gathered, state0, state1, state2, state3, out, *refs):
-    grid, buffer, whole, window, swept3, corr1, corr2, corr3, merged0, merged1, merged2 = refs
+    grid, buffer, whole, window, swept3, corr1, corr2, corr3, merged0, merged1, merged2 = refs[:11]
+    finished, sems = refs[11:]
     index_x, index_y = lax.axis_index("gx"), lax.axis_index("gy")
     rows_total, cols_total = CELLS * size_x, CELLS * size_y
     width = 2 * cols_total
@@ -838,6 +840,7 @@
             first, tiles = -1, -(-count // SUB)
         else:
             first, tiles = 0, (count - 2) // SUB
+        copies = []
         for tile in range(tiles):
             coarse_row = first + SUB * tile
             at = origin + coarse_row
@@ -854,11 +857,22 @@
                             corrs[level][2 * comp + p, rows, :] = found[p]
                     else:
                         rows = pl.ds(2 * coarse_row + parity, SUB, stride=2)
-                        out[comp, rows, :] = jnp.where(
+                        finished[comp, rows, :] = jnp.where(
                             odd_lane,
                             lane_take(found[1], lane >> 1),
                             lane_take(found[0], lane >> 1),
                         )
+            if level == 0 and tile + 1 in PIECES:
+                piece = len(copies)
+                begin = 2 * SUB * PIECES[piece - 1] if piece else 0
+                rows = pl.ds(begin, 2 * SUB * (tile + 1) - begin)
+                copy = pltpu.make_async_copy(
+                    finished.at[:, rows, :], out.at[:, rows, :], sems.at[piece]
+                )
+                copy.start()
+                copies.append(copy)
+        for copy in copies:
+            copy.wait()
 
 
 def params():
@@ -957,7 +971,7 @@
         functools.partial(up_kernel, size_x, size_y),
         out_shape=jax.ShapeDtypeStruct((2, LANES, LANES), F32),
         in_specs=[VMEM_SPEC] * (1 + LOCAL),
-        out_specs=VMEM_SPEC,
+        out_specs=HBM_SPEC,
         scratch_shapes=[
             pltpu.VMEM((3, width // LANES, rows_total, LANES), F32),
             pltpu.VMEM((6, width // LANES, rows_total + 3 * SUB, LANES), F32),
@@ -966,7 +980,8 @@
             pltpu.VMEM((4, HELD[3], LANES), F32),
         ]
         + [pltpu.VMEM((4, HELD[level], LANES), F32) for level in (1, 2, 3)]
-        + [pltpu.VMEM((6, HELD[level + 1], LANES), F32) for level in (0, 1, 2)],
+        + [pltpu.VMEM((6, HELD[level + 1], LANES), F32) for level in (0, 1, 2)]
+        + [pltpu.VMEM((2, LANES, LANES), F32), pltpu.SemaphoreType.DMA((len(PIECES),))],
         compiler_params=params(),
         name="up",
     )(gathered, *states)

time: 27.3 us -> 27.3 us (level)
  no operation moved by 1% of the time
where the time goes in v12:
time: 27.3 us; the launch traced here: 27 us
  blocking collectives  11.4 us (42%)
  starting transfers between devices  6.76 us (25%)
  Pallas kernels  4.49 us (16%)
  waiting for transfers between devices  3.63 us (13%)
  between operations  0.71 us (3%)
    all_to_all x1, blocking collectives, per_device(): gathered = lax.all_to_all(chunks, axes, 0, 0, tiled=True)  11.4 us
    ppermute x1, starting transfers between devices, per_device(): first = lax.ppermute(first, axes, routes[0])  4.15 us
    ppermute x1, starting transfers between devices, per_device(): second = lax.ppermute(second, axes, routes[3])  2.09 us
    pallas_call x1, Pallas kernels, per_device(): pl.pallas_call(functools.partial(up_kernel, size_x, size_y), out_shape=ja...  2 us
    ppermute x1, waiting for transfers between devices, per_device(): first = lax.ppermute(first, axes, routes[0])  1.89 us
    ppermute x1, waiting for transfers between devices, per_device(): second = lax.ppermute(second, axes, routes[3])  1.73 us
    pallas_call x1, Pallas kernels, per_device(): pl.pallas_call(functools.partial(down_kernel, size_y, devices), out_shape...  1.17 us
    pallas_call x1, Pallas kernels, per_device(): pl.pallas_call(bands_kernel, out_shape=(band, band), in_specs=[SMEM_SPEC]...  0.92 us
  transfers between devices with their start and end apart: 4, of which 2 were waited for; matrix products, arithmetic and copies ran while one was open for 0% of the time, Pallas kernels for 1%

profile of v12, /device:TPU:0, one launch (start us, length us, event | category | flops | bytes accessed | tf_op | source)
XLA Modules:
  0.0 27.0 jit_solution(16379418370657864009)
XLA Ops:
  0.7 0.0 copy-start
  0.7 0.0 copy-start.1
  0.7 0.0 copy-start.2
  0.7 0.9 %bands.1 = (f32[4,16,128]{2,1,0:T(8,128)S(1)}, f32[4,16,128]{2,1,0:T(8,128)S(1)}) custom-call(s32[1,1]{1,0:T(1,128)S(6)} %copy.5.wet, f32[2,128,128]{2,1,0:T(8,128)} %right_side.5, f32[128,128]{1,0:T(8,128)} %shift_coef.5, f32[128,128]{1,0:T(8,128)} %viscosity.5), custom_call_target="tpu_custom_call" | custom-call | tf_op jit(solution)/shard_map/bands/pallas_call | solution.py:915
  1.6 0.5 %collective-permute-start = (f32[4,16,128]{2,1,0:T(8,128)S(1)}, f32[4,16,128]{2,1,0:T(8,128)S(1)}, u32[]{:S(2)}, u32[]{:S(2)}) collective-permute-start(f32[4,16,128]{2,1,0:T(8,128)S(1)} %get-tuple-element.14), channel_id=1, source_target_pairs={{0,1},{1,0},{2,3},{3,2},{4,5},{5,4},{6,7},{7,6},{8,16},{9,17},{10,... | collective-permute-start | bytes 98312 | tf_op jit(solution)/shard_map/ppermute | solution.py:924
  2.1 4.1 %collective-permute-start.1 = (f32[4,16,128]{2,1,0:T(8,128)S(1)}, f32[4,16,128]{2,1,0:T(8,128)S(1)}, u32[]{:S(2)}, u32[]{:S(2)}) collective-permute-start(f32[4,16,128]{2,1,0:T(8,128)S(1)} %get-tuple-element.15), channel_id=1, source_target_pairs={{0,8},{1,9},{2,10},{3,11},{4,12},{5,13},{6,14},{7,15},{8,0},{9,1},... | collective-permute-start | bytes 98312 | tf_op jit(solution)/shard_map/ppermute | solution.py:925
  6.3 0.0 collective-permute-done.got_second
  6.3 1.9 %collective-permute-done.1.got_first = f32[4,16,128]{2,1,0:T(8,128)S(1)} collective-permute-done((f32[4,16,128]{2,1,0:T(8,128)S(1)}, f32[4,16,128]{2,1,0:T(8,128)S(1)}, u32[]{:S(2)}, u32[]{:S(2)}) %collective-permute-start.1) | collective-permute-done | bytes 32800 | tf_op jit(solution)/shard_map/ppermute | solution.py:925
  8.2 0.0 copy-done
  8.2 0.0 copy-done.1
  8.2 0.0 copy-done.2
  8.2 0.2 strips.1
  8.3 2.1 %collective-permute-start.2 = (f32[80,128]{1,0:T(8,128)S(1)}, f32[80,128]{1,0:T(8,128)S(1)}, u32[]{:S(2)}, u32[]{:S(2)}) collective-permute-start(f32[80,128]{1,0:T(8,128)S(1)} %get-tuple-element.16), channel_id=1, source_target_pairs={{0,8},{1,2},{2,1},{3,4},{4,3},{5,6},{6,5},{7,15},{8,0},{9,10},{10,... | collective-permute-start | bytes 122888 | tf_op jit(solution)/shard_map/ppermute | solution.py:945
  10.4 0.0 collective-permute-start.3
  10.4 0.2 halves.1.held
  10.7 1.7 %collective-permute-done.2.got_second = f32[80,128]{1,0:T(8,128)S(1)} collective-permute-done((f32[80,128]{1,0:T(8,128)S(1)}, f32[80,128]{1,0:T(8,128)S(1)}, u32[]{:S(2)}, u32[]{:S(2)}) %collective-permute-start.2) | collective-permute-done | bytes 40992 | tf_op jit(solution)/shard_map/ppermute | solution.py:945
  12.4 0.0 collective-permute-done.3.got_first
  12.4 1.2 %down.1 = (f32[128,128]{1,0:T(8,128)S(1)}, f32[10,184,128]{2,1,0:T(8,128)S(1)}, f32[10,104,128]{2,1,0:T(8,128)S(1)}, f32[10,64,128]{2,1,0:T(8,128)S(1)}, f32[16,48,128]{2,1,0:T(8,128)S(1)}) custom-call(f32[80,128]{1,0:T(8,128)S(1)} %collective-permute-done.2.got_second, f32[80,128]{1,0:T(8,128)S(1)} %collective-permute-done.3.got_first, ...), custom_call_target="tpu_custom_call" | custom-call | tf_op jit(solution)/shard_map/down/pallas_call | solution.py:951
  13.6 11.4 %all_to_all.11 = f32[32,4,128]{2,1,0:T(4,128)S(1)} all-to-all(f32[32,4,128]{2,1,0:T(4,128)S(1)} %bitcast.3), channel_id=1, replica_groups=mesh['gx'=4,'gy'=8] {'gx','gy'}, dimensions={0} | all-to-all | bytes 131072 | tf_op jit(solution)/shard_map/all_to_all | solution.py:967
  25.0 2.0 %up.1 = f32[2,128,128]{2,1,0:T(8,128)} custom-call(f32[128,128]{1,0:T(8,128)S(1)} %bitcast.2, f32[10,184,128]{2,1,0:T(8,128)S(1)} %get-tuple-element.19.state0, f32[10,104,128]{2,1,0:T(8,128)S(1)} %get-tuple-element.20.state1, f32[10,64,128]{2,1,0:T(8,128)S(1)} %get-tuple-element.21.state2, f32[16,48,128]{2,1,0:T(8,128)S(1)} %get-tuple-element.22.state3), custom_call_target="tpu_custom_call" | custom-call | tf_op jit(solution)/shard_map/up/pallas_call | solution.py:970
Async XLA Ops:
  0.7 7.5 %copy-start = (f32[2,128,128]{2,1,0:T(8,128)S(1)}, f32[2,128,128]{2,1,0:T(8,128)}, u32[]{:S(2)}) copy-start(f32[2,128,128]{2,1,0:T(8,128)} %right_side.5) | copy-start | bytes 393220
  0.7 7.5 %copy-start.1 = (f32[128,128]{1,0:T(8,128)S(1)}, f32[128,128]{1,0:T(8,128)}, u32[]{:S(2)}) copy-start(f32[128,128]{1,0:T(8,128)} %shift_coef.5) | copy-start | bytes 196612
  0.7 7.5 %copy-start.2 = (f32[128,128]{1,0:T(8,128)S(1)}, f32[128,128]{1,0:T(8,128)}, u32[]{:S(2)}) copy-start(f32[128,128]{1,0:T(8,128)} %viscosity.5) | copy-start | bytes 196612
  1.6 4.7 %collective-permute-start = (f32[4,16,128]{2,1,0:T(8,128)S(1)}, f32[4,16,128]{2,1,0:T(8,128)S(1)}, u32[]{:S(2)}, u32[]{:S(2)}) collective-permute-start(f32[4,16,128]{2,1,0:T(8,128)S(1)} %get-tuple-element.14), channel_id=1, source_target_pairs={{0,1},{1,0},{2,3},{3,2},{4,5},{5,4},{6,7},{7,6},{8,16},{9,17},{10,... | collective-permute-start | bytes 98312 | tf_op jit(solution)/shard_map/ppermute | solution.py:924
  2.1 6.0 %collective-permute-start.1 = (f32[4,16,128]{2,1,0:T(8,128)S(1)}, f32[4,16,128]{2,1,0:T(8,128)S(1)}, u32[]{:S(2)}, u32[]{:S(2)}) collective-permute-start(f32[4,16,128]{2,1,0:T(8,128)S(1)} %get-tuple-element.15), channel_id=1, source_target_pairs={{0,8},{1,9},{2,10},{3,11},{4,12},{5,13},{6,14},{7,15},{8,0},{9,1},... | collective-permute-start | bytes 98312 | tf_op jit(solution)/shard_map/ppermute | solution.py:925
  8.3 4.1 %collective-permute-start.2 = (f32[80,128]{1,0:T(8,128)S(1)}, f32[80,128]{1,0:T(8,128)S(1)}, u32[]{:S(2)}, u32[]{:S(2)}) collective-permute-start(f32[80,128]{1,0:T(8,128)S(1)} %get-tuple-element.16), channel_id=1, source_target_pairs={{0,8},{1,2},{2,1},{3,4},{4,3},{5,6},{6,5},{7,15},{8,0},{9,10},{10,... | collective-permute-start | bytes 122888 | tf_op jit(solution)/shard_map/ppermute | solution.py:945
  10.4 2.0 %collective-permute-start.3 = (f32[80,128]{1,0:T(8,128)S(1)}, f32[80,128]{1,0:T(8,128)S(1)}, u32[]{:S(2)}, u32[]{:S(2)}) collective-permute-start(f32[80,128]{1,0:T(8,128)S(1)} %get-tuple-element.17), channel_id=1, source_target_pairs={{0,1},{1,0},{2,3},{3,2},{4,5},{5,4},{6,7},{7,6},{8,9},{9,8},{10,11... | collective-permute-start | bytes 122888 | tf_op jit(solution)/shard_map/ppermute | solution.py:946

commit v13 on v12

--- a/solution.py
+++ b/solution.py
@@ -53,9 +53,8 @@
     return ref[slot, row : row + SUB, :]
 
 
-def bands_kernel(wet, right_side, shift_coef, viscosity, first, second, sems):
+def bands_kernel(right_side, shift_coef, viscosity, first, second, sems):
     odd = lax.axis_index("gx") % 2
-    wetness = wet[0, 0].astype(F32)
     bottom = LANES - HALO
     copies = []
     for slot, (start, out) in enumerate(((bottom - bottom * odd, first), (bottom * odd, second))):
@@ -72,9 +71,6 @@
         copy.start()
     for copy in copies:
         copy.wait()
-    for out in (first, second):
-        for field in (0, 1, 3):
-            out[field] = out[field] * wetness
 
 
 def own_rows(right_side, shift_coef, viscosity, field, tile):
@@ -92,14 +88,26 @@
 
 
 def strips_kernel(
-    size_x, wet, got_second, got_first, right_side, shift_coef, viscosity, first, second
+    size_x,
+    wet,
+    got_second,
+    got_first,
+    wet_second,
+    wet_first,
+    right_side,
+    shift_coef,
+    viscosity,
+    first,
+    second,
 ):
     index_x = lax.axis_index("gx")
     odd_x = index_x % 2 == 1
     odd_y = lax.axis_index("gy") % 2 == 1
-    wetness = wet[0, 0].astype(F32)
-    above = (index_x > 0).astype(F32)
-    below = (index_x < size_x - 1).astype(F32)
+    wetness = wet[...]
+    wet_above = jnp.where(odd_x, wet_first[...], wet_second[...])
+    wet_below = jnp.where(odd_x, wet_second[...], wet_first[...])
+    above = wet_above * (index_x > 0).astype(F32)
+    below = wet_below * (index_x < size_x - 1).astype(F32)
     lane = iota(1)
     rim_tiles = HALO // SUB
 
@@ -124,7 +132,10 @@
             if rim_tiles <= at < TILES[0] - rim_tiles:
                 value = value * jnp.where(owner == 2, 1.0, wetness)
             else:
-                value = value * jnp.where(owner == 3, above if at < rim_tiles else below, 1.0)
+                flags = (wet_above, above) if at < rim_tiles else (wet_below, below)
+                value = value * jnp.where(
+                    owner == 2, 1.0, jnp.where(owner == 3, flags[1], flags[0])
+                )
             found[half, tile] = value
     for tile in range(HALF_TILES):
         left = jnp.where(places[0][0], found[0, tile], found[1, tile])
@@ -135,13 +146,24 @@
 
 
 def halves_kernel(
-    size_x, wet, got_second, got_first, right_side, shift_coef, viscosity, fields
+    size_x,
+    wet,
+    got_second,
+    got_first,
+    wet_second,
+    wet_first,
+    right_side,
+    shift_coef,
+    viscosity,
+    fields,
 ):
     index_x = lax.axis_index("gx")
     odd_x = index_x % 2 == 1
-    wetness = wet[0, 0].astype(F32)
-    above = (index_x > 0).astype(F32)
-    below = (index_x < size_x - 1).astype(F32)
+    wetness = wet[...]
+    wet_above = jnp.where(odd_x, wet_first[...], wet_second[...])
+    wet_below = jnp.where(odd_x, wet_second[...], wet_first[...])
+    above = wet_above * (index_x > 0).astype(F32)
+    below = wet_below * (index_x < size_x - 1).astype(F32)
     lane = iota(1)
     rim_tiles = HALO // SUB
     for tile in range(TILES[0]):
@@ -158,6 +180,8 @@
                 value = jnp.where(odd_x, one, two) if top else jnp.where(odd_x, two, one)
                 if field == 3:
                     value = value * (above if top else below)
+                elif field < 2:
+                    value = value * (wet_above if top else wet_below)
             for parity in range(2):
                 fields[2 * field + parity, row : row + SUB, :] = lane_take(
                     value, (2 * lane + parity) & (LANES - 1)
@@ -880,7 +904,6 @@
 
 
 VMEM_SPEC = pl.BlockSpec(memory_space=pltpu.VMEM)
-SMEM_SPEC = pl.BlockSpec(memory_space=pltpu.SMEM)
 HBM_SPEC = pl.BlockSpec(memory_space=pltpu.HBM)
 
 
@@ -915,33 +938,37 @@
     first, second = pl.pallas_call(
         bands_kernel,
         out_shape=(band, band),
-        in_specs=[SMEM_SPEC] + [HBM_SPEC] * 3,
+        in_specs=[HBM_SPEC] * 3,
         out_specs=(VMEM_SPEC,) * 2,
         scratch_shapes=[pltpu.SemaphoreType.DMA((6,))],
         compiler_params=params(),
         name="bands",
-    )(wet_tiles, *[pltpu.with_memory_space_constraint(array, pltpu.HBM) for array in own])
+    )(*[pltpu.with_memory_space_constraint(array, pltpu.HBM) for array in own])
+    flag, _ = lax.optimization_barrier((wet_tiles, first))
+    wet = jnp.broadcast_to(flag.astype(F32), (SUB, LANES))
     second = lax.ppermute(second, axes, routes[1])
     first = lax.ppermute(first, axes, routes[0])
+    wet_second = lax.ppermute(wet, axes, routes[1])
+    wet_first = lax.ppermute(wet, axes, routes[0])
     strip = jax.ShapeDtypeStruct((MESSAGE, LANES), F32)
-    got = (second, first)
+    got = (second, first, wet_second, wet_first)
     first, second = pl.pallas_call(
         functools.partial(strips_kernel, size_x),
         out_shape=(strip, strip),
-        in_specs=[SMEM_SPEC] + [VMEM_SPEC] * 5,
+        in_specs=[VMEM_SPEC] * 8,
         out_specs=(VMEM_SPEC,) * 2,
         compiler_params=params(),
         name="strips",
-    )(wet_tiles, *got, *own)
+    )(wet, *got, *own)
     fields = pl.pallas_call(
         functools.partial(halves_kernel, size_x),
         out_shape=pltpu.VMEM((8, HELD[0], LANES), F32),
-        in_specs=[SMEM_SPEC] + [VMEM_SPEC] * 5,
+        in_specs=[VMEM_SPEC] * 8,
         out_specs=VMEM_SPEC,
         cost_estimate=pl.CostEstimate(flops=1 << 20, bytes_accessed=1 << 21, transcendentals=0),
         compiler_params=params(),
         name="halves",
-    )(wet_tiles, *got, *own)
+    )(wet, *got, *own)
     second = lax.ppermute(second, axes, routes[3])
     first = lax.ppermute(first, axes, routes[2])
 

time: 27.3 us -> 28.5 us (1.044)
  waiting for transfers between devices: 3.63 us -> 5.26 us
  blocking collectives: 11.4 us -> 10.9 us
    ppermute x0 -> x2, waiting for transfers between devices: none -> 3.52 us  [the longest x1 3.51 us: per_device(): wet_first = lax.ppermute(wet, axes, routes[0])]
    ppermute x1, waiting for transfers between devices: 1.89 us -> 0.01 us  [per_device(): first = lax.ppermute(first, axes, routes[0])]
    all_to_all x1, blocking collectives: 11.4 us -> 10.9 us  [per_device(): gathered = lax.all_to_all(chunks, axes, 0, 0, tiled=True)]
  transfers between devices with their start and end apart: 4 -> 6, of which waited for: 2 -> 2; matrix products, arithmetic and copies ran while one was open for 0% -> 0% of each run, Pallas kernels for 1% -> 1%
where the time goes in v13:
time: 28.5 us; the launch traced here: 28.3 us
  blocking collectives  10.9 us (38%)
  starting transfers between devices  6.91 us (24%)
  waiting for transfers between devices  5.26 us (18%)
  Pallas kernels  4.46 us (16%)
  between operations  0.73 us (3%)
    all_to_all x1, blocking collectives, per_device(): gathered = lax.all_to_all(chunks, axes, 0, 0, tiled=True)  10.9 us
    ppermute x1, starting transfers between devices, per_device(): first = lax.ppermute(first, axes, routes[0])  4.15 us
    ppermute x1, waiting for transfers between devices, per_device(): wet_first = lax.ppermute(wet, axes, routes[0])  3.51 us
    ppermute x1, starting transfers between devices, per_device(): second = lax.ppermute(second, axes, routes[3])  2.08 us
    pallas_call x1, Pallas kernels, per_device(): pl.pallas_call(functools.partial(up_kernel, size_x, size_y), out_shape=ja...  2 us
    ppermute x1, waiting for transfers between devices, per_device(): second = lax.ppermute(second, axes, routes[3])  1.73 us
    pallas_call x1, Pallas kernels, per_device(): pl.pallas_call(functools.partial(down_kernel, size_y, devices), out_shape...  1.17 us
    pallas_call x1, Pallas kernels, per_device(): pl.pallas_call(bands_kernel, out_shape=(band, band), in_specs=[HBM_SPEC]...  0.87 us
  transfers between devices with their start and end apart: 6, of which 2 were waited for; matrix products, arithmetic and copies ran while one was open for 0% of the time, Pallas kernels for 1%

profile of v13, /device:TPU:0, one launch (start us, length us, event | category | flops | bytes accessed | tf_op | source)
XLA Modules:
  0.0 28.3 jit_solution(4785965321860874488)
XLA Ops:
  0.0 0.0 copy-start.2
  0.0 0.0 copy-start.1
  0.0 0.0 copy-start
  0.0 0.9 %bands.1 = (f32[4,16,128]{2,1,0:T(8,128)S(1)}, f32[4,16,128]{2,1,0:T(8,128)S(1)}) custom-call(f32[2,128,128]{2,1,0:T(8,128)} %right_side.5, f32[128,128]{1,0:T(8,128)} %shift_coef.5, f32[128,128]{1,0:T(8,128)} %viscosity.5), custom_call_target="tpu_custom_call" | custom-call | tf_op jit(solution)/shard_map/bands/pallas_call | solution.py:938
  0.9 0.5 %collective-permute-start = (f32[4,16,128]{2,1,0:T(8,128)S(1)}, f32[4,16,128]{2,1,0:T(8,128)S(1)}, u32[]{:S(2)}, u32[]{:S(2)}) collective-permute-start(f32[4,16,128]{2,1,0:T(8,128)S(1)} %get-tuple-element.17), channel_id=1, source_target_pairs={{0,1},{1,0},{2,3},{3,2},{4,5},{5,4},{6,7},{7,6},{8,16},{9,17},{10,... | collective-permute-start | bytes 98312 | tf_op jit(solution)/shard_map/ppermute | solution.py:949
  1.4 4.1 %collective-permute-start.1 = (f32[4,16,128]{2,1,0:T(8,128)S(1)}, f32[4,16,128]{2,1,0:T(8,128)S(1)}, u32[]{:S(2)}, u32[]{:S(2)}) collective-permute-start(f32[4,16,128]{2,1,0:T(8,128)S(1)} %get-tuple-element.15), channel_id=1, source_target_pairs={{0,8},{1,9},{2,10},{3,11},{4,12},{5,13},{6,14},{7,15},{8,0},{9,1},... | collective-permute-start | bytes 98312 | tf_op jit(solution)/shard_map/ppermute | solution.py:950
  6.2 0.1 collective-permute-start.3
  6.3 0.1 collective-permute-start.2
  6.4 3.5 %collective-permute-done.3.wet_first = f32[8,128]{1,0:T(8,128)S(1)} collective-permute-done((f32[8,128]{1,0:T(8,128)S(1)}, f32[8,128]{1,0:T(8,128)S(1)}, u32[]{:S(2)}, u32[]{:S(2)}) %collective-permute-start.3) | collective-permute-done | bytes 4128 | tf_op jit(solution)/shard_map/ppermute | solution.py:952
  9.9 0.0 collective-permute-done.2.wet_second
  9.9 0.0 collective-permute-done.got_second
  9.9 0.0 collective-permute-done.1.got_first
  9.9 0.0 copy-done.2
  9.9 0.0 copy-done.1
  9.9 0.0 copy-done
  9.9 0.2 strips.1
  10.1 2.1 %collective-permute-start.4 = (f32[80,128]{1,0:T(8,128)S(1)}, f32[80,128]{1,0:T(8,128)S(1)}, u32[]{:S(2)}, u32[]{:S(2)}) collective-permute-start(f32[80,128]{1,0:T(8,128)S(1)} %get-tuple-element.18), channel_id=1, source_target_pairs={{0,8},{1,2},{2,1},{3,4},{4,3},{5,6},{6,5},{7,15},{8,0},{9,10},{10,... | collective-permute-start | bytes 122888 | tf_op jit(solution)/shard_map/ppermute | solution.py:972
  12.2 0.0 collective-permute-start.5
  12.2 0.2 halves.1.held
  12.5 1.7 %collective-permute-done.4.got_second = f32[80,128]{1,0:T(8,128)S(1)} collective-permute-done((f32[80,128]{1,0:T(8,128)S(1)}, f32[80,128]{1,0:T(8,128)S(1)}, u32[]{:S(2)}, u32[]{:S(2)}) %collective-permute-start.4) | collective-permute-done | bytes 40992 | tf_op jit(solution)/shard_map/ppermute | solution.py:972
  14.2 0.0 collective-permute-done.5.got_first
  14.2 1.2 %down.1 = (f32[128,128]{1,0:T(8,128)S(1)}, f32[10,184,128]{2,1,0:T(8,128)S(1)}, f32[10,104,128]{2,1,0:T(8,128)S(1)}, f32[10,64,128]{2,1,0:T(8,128)S(1)}, f32[16,48,128]{2,1,0:T(8,128)S(1)}) custom-call(f32[80,128]{1,0:T(8,128)S(1)} %collective-permute-done.4.got_second, f32[80,128]{1,0:T(8,128)S(1)} %collective-permute-done.5.got_first, ...), custom_call_target="tpu_custom_call" | custom-call | tf_op jit(solution)/shard_map/down/pallas_call | solution.py:978
  15.4 10.9 %all_to_all.11 = f32[32,4,128]{2,1,0:T(4,128)S(1)} all-to-all(f32[32,4,128]{2,1,0:T(4,128)S(1)} %bitcast.4), channel_id=1, replica_groups=mesh['gx'=4,'gy'=8] {'gx','gy'}, dimensions={0} | all-to-all | bytes 131072 | tf_op jit(solution)/shard_map/all_to_all | solution.py:994
  26.3 2.0 %up.1 = f32[2,128,128]{2,1,0:T(8,128)} custom-call(f32[128,128]{1,0:T(8,128)S(1)} %bitcast.3, f32[10,184,128]{2,1,0:T(8,128)S(1)} %get-tuple-element.21.state0, f32[10,104,128]{2,1,0:T(8,128)S(1)} %get-tuple-element.22.state1, f32[10,64,128]{2,1,0:T(8,128)S(1)} %get-tuple-element.23.state2, f32[16,48,128]{2,1,0:T(8,128)S(1)} %get-tuple-element.24.state3), custom_call_target="tpu_custom_call" | custom-call | tf_op jit(solution)/shard_map/up/pallas_call | solution.py:997
  (1 shorter events, 0.0 us)
Async XLA Ops:
  0.0 9.9 %copy-start.2 = (f32[128,128]{1,0:T(8,128)S(1)}, f32[128,128]{1,0:T(8,128)}, u32[]{:S(2)}) copy-start(f32[128,128]{1,0:T(8,128)} %viscosity.5) | copy-start | bytes 196612
  0.0 9.9 %copy-start.1 = (f32[128,128]{1,0:T(8,128)S(1)}, f32[128,128]{1,0:T(8,128)}, u32[]{:S(2)}) copy-start(f32[128,128]{1,0:T(8,128)} %shift_coef.5) | copy-start | bytes 196612
  0.0 9.9 %copy-start = (f32[2,128,128]{2,1,0:T(8,128)S(1)}, f32[2,128,128]{2,1,0:T(8,128)}, u32[]{:S(2)}) copy-start(f32[2,128,128]{2,1,0:T(8,128)} %right_side.5) | copy-start | bytes 393220
  0.9 9.0 %collective-permute-start = (f32[4,16,128]{2,1,0:T(8,128)S(1)}, f32[4,16,128]{2,1,0:T(8,128)S(1)}, u32[]{:S(2)}, u32[]{:S(2)}) collective-permute-start(f32[4,16,128]{2,1,0:T(8,128)S(1)} %get-tuple-element.17), channel_id=1, source_target_pairs={{0,1},{1,0},{2,3},{3,2},{4,5},{5,4},{6,7},{7,6},{8,16},{9,17},{10,... | collective-permute-start | bytes 98312 | tf_op jit(solution)/shard_map/ppermute | solution.py:949
  1.4 8.5 %collective-permute-start.1 = (f32[4,16,128]{2,1,0:T(8,128)S(1)}, f32[4,16,128]{2,1,0:T(8,128)S(1)}, u32[]{:S(2)}, u32[]{:S(2)}) collective-permute-start(f32[4,16,128]{2,1,0:T(8,128)S(1)} %get-tuple-element.15), channel_id=1, source_target_pairs={{0,8},{1,9},{2,10},{3,11},{4,12},{5,13},{6,14},{7,15},{8,0},{9,1},... | collective-permute-start | bytes 98312 | tf_op jit(solution)/shard_map/ppermute | solution.py:950
  6.2 3.7 %collective-permute-start.3 = (f32[8,128]{1,0:T(8,128)S(1)}, f32[8,128]{1,0:T(8,128)S(1)}, u32[]{:S(2)}, u32[]{:S(2)}) collective-permute-start(f32[8,128]{1,0:T(8,128)S(1)} %broadcast_in_dim.8.wet), channel_id=1, source_target_pairs={{0,8},{1,9},{2,10},{3,11},{4,12},{5,13},{6,14},{7,15},{8,0},{9,1},... | collective-permute-start | bytes 12296 | tf_op jit(solution)/shard_map/ppermute | solution.py:952
  6.3 3.6 %collective-permute-start.2 = (f32[8,128]{1,0:T(8,128)S(1)}, f32[8,128]{1,0:T(8,128)S(1)}, u32[]{:S(2)}, u32[]{:S(2)}) collective-permute-start(f32[8,128]{1,0:T(8,128)S(1)} %broadcast_in_dim.8.wet), channel_id=1, source_target_pairs={{0,1},{1,0},{2,3},{3,2},{4,5},{5,4},{6,7},{7,6},{8,16},{9,17},{10,... | collective-permute-start | bytes 12296 | tf_op jit(solution)/shard_map/ppermute | solution.py:951
  10.1 4.1 %collective-permute-start.4 = (f32[80,128]{1,0:T(8,128)S(1)}, f32[80,128]{1,0:T(8,128)S(1)}, u32[]{:S(2)}, u32[]{:S(2)}) collective-permute-start(f32[80,128]{1,0:T(8,128)S(1)} %get-tuple-element.18), channel_id=1, source_target_pairs={{0,8},{1,2},{2,1},{3,4},{4,3},{5,6},{6,5},{7,15},{8,0},{9,10},{10,... | collective-permute-start | bytes 122888 | tf_op jit(solution)/shard_map/ppermute | solution.py:972
  12.2 2.0 %collective-permute-start.5 = (f32[80,128]{1,0:T(8,128)S(1)}, f32[80,128]{1,0:T(8,128)S(1)}, u32[]{:S(2)}, u32[]{:S(2)}) collective-permute-start(f32[80,128]{1,0:T(8,128)S(1)} %get-tuple-element.19), channel_id=1, source_target_pairs={{0,1},{1,0},{2,3},{3,2},{4,5},{5,4},{6,7},{7,6},{8,9},{9,8},{10,11... | collective-permute-start | bytes 122888 | tf_op jit(solution)/shard_map/ppermute | solution.py:973

commit v14 on v12

--- a/solution.py
+++ b/solution.py
@@ -30,6 +30,7 @@
 CHUNK = 4
 PIECES = (4, 8)
 F32 = jnp.float32
+FIRST_COST = 1 << 31
 VMEM_LIMIT = 48 * 1024 * 1024
 
 SWEPT, CENTRE, SIDE, ACROSS = 0, 4, 6, 8
@@ -53,28 +54,20 @@
     return ref[slot, row : row + SUB, :]
 
 
-def bands_kernel(wet, right_side, shift_coef, viscosity, first, second, sems):
+def first_kernel(blank):
+    blank[...] = jnp.zeros((SUB, LANES), F32)
+
+
+def bands_kernel(wet, blank, right_side, shift_coef, viscosity, first, second):
     odd = lax.axis_index("gx") % 2
     wetness = wet[0, 0].astype(F32)
     bottom = LANES - HALO
-    copies = []
-    for slot, (start, out) in enumerate(((bottom - bottom * odd, first), (bottom * odd, second))):
+    for start, out in ((bottom - bottom * odd, first), (bottom * odd, second)):
         rows = pl.ds(pl.multiple_of(start, SUB), HALO)
-        for kind, (source, target) in enumerate(
-            (
-                (right_side.at[:, rows, :], out.at[0:2]),
-                (shift_coef.at[rows, :], out.at[2]),
-                (viscosity.at[rows, :], out.at[3]),
-            )
-        ):
-            copies.append(pltpu.make_async_copy(source, target, sems.at[3 * slot + kind]))
-    for copy in copies:
-        copy.start()
-    for copy in copies:
-        copy.wait()
-    for out in (first, second):
-        for field in (0, 1, 3):
-            out[field] = out[field] * wetness
+        out[0] = right_side[0, rows, :] * wetness
+        out[1] = right_side[1, rows, :] * wetness
+        out[2] = shift_coef[rows, :]
+        out[3] = viscosity[rows, :] * wetness
 
 
 def own_rows(right_side, shift_coef, viscosity, field, tile):
@@ -912,15 +905,23 @@
     routes = swap_routes(size_x, size_y)
     band = pltpu.VMEM((4, HALO, LANES), F32)
     own = (right_side, shift_coef, viscosity)
+    blank = pl.pallas_call(
+        first_kernel,
+        out_shape=pltpu.VMEM((SUB, LANES), F32),
+        out_specs=VMEM_SPEC,
+        cost_estimate=pl.CostEstimate(flops=FIRST_COST, bytes_accessed=FIRST_COST // 16, transcendentals=0),
+        compiler_params=params(),
+        name="first",
+    )()
+    wet_tiles, blank = lax.optimization_barrier((wet_tiles, blank))
     first, second = pl.pallas_call(
         bands_kernel,
         out_shape=(band, band),
-        in_specs=[SMEM_SPEC] + [HBM_SPEC] * 3,
+        in_specs=[SMEM_SPEC] + [VMEM_SPEC] * 4,
         out_specs=(VMEM_SPEC,) * 2,
-        scratch_shapes=[pltpu.SemaphoreType.DMA((6,))],
         compiler_params=params(),
         name="bands",
-    )(wet_tiles, *[pltpu.with_memory_space_constraint(array, pltpu.HBM) for array in own])
+    )(wet_tiles, blank, *own)
     second = lax.ppermute(second, axes, routes[1])
     first = lax.ppermute(first, axes, routes[0])
     strip = jax.ShapeDtypeStruct((MESSAGE, LANES), F32)

time: 27.3 us -> 26.5 us (0.971)
  Pallas kernels: 4.49 us -> 3.59 us
  local copies, waits for them, and re-layouts: 0.01 us -> 0.29 us
    pallas_call x1, Pallas kernels: 0.92 us -> 0.01 us  [per_device(): pl.pallas_call(bands_kernel, out_shape=(band, band), in_specs=[SMEM_SPEC]...]
    unnamed x6, local copies, waits for them, and re-layouts: 0.01 us -> 0.29 us
where the time goes in v14:
time: 26.5 us; the launch traced here: 26.4 us
  blocking collectives  11.4 us (43%)
  starting transfers between devices  6.73 us (25%)
  waiting for transfers between devices  3.62 us (14%)
  Pallas kernels  3.59 us (14%)
  between operations  0.72 us (3%)
  local copies, waits for them, and re-layouts  0.29 us (1%)
    all_to_all x1, blocking collectives, per_device(): gathered = lax.all_to_all(chunks, axes, 0, 0, tiled=True)  11.4 us
    ppermute x1, starting transfers between devices, per_device(): first = lax.ppermute(first, axes, routes[0])  4.15 us
    ppermute x1, starting transfers between devices, per_device(): second = lax.ppermute(second, axes, routes[3])  2.09 us
    pallas_call x1, Pallas kernels, per_device(): pl.pallas_call(functools.partial(up_kernel, size_x, size_y), out_shape=ja...  2 us
    ppermute x1, waiting for transfers between devices, per_device(): first = lax.ppermute(first, axes, routes[0])  1.89 us
    ppermute x1, waiting for transfers between devices, per_device(): second = lax.ppermute(second, axes, routes[3])  1.73 us
    pallas_call x1, Pallas kernels, per_device(): pl.pallas_call(functools.partial(down_kernel, size_y, devices), out_shape...  1.17 us
  transfers between devices with their start and end apart: 4, of which 2 were waited for; matrix products, arithmetic and copies ran while one was open for 0% of the time, Pallas kernels for 1%

profile of v14, /device:TPU:0, one launch (start us, length us, event | category | flops | bytes accessed | tf_op | source)
XLA Modules:
  0.0 26.4 jit_solution(8094426529882669650)
XLA Ops:
  0.0 0.0 copy-start.2
  0.0 0.0 copy-start.1
  0.0 0.0 copy-start
  0.7 0.1 copy-done.2
  0.8 0.0 copy-done.1
  0.9 0.1 copy-done
  1.0 0.5 %collective-permute-start = (f32[4,16,128]{2,1,0:T(8,128)S(1)}, f32[4,16,128]{2,1,0:T(8,128)S(1)}, u32[]{:S(2)}, u32[]{:S(2)}) collective-permute-start(f32[4,16,128]{2,1,0:T(8,128)S(1)} %get-tuple-element.18), channel_id=1, source_target_pairs={{0,1},{1,0},{2,3},{3,2},{4,5},{5,4},{6,7},{7,6},{8,16},{9,17},{10,... | collective-permute-start | bytes 98312 | tf_op jit(solution)/shard_map/ppermute | solution.py:925
  1.5 4.1 %collective-permute-start.1 = (f32[4,16,128]{2,1,0:T(8,128)S(1)}, f32[4,16,128]{2,1,0:T(8,128)S(1)}, u32[]{:S(2)}, u32[]{:S(2)}) collective-permute-start(f32[4,16,128]{2,1,0:T(8,128)S(1)} %get-tuple-element.19), channel_id=1, source_target_pairs={{0,8},{1,9},{2,10},{3,11},{4,12},{5,13},{6,14},{7,15},{8,0},{9,1},... | collective-permute-start | bytes 98312 | tf_op jit(solution)/shard_map/ppermute | solution.py:926
  5.6 0.0 collective-permute-done.got_second
  5.6 1.9 %collective-permute-done.1.got_first = f32[4,16,128]{2,1,0:T(8,128)S(1)} collective-permute-done((f32[4,16,128]{2,1,0:T(8,128)S(1)}, f32[4,16,128]{2,1,0:T(8,128)S(1)}, u32[]{:S(2)}, u32[]{:S(2)}) %collective-permute-start.1) | collective-permute-done | bytes 32800 | tf_op jit(solution)/shard_map/ppermute | solution.py:926
  7.5 0.2 strips.1
  7.7 2.1 %collective-permute-start.2 = (f32[80,128]{1,0:T(8,128)S(1)}, f32[80,128]{1,0:T(8,128)S(1)}, u32[]{:S(2)}, u32[]{:S(2)}) collective-permute-start(f32[80,128]{1,0:T(8,128)S(1)} %get-tuple-element.20), channel_id=1, source_target_pairs={{0,8},{1,2},{2,1},{3,4},{4,3},{5,6},{6,5},{7,15},{8,0},{9,10},{10,... | collective-permute-start | bytes 122888 | tf_op jit(solution)/shard_map/ppermute | solution.py:946
  9.8 0.0 collective-permute-start.3
  9.8 0.2 halves.1.held
  10.0 1.7 %collective-permute-done.2.got_second = f32[80,128]{1,0:T(8,128)S(1)} collective-permute-done((f32[80,128]{1,0:T(8,128)S(1)}, f32[80,128]{1,0:T(8,128)S(1)}, u32[]{:S(2)}, u32[]{:S(2)}) %collective-permute-start.2) | collective-permute-done | bytes 40992 | tf_op jit(solution)/shard_map/ppermute | solution.py:946
  11.8 0.0 collective-permute-done.3.got_first
  11.8 1.2 %down.1 = (f32[128,128]{1,0:T(8,128)S(1)}, f32[10,184,128]{2,1,0:T(8,128)S(1)}, f32[10,104,128]{2,1,0:T(8,128)S(1)}, f32[10,64,128]{2,1,0:T(8,128)S(1)}, f32[16,48,128]{2,1,0:T(8,128)S(1)}) custom-call(f32[80,128]{1,0:T(8,128)S(1)} %collective-permute-done.2.got_second, f32[80,128]{1,0:T(8,128)S(1)} %collective-permute-done.3.got_first, ...), custom_call_target="tpu_custom_call" | custom-call | tf_op jit(solution)/shard_map/down/pallas_call | solution.py:952
  13.0 11.4 %all_to_all.11 = f32[32,4,128]{2,1,0:T(4,128)S(1)} all-to-all(f32[32,4,128]{2,1,0:T(4,128)S(1)} %bitcast.3), channel_id=1, replica_groups=mesh['gx'=4,'gy'=8] {'gx','gy'}, dimensions={0} | all-to-all | bytes 131072 | tf_op jit(solution)/shard_map/all_to_all | solution.py:968
  24.4 2.0 %up.1 = f32[2,128,128]{2,1,0:T(8,128)} custom-call(f32[128,128]{1,0:T(8,128)S(1)} %bitcast.2, f32[10,184,128]{2,1,0:T(8,128)S(1)} %get-tuple-element.23.state0, f32[10,104,128]{2,1,0:T(8,128)S(1)} %get-tuple-element.24.state1, f32[10,64,128]{2,1,0:T(8,128)S(1)} %get-tuple-element.25.state2, f32[16,48,128]{2,1,0:T(8,128)S(1)} %get-tuple-element.26.state3), custom_call_target="tpu_custom_call" | custom-call | tf_op jit(solution)/shard_map/up/pallas_call | solution.py:971
  (2 shorter events, 0.0 us)
Async XLA Ops:
  0.0 0.8 %copy-start.2 = (f32[128,128]{1,0:T(8,128)S(1)}, f32[128,128]{1,0:T(8,128)}, u32[]{:S(2)}) copy-start(f32[128,128]{1,0:T(8,128)} %viscosity.5) | copy-start | bytes 196612
  0.0 0.9 %copy-start.1 = (f32[128,128]{1,0:T(8,128)S(1)}, f32[128,128]{1,0:T(8,128)}, u32[]{:S(2)}) copy-start(f32[128,128]{1,0:T(8,128)} %shift_coef.5) | copy-start | bytes 196612
  0.0 1.0 %copy-start = (f32[2,128,128]{2,1,0:T(8,128)S(1)}, f32[2,128,128]{2,1,0:T(8,128)}, u32[]{:S(2)}) copy-start(f32[2,128,128]{2,1,0:T(8,128)} %right_side.5) | copy-start | bytes 393220
  1.0 4.6 %collective-permute-start = (f32[4,16,128]{2,1,0:T(8,128)S(1)}, f32[4,16,128]{2,1,0:T(8,128)S(1)}, u32[]{:S(2)}, u32[]{:S(2)}) collective-permute-start(f32[4,16,128]{2,1,0:T(8,128)S(1)} %get-tuple-element.18), channel_id=1, source_target_pairs={{0,1},{1,0},{2,3},{3,2},{4,5},{5,4},{6,7},{7,6},{8,16},{9,17},{10,... | collective-permute-start | bytes 98312 | tf_op jit(solution)/shard_map/ppermute | solution.py:925
  1.5 6.0 %collective-permute-start.1 = (f32[4,16,128]{2,1,0:T(8,128)S(1)}, f32[4,16,128]{2,1,0:T(8,128)S(1)}, u32[]{:S(2)}, u32[]{:S(2)}) collective-permute-start(f32[4,16,128]{2,1,0:T(8,128)S(1)} %get-tuple-element.19), channel_id=1, source_target_pairs={{0,8},{1,9},{2,10},{3,11},{4,12},{5,13},{6,14},{7,15},{8,0},{9,1},... | collective-permute-start | bytes 98312 | tf_op jit(solution)/shard_map/ppermute | solution.py:926
  7.7 4.1 %collective-permute-start.2 = (f32[80,128]{1,0:T(8,128)S(1)}, f32[80,128]{1,0:T(8,128)S(1)}, u32[]{:S(2)}, u32[]{:S(2)}) collective-permute-start(f32[80,128]{1,0:T(8,128)S(1)} %get-tuple-element.20), channel_id=1, source_target_pairs={{0,8},{1,2},{2,1},{3,4},{4,3},{5,6},{6,5},{7,15},{8,0},{9,10},{10,... | collective-permute-start | bytes 122888 | tf_op jit(solution)/shard_map/ppermute | solution.py:946
  9.8 2.0 %collective-permute-start.3 = (f32[80,128]{1,0:T(8,128)S(1)}, f32[80,128]{1,0:T(8,128)S(1)}, u32[]{:S(2)}, u32[]{:S(2)}) collective-permute-start(f32[80,128]{1,0:T(8,128)S(1)} %get-tuple-element.21), channel_id=1, source_target_pairs={{0,1},{1,0},{2,3},{3,2},{4,5},{5,4},{6,7},{7,6},{8,9},{9,8},{10,11... | collective-permute-start | bytes 122888 | tf_op jit(solution)/shard_map/ppermute | solution.py:947

commit v15 on v14

--- a/solution.py
+++ b/solution.py
@@ -84,45 +84,64 @@
     return to_left, q >> 1, cell
 
 
-def strips_kernel(
-    size_x, wet, got_second, got_first, right_side, shift_coef, viscosity, first, second
-):
+def rim_value(pieces, place):
+    _, owner, cell = place
+    value = None
+    for field in range(4):
+        part = lane_take(pieces[field], cell)
+        value = part if value is None else jnp.where(owner == field, part, value)
+    return value
+
+
+RIM_TILES = HALO // SUB
+
+
+def edges_kernel(wet, right_side, shift_coef, viscosity, lefts, rights):
+    wetness = wet[0, 0].astype(F32)
+    lane = iota(1)
+    places = [rim_place(half, lane) for half in range(2)]
+    found = {}
+    for half in range(2):
+        mask = jnp.where(places[half][1] == 2, 1.0, wetness)
+        for tile in range(HALF_TILES):
+            at = tile + half * HALF_TILES - RIM_TILES
+            if 0 <= at < LANES // SUB:
+                pieces = [own_rows(right_side, shift_coef, viscosity, f, at) for f in range(4)]
+                found[half, tile] = rim_value(pieces, places[half]) * mask
+    blank = jnp.zeros((SUB, LANES), F32)
+    for tile in range(HALF_TILES):
+        upper, lower = (found.get((half, tile), blank) for half in range(2))
+        rows = slice(SUB * tile, SUB * tile + SUB)
+        lefts[rows, :] = jnp.where(places[0][0], upper, lower)
+        rights[rows, :] = jnp.where(places[0][0], lower, upper)
+
+
+def strips_kernel(size_x, got_second, got_first, lefts, rights, first, second):
     index_x = lax.axis_index("gx")
     odd_x = index_x % 2 == 1
     odd_y = lax.axis_index("gy") % 2 == 1
-    wetness = wet[0, 0].astype(F32)
     above = (index_x > 0).astype(F32)
     below = (index_x < size_x - 1).astype(F32)
     lane = iota(1)
-    rim_tiles = HALO // SUB
-
-    def piece(field, tile):
-        if rim_tiles <= tile < TILES[0] - rim_tiles:
-            return own_rows(right_side, shift_coef, viscosity, field, tile - rim_tiles)
-        top = tile < rim_tiles
-        row = SUB * (tile if top else tile - (TILES[0] - rim_tiles))
-        one, two = tile_at(got_first, field, row), tile_at(got_second, field, row)
-        return jnp.where(odd_x, one, two) if top else jnp.where(odd_x, two, one)
-
     places = [rim_place(half, lane) for half in range(2)]
     found = {}
     for half in range(2):
-        _, owner, cell = places[half]
-        for tile in range(HALF_TILES):
-            at = tile + half * HALF_TILES
-            value = None
+        mask = jnp.where(places[half][1] == 3, below if half else above, 1.0)
+        for tile in range(RIM_TILES):
+            row = SUB * tile
+            pieces = []
             for field in range(4):
-                part = lane_take(piece(field, at), cell)
-                value = part if value is None else jnp.where(owner == field, part, value)
-            if rim_tiles <= at < TILES[0] - rim_tiles:
-                value = value * jnp.where(owner == 2, 1.0, wetness)
-            else:
-                value = value * jnp.where(owner == 3, above if at < rim_tiles else below, 1.0)
-            found[half, tile] = value
+                one, two = tile_at(got_first, field, row), tile_at(got_second, field, row)
+                pieces.append(jnp.where(odd_x, two, one) if half else jnp.where(odd_x, one, two))
+            at = HALF_TILES - RIM_TILES + tile if half else tile
+            found[at] = (half, rim_value(pieces, places[half]) * mask)
     for tile in range(HALF_TILES):
-        left = jnp.where(places[0][0], found[0, tile], found[1, tile])
-        right = jnp.where(places[0][0], found[1, tile], found[0, tile])
         rows = slice(SUB * tile, SUB * tile + SUB)
+        left, right = lefts[rows, :], rights[rows, :]
+        if tile in found:
+            half, value = found[tile]
+            left = jnp.where(places[half][0], value, left)
+            right = jnp.where(places[half][0], right, value)
         first[rows, :] = jnp.where(odd_y, left, right)
         second[rows, :] = jnp.where(odd_y, right, left)
 
@@ -926,20 +945,30 @@
     first = lax.ppermute(first, axes, routes[0])
     strip = jax.ShapeDtypeStruct((MESSAGE, LANES), F32)
     got = (second, first)
+    meantime = pl.CostEstimate(flops=1 << 20, bytes_accessed=1 << 21, transcendentals=0)
+    edges = pl.pallas_call(
+        edges_kernel,
+        out_shape=(pltpu.VMEM((MESSAGE, LANES), F32),) * 2,
+        in_specs=[SMEM_SPEC] + [VMEM_SPEC] * 3,
+        out_specs=(VMEM_SPEC,) * 2,
+        cost_estimate=meantime,
+        compiler_params=params(),
+        name="edges",
+    )(wet_tiles, *own)
     first, second = pl.pallas_call(
         functools.partial(strips_kernel, size_x),
         out_shape=(strip, strip),
-        in_specs=[SMEM_SPEC] + [VMEM_SPEC] * 5,
+        in_specs=[VMEM_SPEC] * 4,
         out_specs=(VMEM_SPEC,) * 2,
         compiler_params=params(),
         name="strips",
-    )(wet_tiles, *got, *own)
+    )(*got, *edges)
     fields = pl.pallas_call(
         functools.partial(halves_kernel, size_x),
         out_shape=pltpu.VMEM((8, HELD[0], LANES), F32),
         in_specs=[SMEM_SPEC] + [VMEM_SPEC] * 5,
         out_specs=VMEM_SPEC,
-        cost_estimate=pl.CostEstimate(flops=1 << 20, bytes_accessed=1 << 21, transcendentals=0),
+        cost_estimate=meantime,
         compiler_params=params(),
         name="halves",
     )(wet_tiles, *got, *own)

time: 26.5 us -> 26.5 us (level)
  no operation moved by 1% of the time
where the time goes in v15:
time: 26.5 us; the launch traced here: 26.3 us
  blocking collectives  11.4 us (43%)
  starting transfers between devices  6.73 us (25%)
  Pallas kernels  3.67 us (14%)
  waiting for transfers between devices  3.47 us (13%)
  between operations  0.73 us (3%)
  local copies, waits for them, and re-layouts  0.29 us (1%)
    all_to_all x1, blocking collectives, per_device(): gathered = lax.all_to_all(chunks, axes, 0, 0, tiled=True)  11.4 us
    ppermute x1, starting transfers between devices, per_device(): first = lax.ppermute(first, axes, routes[0])  4.15 us
    ppermute x1, starting transfers between devices, per_device(): second = lax.ppermute(second, axes, routes[3])  2.09 us
    pallas_call x1, Pallas kernels, per_device(): pl.pallas_call(functools.partial(up_kernel, size_x, size_y), out_shape=ja...  2 us
    ppermute x1, waiting for transfers between devices, per_device(): second = lax.ppermute(second, axes, routes[3])  1.73 us
    ppermute x1, waiting for transfers between devices, per_device(): first = lax.ppermute(first, axes, routes[0])  1.73 us
    pallas_call x1, Pallas kernels, per_device(): pl.pallas_call(functools.partial(down_kernel, size_y, devices), out_shape...  1.17 us
  transfers between devices with their start and end apart: 4, of which 2 were waited for; matrix products, arithmetic and copies ran while one was open for 0% of the time, Pallas kernels for 1%

profile of v15, /device:TPU:0, one launch (start us, length us, event | category | flops | bytes accessed | tf_op | source)
XLA Modules:
  0.0 26.3 jit_solution(13219222596205960368)
XLA Ops:
  0.0 0.0 copy-start.2
  0.0 0.0 copy-start.1
  0.0 0.0 copy-start
  0.7 0.1 copy-done.2
  0.8 0.0 copy-done.1
  0.9 0.1 copy-done
  1.0 0.5 %collective-permute-start = (f32[4,16,128]{2,1,0:T(8,128)S(1)}, f32[4,16,128]{2,1,0:T(8,128)S(1)}, u32[]{:S(2)}, u32[]{:S(2)}) collective-permute-start(f32[4,16,128]{2,1,0:T(8,128)S(1)} %get-tuple-element.20), channel_id=1, source_target_pairs={{0,1},{1,0},{2,3},{3,2},{4,5},{5,4},{6,7},{7,6},{8,16},{9,17},{10,... | collective-permute-start | bytes 98312 | tf_op jit(solution)/shard_map/ppermute | solution.py:944
  1.5 4.1 %collective-permute-start.1 = (f32[4,16,128]{2,1,0:T(8,128)S(1)}, f32[4,16,128]{2,1,0:T(8,128)S(1)}, u32[]{:S(2)}, u32[]{:S(2)}) collective-permute-start(f32[4,16,128]{2,1,0:T(8,128)S(1)} %get-tuple-element.21), channel_id=1, source_target_pairs={{0,8},{1,9},{2,10},{3,11},{4,12},{5,13},{6,14},{7,15},{8,0},{9,1},... | collective-permute-start | bytes 98312 | tf_op jit(solution)/shard_map/ppermute | solution.py:945
  5.6 0.1 edges.1
  5.8 0.0 collective-permute-done.got_second
  5.8 1.7 %collective-permute-done.1.got_first = f32[4,16,128]{2,1,0:T(8,128)S(1)} collective-permute-done((f32[4,16,128]{2,1,0:T(8,128)S(1)}, f32[4,16,128]{2,1,0:T(8,128)S(1)}, u32[]{:S(2)}, u32[]{:S(2)}) %collective-permute-start.1) | collective-permute-done | bytes 32800 | tf_op jit(solution)/shard_map/ppermute | solution.py:945
  7.5 0.1 strips.1
  7.6 2.1 %collective-permute-start.2 = (f32[80,128]{1,0:T(8,128)S(1)}, f32[80,128]{1,0:T(8,128)S(1)}, u32[]{:S(2)}, u32[]{:S(2)}) collective-permute-start(f32[80,128]{1,0:T(8,128)S(1)} %get-tuple-element.24), channel_id=1, source_target_pairs={{0,8},{1,2},{2,1},{3,4},{4,3},{5,6},{6,5},{7,15},{8,0},{9,10},{10,... | collective-permute-start | bytes 122888 | tf_op jit(solution)/shard_map/ppermute | solution.py:975
  9.7 0.0 collective-permute-start.3
  9.7 0.2 halves.1.held
  10.0 1.7 %collective-permute-done.2.got_second = f32[80,128]{1,0:T(8,128)S(1)} collective-permute-done((f32[80,128]{1,0:T(8,128)S(1)}, f32[80,128]{1,0:T(8,128)S(1)}, u32[]{:S(2)}, u32[]{:S(2)}) %collective-permute-start.2) | collective-permute-done | bytes 40992 | tf_op jit(solution)/shard_map/ppermute | solution.py:975
  11.7 0.0 collective-permute-done.3.got_first
  11.7 1.2 %down.1 = (f32[128,128]{1,0:T(8,128)S(1)}, f32[10,184,128]{2,1,0:T(8,128)S(1)}, f32[10,104,128]{2,1,0:T(8,128)S(1)}, f32[10,64,128]{2,1,0:T(8,128)S(1)}, f32[16,48,128]{2,1,0:T(8,128)S(1)}) custom-call(f32[80,128]{1,0:T(8,128)S(1)} %collective-permute-done.2.got_second, f32[80,128]{1,0:T(8,128)S(1)} %collective-permute-done.3.got_first, ...), custom_call_target="tpu_custom_call" | custom-call | tf_op jit(solution)/shard_map/down/pallas_call | solution.py:981
  12.9 11.4 %all_to_all.11 = f32[32,4,128]{2,1,0:T(4,128)S(1)} all-to-all(f32[32,4,128]{2,1,0:T(4,128)S(1)} %bitcast.3), channel_id=1, replica_groups=mesh['gx'=4,'gy'=8] {'gx','gy'}, dimensions={0} | all-to-all | bytes 131072 | tf_op jit(solution)/shard_map/all_to_all | solution.py:997
  24.3 2.0 %up.1 = f32[2,128,128]{2,1,0:T(8,128)} custom-call(f32[128,128]{1,0:T(8,128)S(1)} %bitcast.2, f32[10,184,128]{2,1,0:T(8,128)S(1)} %get-tuple-element.27.state0, f32[10,104,128]{2,1,0:T(8,128)S(1)} %get-tuple-element.28.state1, f32[10,64,128]{2,1,0:T(8,128)S(1)} %get-tuple-element.29.state2, f32[16,48,128]{2,1,0:T(8,128)S(1)} %get-tuple-element.30.state3), custom_call_target="tpu_custom_call" | custom-call | tf_op jit(solution)/shard_map/up/pallas_call | solution.py:1000
  (2 shorter events, 0.0 us)
Async XLA Ops:
  0.0 0.8 %copy-start.2 = (f32[128,128]{1,0:T(8,128)S(1)}, f32[128,128]{1,0:T(8,128)}, u32[]{:S(2)}) copy-start(f32[128,128]{1,0:T(8,128)} %viscosity.5) | copy-start | bytes 196612
  0.0 0.9 %copy-start.1 = (f32[128,128]{1,0:T(8,128)S(1)}, f32[128,128]{1,0:T(8,128)}, u32[]{:S(2)}) copy-start(f32[128,128]{1,0:T(8,128)} %shift_coef.5) | copy-start | bytes 196612
  0.0 1.0 %copy-start = (f32[2,128,128]{2,1,0:T(8,128)S(1)}, f32[2,128,128]{2,1,0:T(8,128)}, u32[]{:S(2)}) copy-start(f32[2,128,128]{2,1,0:T(8,128)} %right_side.5) | copy-start | bytes 393220
  1.0 4.8 %collective-permute-start = (f32[4,16,128]{2,1,0:T(8,128)S(1)}, f32[4,16,128]{2,1,0:T(8,128)S(1)}, u32[]{:S(2)}, u32[]{:S(2)}) collective-permute-start(f32[4,16,128]{2,1,0:T(8,128)S(1)} %get-tuple-element.20), channel_id=1, source_target_pairs={{0,1},{1,0},{2,3},{3,2},{4,5},{5,4},{6,7},{7,6},{8,16},{9,17},{10,... | collective-permute-start | bytes 98312 | tf_op jit(solution)/shard_map/ppermute | solution.py:944
  1.5 6.0 %collective-permute-start.1 = (f32[4,16,128]{2,1,0:T(8,128)S(1)}, f32[4,16,128]{2,1,0:T(8,128)S(1)}, u32[]{:S(2)}, u32[]{:S(2)}) collective-permute-start(f32[4,16,128]{2,1,0:T(8,128)S(1)} %get-tuple-element.21), channel_id=1, source_target_pairs={{0,8},{1,9},{2,10},{3,11},{4,12},{5,13},{6,14},{7,15},{8,0},{9,1},... | collective-permute-start | bytes 98312 | tf_op jit(solution)/shard_map/ppermute | solution.py:945
  7.6 4.1 %collective-permute-start.2 = (f32[80,128]{1,0:T(8,128)S(1)}, f32[80,128]{1,0:T(8,128)S(1)}, u32[]{:S(2)}, u32[]{:S(2)}) collective-permute-start(f32[80,128]{1,0:T(8,128)S(1)} %get-tuple-element.24), channel_id=1, source_target_pairs={{0,8},{1,2},{2,1},{3,4},{4,3},{5,6},{6,5},{7,15},{8,0},{9,10},{10,... | collective-permute-start | bytes 122888 | tf_op jit(solution)/shard_map/ppermute | solution.py:975
  9.7 2.0 %collective-permute-start.3 = (f32[80,128]{1,0:T(8,128)S(1)}, f32[80,128]{1,0:T(8,128)S(1)}, u32[]{:S(2)}, u32[]{:S(2)}) collective-permute-start(f32[80,128]{1,0:T(8,128)S(1)} %get-tuple-element.25), channel_id=1, source_target_pairs={{0,1},{1,0},{2,3},{3,2},{4,5},{5,4},{6,7},{7,6},{8,9},{9,8},{10,11... | collective-permute-start | bytes 122888 | tf_op jit(solution)/shard_map/ppermute | solution.py:976

commit v16 on v15

--- a/solution.py
+++ b/solution.py
@@ -28,7 +28,7 @@
 HALF_TILES = TILES[0] // 2
 MESSAGE = ROWS[0] // 2
 CHUNK = 4
-PIECES = (4, 8)
+PIECES = (8,)
 F32 = jnp.float32
 FIRST_COST = 1 << 31
 VMEM_LIMIT = 48 * 1024 * 1024
@@ -210,7 +210,8 @@
             both = jnp.where(even_block, before, after)
         values = []
         for slot in slots:
-            rim = lane_roll(both, HALF - 16 * slot - 8 * half)
+            shift = HALF - 16 * slot - 8 * half
+            rim = lane_roll(both, shift) if shift else both
             if slot >= 4:
                 rim = jnp.where(side_ok > 0, rim, 1.0 if slot < 6 else 0.0)
             values.append(jnp.where(inner, tile_at(held, slot, row), rim))

time: 26.5 us -> 26.5 us (level)
  no operation moved by 1% of the time
where the time goes in v16:
time: 26.5 us; the launch traced here: 26.3 us
  blocking collectives  11.4 us (43%)
  starting transfers between devices  6.73 us (25%)
  Pallas kernels  3.68 us (14%)
  waiting for transfers between devices  3.47 us (13%)
  between operations  0.73 us (3%)
  local copies, waits for them, and re-layouts  0.29 us (1%)
    all_to_all x1, blocking collectives, per_device(): gathered = lax.all_to_all(chunks, axes, 0, 0, tiled=True)  11.4 us
    ppermute x1, starting transfers between devices, per_device(): first = lax.ppermute(first, axes, routes[0])  4.15 us
    ppermute x1, starting transfers between devices, per_device(): second = lax.ppermute(second, axes, routes[3])  2.09 us
    pallas_call x1, Pallas kernels, per_device(): pl.pallas_call(functools.partial(up_kernel, size_x, size_y), out_shape=ja...  2.01 us
    ppermute x1, waiting for transfers between devices, per_device(): second = lax.ppermute(second, axes, routes[3])  1.73 us
    ppermute x1, waiting for transfers between devices, per_device(): first = lax.ppermute(first, axes, routes[0])  1.73 us
    pallas_call x1, Pallas kernels, per_device(): pl.pallas_call(functools.partial(down_kernel, size_y, devices), out_shape...  1.17 us
  transfers between devices with their start and end apart: 4, of which 2 were waited for; matrix products, arithmetic and copies ran while one was open for 0% of the time, Pallas kernels for 1%

profile of v16, /device:TPU:0, one launch (start us, length us, event | category | flops | bytes accessed | tf_op | source)
XLA Modules:
  0.0 26.3 jit_solution(14977171415868204263)
XLA Ops:
  0.0 0.0 copy-start.2
  0.0 0.0 copy-start.1
  0.0 0.0 copy-start
  0.7 0.1 copy-done.2
  0.8 0.0 copy-done.1
  0.9 0.1 copy-done
  1.0 0.5 %collective-permute-start = (f32[4,16,128]{2,1,0:T(8,128)S(1)}, f32[4,16,128]{2,1,0:T(8,128)S(1)}, u32[]{:S(2)}, u32[]{:S(2)}) collective-permute-start(f32[4,16,128]{2,1,0:T(8,128)S(1)} %get-tuple-element.20), channel_id=1, source_target_pairs={{0,1},{1,0},{2,3},{3,2},{4,5},{5,4},{6,7},{7,6},{8,16},{9,17},{10,... | collective-permute-start | bytes 98312 | tf_op jit(solution)/shard_map/ppermute | solution.py:945
  1.5 4.1 %collective-permute-start.1 = (f32[4,16,128]{2,1,0:T(8,128)S(1)}, f32[4,16,128]{2,1,0:T(8,128)S(1)}, u32[]{:S(2)}, u32[]{:S(2)}) collective-permute-start(f32[4,16,128]{2,1,0:T(8,128)S(1)} %get-tuple-element.21), channel_id=1, source_target_pairs={{0,8},{1,9},{2,10},{3,11},{4,12},{5,13},{6,14},{7,15},{8,0},{9,1},... | collective-permute-start | bytes 98312 | tf_op jit(solution)/shard_map/ppermute | solution.py:946
  5.6 0.1 edges.1
  5.8 0.0 collective-permute-done.got_second
  5.8 1.7 %collective-permute-done.1.got_first = f32[4,16,128]{2,1,0:T(8,128)S(1)} collective-permute-done((f32[4,16,128]{2,1,0:T(8,128)S(1)}, f32[4,16,128]{2,1,0:T(8,128)S(1)}, u32[]{:S(2)}, u32[]{:S(2)}) %collective-permute-start.1) | collective-permute-done | bytes 32800 | tf_op jit(solution)/shard_map/ppermute | solution.py:946
  7.5 0.1 strips.1
  7.6 2.1 %collective-permute-start.2 = (f32[80,128]{1,0:T(8,128)S(1)}, f32[80,128]{1,0:T(8,128)S(1)}, u32[]{:S(2)}, u32[]{:S(2)}) collective-permute-start(f32[80,128]{1,0:T(8,128)S(1)} %get-tuple-element.24), channel_id=1, source_target_pairs={{0,8},{1,2},{2,1},{3,4},{4,3},{5,6},{6,5},{7,15},{8,0},{9,10},{10,... | collective-permute-start | bytes 122888 | tf_op jit(solution)/shard_map/ppermute | solution.py:976
  9.7 0.0 collective-permute-start.3
  9.7 0.2 halves.1.held
  10.0 1.7 %collective-permute-done.2.got_second = f32[80,128]{1,0:T(8,128)S(1)} collective-permute-done((f32[80,128]{1,0:T(8,128)S(1)}, f32[80,128]{1,0:T(8,128)S(1)}, u32[]{:S(2)}, u32[]{:S(2)}) %collective-permute-start.2) | collective-permute-done | bytes 40992 | tf_op jit(solution)/shard_map/ppermute | solution.py:976
  11.7 0.0 collective-permute-done.3.got_first
  11.7 1.2 %down.1 = (f32[128,128]{1,0:T(8,128)S(1)}, f32[10,184,128]{2,1,0:T(8,128)S(1)}, f32[10,104,128]{2,1,0:T(8,128)S(1)}, f32[10,64,128]{2,1,0:T(8,128)S(1)}, f32[16,48,128]{2,1,0:T(8,128)S(1)}) custom-call(f32[80,128]{1,0:T(8,128)S(1)} %collective-permute-done.2.got_second, f32[80,128]{1,0:T(8,128)S(1)} %collective-permute-done.3.got_first, ...), custom_call_target="tpu_custom_call" | custom-call | tf_op jit(solution)/shard_map/down/pallas_call | solution.py:982
  12.9 11.4 %all_to_all.11 = f32[32,4,128]{2,1,0:T(4,128)S(1)} all-to-all(f32[32,4,128]{2,1,0:T(4,128)S(1)} %bitcast.3), channel_id=1, replica_groups=mesh['gx'=4,'gy'=8] {'gx','gy'}, dimensions={0} | all-to-all | bytes 131072 | tf_op jit(solution)/shard_map/all_to_all | solution.py:998
  24.3 2.0 %up.1 = f32[2,128,128]{2,1,0:T(8,128)} custom-call(f32[128,128]{1,0:T(8,128)S(1)} %bitcast.2, f32[10,184,128]{2,1,0:T(8,128)S(1)} %get-tuple-element.27.state0, f32[10,104,128]{2,1,0:T(8,128)S(1)} %get-tuple-element.28.state1, f32[10,64,128]{2,1,0:T(8,128)S(1)} %get-tuple-element.29.state2, f32[16,48,128]{2,1,0:T(8,128)S(1)} %get-tuple-element.30.state3), custom_call_target="tpu_custom_call" | custom-call | tf_op jit(solution)/shard_map/up/pallas_call | solution.py:1001
  (2 shorter events, 0.0 us)
Async XLA Ops:
  0.0 0.8 %copy-start.2 = (f32[128,128]{1,0:T(8,128)S(1)}, f32[128,128]{1,0:T(8,128)}, u32[]{:S(2)}) copy-start(f32[128,128]{1,0:T(8,128)} %viscosity.5) | copy-start | bytes 196612
  0.0 0.9 %copy-start.1 = (f32[128,128]{1,0:T(8,128)S(1)}, f32[128,128]{1,0:T(8,128)}, u32[]{:S(2)}) copy-start(f32[128,128]{1,0:T(8,128)} %shift_coef.5) | copy-start | bytes 196612
  0.0 1.0 %copy-start = (f32[2,128,128]{2,1,0:T(8,128)S(1)}, f32[2,128,128]{2,1,0:T(8,128)}, u32[]{:S(2)}) copy-start(f32[2,128,128]{2,1,0:T(8,128)} %right_side.5) | copy-start | bytes 393220
  1.0 4.8 %collective-permute-start = (f32[4,16,128]{2,1,0:T(8,128)S(1)}, f32[4,16,128]{2,1,0:T(8,128)S(1)}, u32[]{:S(2)}, u32[]{:S(2)}) collective-permute-start(f32[4,16,128]{2,1,0:T(8,128)S(1)} %get-tuple-element.20), channel_id=1, source_target_pairs={{0,1},{1,0},{2,3},{3,2},{4,5},{5,4},{6,7},{7,6},{8,16},{9,17},{10,... | collective-permute-start | bytes 98312 | tf_op jit(solution)/shard_map/ppermute | solution.py:945
  1.5 6.0 %collective-permute-start.1 = (f32[4,16,128]{2,1,0:T(8,128)S(1)}, f32[4,16,128]{2,1,0:T(8,128)S(1)}, u32[]{:S(2)}, u32[]{:S(2)}) collective-permute-start(f32[4,16,128]{2,1,0:T(8,128)S(1)} %get-tuple-element.21), channel_id=1, source_target_pairs={{0,8},{1,9},{2,10},{3,11},{4,12},{5,13},{6,14},{7,15},{8,0},{9,1},... | collective-permute-start | bytes 98312 | tf_op jit(solution)/shard_map/ppermute | solution.py:946
  7.6 4.1 %collective-permute-start.2 = (f32[80,128]{1,0:T(8,128)S(1)}, f32[80,128]{1,0:T(8,128)S(1)}, u32[]{:S(2)}, u32[]{:S(2)}) collective-permute-start(f32[80,128]{1,0:T(8,128)S(1)} %get-tuple-element.24), channel_id=1, source_target_pairs={{0,8},{1,2},{2,1},{3,4},{4,3},{5,6},{6,5},{7,15},{8,0},{9,10},{10,... | collective-permute-start | bytes 122888 | tf_op jit(solution)/shard_map/ppermute | solution.py:976
  9.7 2.0 %collective-permute-start.3 = (f32[80,128]{1,0:T(8,128)S(1)}, f32[80,128]{1,0:T(8,128)S(1)}, u32[]{:S(2)}, u32[]{:S(2)}) collective-permute-start(f32[80,128]{1,0:T(8,128)S(1)} %get-tuple-element.25), channel_id=1, source_target_pairs={{0,1},{1,0},{2,3},{3,2},{4,5},{5,4},{6,7},{7,6},{8,9},{9,8},{10,11... | collective-permute-start | bytes 122888 | tf_op jit(solution)/shard_map/ppermute | solution.py:977
